TPU v7x, 32 devices: a whole 2x2x4 slice. The times are simulated.
32 devices in a mesh: section: 4 (over y, x), dp: 8 (over z, core).
Axes of the slice: x: 2, y: 2, z: 4, core: 2. Of those that a mesh axis runs over, the one named last changes fastest.
Arguments:
- start: bfloat16 [64, 128, 768], P('dp'), may hold values from -12 to 12
- cotangent: bfloat16 [64, 128, 768], P('dp'), may hold values from -6 to 6
- first_weights: bfloat16 [4, 768, 3072], P('section')
- second_weights: bfloat16 [4, 3072, 768], P('section'), may hold values from -0.109375 to 0.109375
- norm_params: float32 [4, 2, 768], P('section')
- bias_params: float32 [4, 3840], P('section'), may hold values from -1 to 1
- segment_ids: int32 [64, 128], P('dp'), may hold values from 0 to 5, never falling along the last dimension, each value on 1 to 64 neighbouring positions
- valid_mask: int32 [64, 128], P('dp'), may hold values from 0 to 1, as said below
Outputs:
- residual_streams: bfloat16 [4, 64, 128, 768], P('section', 'dp')
- stream_grads: float32 [4, 64, 128, 768], P('section', 'dp')
- first_grad: float32 [4, 768, 3072], P('section')
- second_grad: float32 [4, 3072, 768], P('section')
- norm_grad: float32 [4, 2, 768], P('section')
- bias_grad: float32 [4, 3840], P('section')
- rms_stats: float32 [4, 2], P('section')
Inputs may be any that keep to these rules, and one draw needn't show every extreme that they name: `segment_ids`: numbers never fall along a row; a sentence has 1 to 64 tokens. `valid_mask`: in each row the ones come first, at least 8 of them.
All inputs are finite; a program needn't handle non-finite values.
Results may differ from a plain program's by a relative error of at most 0.018.
Values may be sent and summed in bfloat16 or wider, within the bound.
A program may use at most 448 MiB of HBM per device.

v0:
```python
import jax
import jax.numpy as jnp
from jax import lax
from jax.sharding import PartitionSpec as P

HEAD_DIM = 64
MICRO = 4


EPS = 1e-05
NEG_FILL = -1e30


def passed_along(block, axis, distance):
    devices = range(lax.axis_size(axis))
    route = [(i - distance, i) for i in devices if i - distance in devices]
    return lax.ppermute(block, axis, route)


def gelu_tanh(inputs):
    return jax.nn.gelu(inputs, approximate=True)


def layer_norm(hidden, norm_gain, norm_shift):
    row_mean = jnp.mean(hidden, axis=-1, keepdims=True)
    centered = hidden - row_mean
    variance = jnp.mean(centered * centered, axis=-1, keepdims=True)
    inv_std = lax.rsqrt(variance + EPS)
    normal = centered * inv_std
    return (normal * norm_gain + norm_shift, normal, inv_std)


def norm_back(normed_grad, normal, inv_std, norm_gain):
    scaled = normed_grad * norm_gain
    mean_one = jnp.mean(scaled, axis=-1, keepdims=True)
    mean_two = jnp.mean(scaled * normal, axis=-1, keepdims=True)
    entry_grad = inv_std * (scaled - mean_one - normal * mean_two)
    return (
        entry_grad,
        jnp.stack([jnp.sum(normed_grad * normal, axis=0), jnp.sum(normed_grad, axis=0)]),
    )


def contract_rows(former, latter):
    return lax.dot_general(
        former, latter, (((0,), (0,)), ((), ())), preferred_element_type=jnp.float32
    )


def contract_cols(former, latter):
    return lax.dot_general(
        former, latter, (((1,), (1,)), ((), ())), preferred_element_type=jnp.float32
    )


def score_mask(segment, validity):
    seq_len = segment.shape[1]
    diagonal = lax.broadcasted_iota(jnp.int32, (seq_len, seq_len), 0) == lax.broadcasted_iota(
        jnp.int32, (seq_len, seq_len), 1
    )
    same_seg = segment[:, :, None] == segment[:, None, :]
    return same_seg & ((validity[:, None, :] > 0) | diagonal[None])


def attention_core(hidden, wide_mat, vectors, norm_values, segment, validity):
    row_count, seq_len = segment.shape
    feature_dim = hidden.shape[1]
    head_count = feature_dim // HEAD_DIM
    normed, normal, inv_std = layer_norm(hidden, norm_values[0], norm_values[1])
    normed_low = normed.astype(jnp.bfloat16)
    projected = jnp.dot(
        normed_low, wide_mat[:, : 3 * feature_dim], preferred_element_type=jnp.float32
    )
    bias_all = jnp.concatenate(
        [
            vectors[:feature_dim],
            jnp.zeros((feature_dim,), jnp.float32),
            vectors[feature_dim : 2 * feature_dim],
        ]
    )
    packed = (
        (projected + bias_all)
        .astype(jnp.bfloat16)
        .reshape(row_count, seq_len, 3, head_count, HEAD_DIM)
    )
    queries = packed[:, :, 0]
    key_heads = packed[:, :, 1]
    value_heads = packed[:, :, 2]
    scores = jnp.einsum(
        "bqhe,bkhe->bhqk", queries, key_heads, preferred_element_type=jnp.float32
    ) * HEAD_DIM ** (-0.5)
    scores = jnp.where(score_mask(segment, validity)[:, None], scores, NEG_FILL)
    row_max = jnp.max(scores, axis=-1, keepdims=True)
    exponent = jnp.exp(scores - row_max)
    attn_prob = exponent / jnp.sum(exponent, axis=-1, keepdims=True)
    attn_low = attn_prob.astype(jnp.bfloat16)
    mixed_out = jnp.einsum(
        "bhqk,bkhe->bqhe", attn_low, value_heads, preferred_element_type=jnp.float32
    )
    mixed_low = mixed_out.astype(jnp.bfloat16).reshape(row_count * seq_len, feature_dim)
    branch = contract_cols(mixed_low, wide_mat[:, 3 * feature_dim :]) + vectors[-feature_dim:]
    saved = (
        normed_low,
        normal,
        inv_std,
        queries,
        key_heads,
        value_heads,
        attn_prob,
        attn_low,
        mixed_low,
    )
    return (branch, saved)


def attention_forward(hidden, wide_mat, narrow, vectors, norm_values, segment, validity):
    return attention_core(hidden, wide_mat, vectors, norm_values, segment, validity)[0]


def attention_backward(hidden, incoming, wide_mat, narrow, vectors, norm_values, segment, validity):
    branch, saved = attention_core(hidden, wide_mat, vectors, norm_values, segment, validity)
    normed_low, normal, inv_std, queries, key_heads, value_heads, attn_prob, attn_low, mixed_low = (
        saved
    )
    row_count, seq_len = segment.shape
    feature_dim = hidden.shape[1]
    head_count = feature_dim // HEAD_DIM
    ff_dim = wide_mat.shape[1]
    scale_factor = HEAD_DIM ** (-0.5)
    out_grad = contract_rows(incoming, mixed_low)
    out_bias = jnp.sum(incoming.astype(jnp.float32), axis=0)
    mixed_grad = jnp.dot(
        incoming, wide_mat[:, 3 * feature_dim :], preferred_element_type=jnp.float32
    )
    mixed_grad = mixed_grad.astype(jnp.bfloat16).reshape(row_count, seq_len, head_count, HEAD_DIM)
    prob_grad = jnp.einsum(
        "bqhe,bkhe->bhqk", mixed_grad, value_heads, preferred_element_type=jnp.float32
    )
    row_dot = jnp.sum(attn_prob * prob_grad, axis=-1, keepdims=True)
    score_grad = (attn_prob * (prob_grad - row_dot)).astype(jnp.bfloat16)
    query_grad = (
        jnp.einsum("bhqk,bkhe->bqhe", score_grad, key_heads, preferred_element_type=jnp.float32)
        * scale_factor
    )
    key_grad = (
        jnp.einsum("bhqk,bqhe->bkhe", score_grad, queries, preferred_element_type=jnp.float32)
        * scale_factor
    )
    value_grad = jnp.einsum(
        "bhqk,bqhe->bkhe", attn_low, mixed_grad, preferred_element_type=jnp.float32
    )
    packed_grad = jnp.stack([query_grad, key_grad, value_grad], axis=2).astype(jnp.bfloat16)
    packed_grad = packed_grad.reshape(row_count * seq_len, 3 * feature_dim)
    proj_grad = contract_rows(normed_low, packed_grad)
    grad_sums = jnp.sum(packed_grad.astype(jnp.float32), axis=0)
    normed_grad = contract_cols(packed_grad, wide_mat[:, : 3 * feature_dim])
    entry_grad, norm_grad = norm_back(normed_grad, normal, inv_std, norm_values[0])
    wide_grad = jnp.concatenate([proj_grad, out_grad], axis=1)
    vector_grad = jnp.concatenate(
        [
            grad_sums[:feature_dim],
            grad_sums[2 * feature_dim :],
            jnp.zeros((ff_dim - 2 * feature_dim,), jnp.float32),
            out_bias,
        ]
    )
    return (
        incoming.astype(jnp.float32) + entry_grad,
        wide_grad,
        jnp.zeros(narrow.shape, jnp.float32),
        norm_grad,
        vector_grad,
    )


def dense_core(hidden, wide_mat, narrow, vectors, norm_values):
    ff_dim = wide_mat.shape[1]
    normed, normal, inv_std = layer_norm(hidden, norm_values[0], norm_values[1])
    normed_low = normed.astype(jnp.bfloat16)
    hidden_pre = (
        jnp.dot(normed_low, wide_mat, preferred_element_type=jnp.float32) + vectors[:ff_dim]
    )
    activation = gelu_tanh(hidden_pre).astype(jnp.bfloat16)
    branch = jnp.dot(activation, narrow, preferred_element_type=jnp.float32) + vectors[ff_dim:]
    return (branch, (normed_low, normal, inv_std, hidden_pre, activation))


def dense_forward(hidden, wide_mat, narrow, vectors, norm_values, segment, validity):
    return dense_core(hidden, wide_mat, narrow, vectors, norm_values)[0]


def dense_backward(hidden, incoming, wide_mat, narrow, vectors, norm_values, segment, validity):
    branch, saved = dense_core(hidden, wide_mat, narrow, vectors, norm_values)
    normed_low, normal, inv_std, hidden_pre, activation = saved
    narrow_grad = contract_rows(activation, incoming)
    out_bias = jnp.sum(incoming.astype(jnp.float32), axis=0)
    act_grad = contract_cols(incoming, narrow)
    gelu_value, gelu_pull = jax.vjp(gelu_tanh, hidden_pre)
    pre_grad = gelu_pull(act_grad)[0].astype(jnp.bfloat16)
    wide_grad = contract_rows(normed_low, pre_grad)
    in_bias = jnp.sum(pre_grad.astype(jnp.float32), axis=0)
    normed_grad = contract_cols(pre_grad, wide_mat)
    entry_grad, norm_grad = norm_back(normed_grad, normal, inv_std, norm_values[0])
    return (
        incoming.astype(jnp.float32) + entry_grad,
        wide_grad,
        narrow_grad,
        norm_grad,
        jnp.concatenate([in_bias, out_bias]),
    )


def local(
    start,
    cotangent,
    first_weights,
    second_weights,
    norm_params,
    bias_params,
    segment_ids,
    valid_mask,
):
    section_id = lax.axis_index("section")
    section_count = lax.axis_size("section")
    is_attention = section_id % 2 == 0
    row_count, seq_len, feature_dim = start.shape
    micro_count = MICRO
    group_rows = row_count // micro_count
    token_count = group_rows * seq_len
    wide_mat = first_weights[0]
    narrow = second_weights[0]
    norm_values = norm_params[0]
    vectors = bias_params[0]
    inputs = start.reshape(micro_count, group_rows, seq_len, feature_dim)
    segments = segment_ids.reshape(micro_count, group_rows, seq_len)
    validities = valid_mask.reshape(micro_count, group_rows, seq_len)
    seed_grads = jnp.where(valid_mask[:, :, None] > 0, cotangent, jnp.zeros_like(cotangent))
    seed_grads = seed_grads.reshape(micro_count, group_rows, seq_len, feature_dim)
    moments = micro_count + section_count - 1

    def forward_step(entry_low, segment, validity):
        hidden = entry_low.reshape(token_count, feature_dim).astype(jnp.float32)
        branch = lax.cond(
            is_attention,
            attention_forward,
            dense_forward,
            hidden,
            wide_mat,
            narrow,
            vectors,
            norm_values,
            segment,
            validity,
        )
        out_low = (hidden + branch).astype(jnp.bfloat16)
        weight = validity.reshape(token_count, 1).astype(jnp.float32)
        out_value = out_low.astype(jnp.float32)
        square_part = jnp.stack(
            [jnp.sum(out_value * out_value * weight), jnp.sum(branch * branch * weight)]
        )
        return (out_low.reshape(group_rows, seq_len, feature_dim), square_part)

    def forward_skip(entry_low, segment, validity):
        return (entry_low, jnp.zeros((2,), jnp.float32))

    kept_in = jnp.zeros_like(inputs)
    kept_out = jnp.zeros_like(inputs)
    squares = jnp.zeros((2,), jnp.float32)
    outgoing = inputs[0]
    for moment in range(moments):
        if moment > 0:
            arrived = passed_along(outgoing, "section", 1)
        else:
            arrived = outgoing
        mb_index = moment - section_id
        active = (mb_index >= 0) & (mb_index < micro_count)
        mb_slot = jnp.clip(mb_index, 0, micro_count - 1)
        current = jnp.where(section_id == 0, inputs[min(moment, micro_count - 1)], arrived)
        outgoing, square_part = lax.cond(
            active, forward_step, forward_skip, current, segments[mb_slot], validities[mb_slot]
        )
        kept_in = lax.dynamic_update_index_in_dim(
            kept_in, jnp.where(active, current, kept_in[mb_slot]), mb_slot, 0
        )
        kept_out = lax.dynamic_update_index_in_dim(
            kept_out, jnp.where(active, outgoing, kept_out[mb_slot]), mb_slot, 0
        )
        squares = squares + square_part

    def backward_step(entry_low, incoming, segment, validity):
        hidden = entry_low.reshape(token_count, feature_dim).astype(jnp.float32)
        flat_grad = incoming.reshape(token_count, feature_dim)
        results = lax.cond(
            is_attention,
            attention_backward,
            dense_backward,
            hidden,
            flat_grad,
            wide_mat,
            narrow,
            vectors,
            norm_values,
            segment,
            validity,
        )
        return (results[0].reshape(group_rows, seq_len, feature_dim),) + tuple(results[1:])

    def backward_skip(entry_low, incoming, segment, validity):
        return (
            jnp.zeros((group_rows, seq_len, feature_dim), jnp.float32),
            jnp.zeros(wide_mat.shape, jnp.float32),
            jnp.zeros(narrow.shape, jnp.float32),
            jnp.zeros(norm_values.shape, jnp.float32),
            jnp.zeros(vectors.shape, jnp.float32),
        )

    totals = backward_skip(inputs[0], inputs[0], segments[0], validities[0])[1:]
    first_part = totals
    stream_grads = jnp.zeros((micro_count, group_rows, seq_len, feature_dim), jnp.float32)
    outgoing = seed_grads[0]
    halfway = section_count + micro_count // 2 - 2
    for moment in range(moments):
        if moment > 0:
            arrived = passed_along(outgoing, "section", -1)
        else:
            arrived = outgoing
        mb_index = moment - (section_count - 1 - section_id)
        active = (mb_index >= 0) & (mb_index < micro_count)
        mb_slot = jnp.clip(mb_index, 0, micro_count - 1)
        current = jnp.where(
            section_id == section_count - 1, seed_grads[min(moment, micro_count - 1)], arrived
        )
        step_out = lax.cond(
            active,
            backward_step,
            backward_skip,
            kept_in[mb_slot],
            current,
            segments[mb_slot],
            validities[mb_slot],
        )
        stream_grads = lax.dynamic_update_index_in_dim(
            stream_grads, jnp.where(active, step_out[0], stream_grads[mb_slot]), mb_slot, 0
        )
        totals = tuple((running + adding for running, adding in zip(totals, step_out[1:])))
        outgoing = step_out[0].astype(jnp.bfloat16)
        if moment == halfway:
            first_part = totals
            totals = tuple((jnp.zeros_like(running) for running in totals))
    valid_total = jnp.sum(valid_mask).astype(jnp.float32)
    local_sums = jnp.concatenate([squares, valid_total[None]])
    merged = tuple((running + adding for running, adding in zip(first_part, totals)))
    wide_sum, narrow_sum, norm_sum, vector_sum, stat_sum = lax.psum(
        (merged[0], merged[1], merged[2], merged[3], local_sums), "dp"
    )
    rms_stats = jnp.sqrt(stat_sum[:2] / (stat_sum[2] * feature_dim))
    return (
        kept_out.reshape(1, row_count, seq_len, feature_dim),
        stream_grads.reshape(1, row_count, seq_len, feature_dim),
        wide_sum[None],
        narrow_sum[None],
        norm_sum[None],
        vector_sum[None],
        rms_stats[None],
    )


def solution(mesh):
    in_specs = (
        P("dp", None, None),
        P("dp", None, None),
        P("section", None, None),
        P("section", None, None),
        P("section", None, None),
        P("section", None),
        P("dp", None),
        P("dp", None),
    )
    out_specs = (
        P("section", "dp", None, None),
        P("section", "dp", None, None),
        P("section", None, None),
        P("section", None, None),
        P("section", None, None),
        P("section", None),
        P("section", None),
    )
    return jax.shard_map(local, mesh=mesh, in_specs=in_specs, out_specs=out_specs, check_vma=False)
```

profile of v0, /device:TPU:3, one launch (start us, length us, event | category | flops | bytes accessed | tf_op | source)
XLA Modules:
  0.0 1116.3 jit_solution(8927561877988761410)
XLA Ops:
  16.4 24.5 %collective-permute-done = bf16[2,128,768]{2,1,0:T(8,128)(2,1)S(1)} collective-permute-done((bf16[2,128,768]{2,1,0:T(8,128)(2,1)S(1)}, bf16[2,128,768]{2,1,0:T(8,128)(2,1)S(1)}, u32[]{:S(2)}, u32[]{:S(2)}) %collective-permute-start) | collective-permute-done | bytes 393248 | tf_op jit(solution)/shard_map/ppermute | solution.py:17
  42.1 12.8 %conditional.29 = (bf16[2,128,768]{2,1,0:T(8,128)(2,1)S(1)}, f32[2]{0:T(128)S(1)}) conditional(s32[]{:T(128)} %convert_element_type.1093, bf16[2,128,768]{2,1,0:T(8,128)(2,1)S(1)} %get-tuple-element.2552, (bf16[2,128,768]{2,1,0:T(8,128)(2,1)S(1)}, pred[]{:T(512)}, s32[4,2,128]{2,1,0:T(2,128)S(1)}, s32[]{:T(128)}, f32[2,768]{1,0:T(2,128)S(1)}, ...), branch_computations={%region_12.13_spmd, %region_13.24_spmd} | conditional | flops 2427912704 | bytes 24984236 | solution.py:279
  56.8 19.0 %collective-permute-done.1 = bf16[2,128,768]{2,1,0:T(8,128)(2,1)S(1)} collective-permute-done((bf16[2,128,768]{2,1,0:T(8,128)(2,1)S(1)}, bf16[2,128,768]{2,1,0:T(8,128)(2,1)S(1)}, u32[]{:S(2)}, u32[]{:S(2)}) %collective-permute-start.1) | collective-permute-done | bytes 393248 | tf_op jit(solution)/shard_map/ppermute | solution.py:17
  95.0 14.8 %collective-permute-done.2 = bf16[2,128,768]{2,1,0:T(8,128)(2,1)S(1)} collective-permute-done((bf16[2,128,768]{2,1,0:T(8,128)(2,1)}, bf16[2,128,768]{2,1,0:T(8,128)(2,1)S(1)}, u32[]{:S(2)}, u32[]{:S(2)}) %collective-permute-start.2) | collective-permute-done | bytes 393248 | tf_op jit(solution)/shard_map/ppermute | solution.py:17
  175.7 28.2 %collective-permute-start.5 = (bf16[2,128,768]{2,1,0:T(8,128)(2,1)S(1)}, bf16[2,128,768]{2,1,0:T(8,128)(2,1)S(1)}, u32[]{:S(2)}, u32[]{:S(2)}) collective-permute-start(bf16[2,128,768]{2,1,0:T(8,128)(2,1)S(1)} %get-tuple-element.2317), channel_id=1, source_target_pairs={{0,8},{8,16},{16,24},{1,9},{9,17},{17,25},{2,10},{10,18},{18,26},{... | collective-permute-start | bytes 1179656 | tf_op jit(solution)/shard_map/ppermute | solution.py:17
  209.6 20.7 %conditional.35 = (f32[2,128,768]{2,1,0:T(8,128)}, f32[768,3072]{1,0:T(8,128)}, f32[3072,768]{1,0:T(8,128)}, f32[2,768]{1,0:T(2,128)}, f32[3840]{0:T(1024)}) conditional(s32[]{:T(128)} %convert_element_type.1099, () %tuple.372, (pred[]{:T(512)}, bf16[4,2,128,768]{3,2,1,0:T(8,128)(2,1)S(1)}, s32[]{:T(128)}, bf16[8,128,768]{2,1,0:T(8,128)(2,1)}, ...), branch_computations={%region_84.85_spmd, %region_85.107_spmd} | conditional | flops 6071648256 | bytes 104986440 | solution.py:333
  241.4 20.2 %conditional.36 = (f32[2,128,768]{2,1,0:T(8,128)}, f32[768,3072]{1,0:T(8,128)}, f32[3072,768]{1,0:T(8,128)}, f32[2,768]{1,0:T(2,128)}, f32[3840]{0:T(1024)}) conditional(s32[]{:T(128)} %convert_element_type.1100, () %tuple.374, (pred[]{:T(512)}, bf16[4,2,128,768]{3,2,1,0:T(8,128)(2,1)S(1)}, s32[]{:T(128)}, bf16[8,128,768]{2,1,0:T(8,128)(2,1)}, ...), branch_computations={%region_107.108_spmd, %region_108.130_spmd} | conditional | flops 6071844864 | bytes 105576264 | solution.py:333
  264.7 60.6 %collective-permute-done.7 = bf16[2,128,768]{2,1,0:T(8,128)(2,1)S(1)} collective-permute-done((bf16[2,128,768]{2,1,0:T(8,128)(2,1)S(1)}, bf16[2,128,768]{2,1,0:T(8,128)(2,1)S(1)}, u32[]{:S(2)}, u32[]{:S(2)}) %collective-permute-start.7) | collective-permute-done | bytes 393248 | tf_op jit(solution)/shard_map/ppermute | solution.py:17
  325.3 38.3 %conditional.37 = (f32[2,128,768]{2,1,0:T(8,128)}, f32[768,3072]{1,0:T(8,128)}, f32[3072,768]{1,0:T(8,128)}, f32[2,768]{1,0:T(2,128)}, f32[3840]{0:T(1024)}) conditional(s32[]{:T(128)} %convert_element_type.1102, () %tuple.376, (pred[]{:T(512)}, bf16[4,2,128,768]{3,2,1,0:T(8,128)(2,1)S(1)}, s32[]{:T(128)}, bf16[8,128,768]{2,1,0:T(8,128)(2,1)}, ...), branch_computations={%region_130.131_spmd, %region_131.153_spmd} | conditional | flops 6071844864 | bytes 105576264 | solution.py:333
  326.4 28.9 %conditional.9 = (f32[768,3072]{1,0:T(8,128)}, f32[3072,768]{1,0:T(8,128)}, f32[2,768]{1,0:T(2,128)}, f32[3840]{0:T(1024)}, f32[2,128,768]{2,1,0:T(8,128)}) conditional(s32[]{:T(128)} %convert_element_type.992, (f32[256,768]{1,0:T(8,128)S(1)}, f32[2,768]{1,0:T(2,128)S(1)}, bf16[256,768]{1,0:T(8,128)(2,1)S(1)}, bf16[3072,768]{1,0:T(8,128)(2,1)}, ...), branch_computations={%region_132.140_spmd, %region_141.152_spmd} | conditional | flops 6071451648 | bytes 102233768 | solution.py:293
  367.7 34.5 %collective-permute-done.8 = bf16[2,128,768]{2,1,0:T(8,128)(2,1)S(1)} collective-permute-done((bf16[2,128,768]{2,1,0:T(8,128)(2,1)S(1)}, bf16[2,128,768]{2,1,0:T(8,128)(2,1)S(1)}, u32[]{:S(2)}, u32[]{:S(2)}) %collective-permute-start.8) | collective-permute-done | bytes 393248 | tf_op jit(solution)/shard_map/ppermute | solution.py:17
  402.2 39.3 %conditional.38 = (f32[2,128,768]{2,1,0:T(8,128)}, f32[768,3072]{1,0:T(8,128)}, f32[3072,768]{1,0:T(8,128)}, f32[2,768]{1,0:T(2,128)}, f32[3840]{0:T(1024)}) conditional(s32[]{:T(128)} %convert_element_type.1104, () %tuple.378, (pred[]{:T(512)}, bf16[4,2,128,768]{3,2,1,0:T(8,128)(2,1)S(1)}, s32[]{:T(128)}, pred[2,128,768]{2,1,0:T(8,128)(4,1)S(1)}, ...), branch_computations={%region_153.154_spmd, %region_154.176_spmd} | conditional | flops 6071844864 | bytes 108722056 | solution.py:333
  404.2 37.2 %conditional.10 = (f32[768,3072]{1,0:T(8,128)}, f32[3072,768]{1,0:T(8,128)}, f32[2,768]{1,0:T(2,128)}, f32[3840]{0:T(1024)}, f32[2,128,768]{2,1,0:T(8,128)}) conditional(s32[]{:T(128)} %convert_element_type.1011, (f32[256,768]{1,0:T(8,128)S(1)}, f32[2,768]{1,0:T(2,128)S(1)}, bf16[256,768]{1,0:T(8,128)(2,1)S(1)}, bf16[3072,768]{1,0:T(8,128)(2,1)}, ...), branch_computations={%region_155.163_spmd, %region_164.175_spmd} | conditional | flops 6071451648 | bytes 103806664 | solution.py:293
  444.6 27.1 %collective-permute-done.9 = bf16[2,128,768]{2,1,0:T(8,128)(2,1)S(1)} collective-permute-done((bf16[2,128,768]{2,1,0:T(8,128)(2,1)S(1)}, bf16[2,128,768]{2,1,0:T(8,128)(2,1)S(1)}, u32[]{:S(2)}, u32[]{:S(2)}) %collective-permute-start.9) | collective-permute-done | bytes 393248 | tf_op jit(solution)/shard_map/ppermute | solution.py:17
  471.7 39.6 %conditional.39 = (f32[2,128,768]{2,1,0:T(8,128)}, f32[768,3072]{1,0:T(8,128)}, f32[3072,768]{1,0:T(8,128)}, f32[2,768]{1,0:T(2,128)}, f32[3840]{0:T(1024)}) conditional(s32[]{:T(128)} %convert_element_type.1106, () %tuple.380, (pred[]{:T(512)}, bf16[4,2,128,768]{3,2,1,0:T(8,128)(2,1)S(1)}, s32[]{:T(128)}, pred[2,128,768]{2,1,0:T(8,128)(4,1)S(1)}, ...), branch_computations={%region_176.177_spmd, %region_177.199_spmd} | conditional | flops 6071844864 | bytes 108722056 | solution.py:333
  473.7 28.5 %conditional.11 = (f32[768,3072]{1,0:T(8,128)}, f32[3072,768]{1,0:T(8,128)}, f32[2,768]{1,0:T(2,128)}, f32[3840]{0:T(1024)}, f32[2,128,768]{2,1,0:T(8,128)}) conditional(s32[]{:T(128)} %convert_element_type.1030, (f32[256,768]{1,0:T(8,128)S(1)}, f32[2,768]{1,0:T(2,128)S(1)}, bf16[256,768]{1,0:T(8,128)(2,1)S(1)}, bf16[3072,768]{1,0:T(8,128)(2,1)}, ...), branch_computations={%region_178.186_spmd, %region_187.198_spmd} | conditional | flops 6071451648 | bytes 103806664 | solution.py:293
  522.7 27.1 %collective-permute-done.10 = bf16[2,128,768]{2,1,0:T(8,128)(2,1)S(1)} collective-permute-done((bf16[2,128,768]{2,1,0:T(8,128)(2,1)S(1)}, bf16[2,128,768]{2,1,0:T(8,128)(2,1)S(1)}, u32[]{:S(2)}, u32[]{:S(2)}) %collective-permute-start.10) | collective-permute-done | bytes 393248 | tf_op jit(solution)/shard_map/ppermute | solution.py:17
  549.8 39.2 %conditional.40 = (f32[2,128,768]{2,1,0:T(8,128)}, f32[768,3072]{1,0:T(8,128)}, f32[3072,768]{1,0:T(8,128)}, f32[2,768]{1,0:T(2,128)}, f32[3840]{0:T(1024)}) conditional(s32[]{:T(128)} %convert_element_type.1108, () %tuple.382, (pred[]{:T(512)}, bf16[4,2,128,768]{3,2,1,0:T(8,128)(2,1)S(1)}, s32[]{:T(128)}, pred[2,128,768]{2,1,0:T(8,128)(4,1)S(1)}, ...), branch_computations={%region_199.200_spmd, %region_200.222_spmd} | conditional | flops 6071844864 | bytes 108722056 | solution.py:333
  551.8 28.8 %conditional.12 = (f32[768,3072]{1,0:T(8,128)}, f32[3072,768]{1,0:T(8,128)}, f32[2,768]{1,0:T(2,128)}, f32[3840]{0:T(1024)}, f32[2,128,768]{2,1,0:T(8,128)}) conditional(s32[]{:T(128)} %convert_element_type.1049, (f32[256,768]{1,0:T(8,128)S(1)}, f32[2,768]{1,0:T(2,128)S(1)}, bf16[256,768]{1,0:T(8,128)(2,1)S(1)}, bf16[3072,768]{1,0:T(8,128)(2,1)}, ...), branch_computations={%region_201.209_spmd, %region_210.221_spmd} | conditional | flops 6071451648 | bytes 103806664 | solution.py:293
  605.3 17.6 %conditional.41 = (f32[2,128,768]{2,1,0:T(8,128)}, f32[768,3072]{1,0:T(8,128)}, f32[3072,768]{1,0:T(8,128)}, f32[2,768]{1,0:T(2,128)}, f32[3840]{0:T(1024)}) conditional(s32[]{:T(128)} %convert_element_type.1110, () %tuple.384, (pred[]{:T(512)}, bf16[4,2,128,768]{3,2,1,0:T(8,128)(2,1)S(1)}, s32[]{:T(128)}, pred[2,128,768]{2,1,0:T(8,128)(4,1)S(1)}, ...), branch_computations={%region_222.223_spmd, %region_223.245_spmd} | conditional | flops 6071844864 | bytes 113637672 | solution.py:333
  622.9 26.7 %add_bitcast_fusion.1 = f32[1,768,3072]{2,1,0:T(8,128)} fusion(f32[768,3072]{1,0:T(8,128)} %get-tuple-element.2331, f32[768,3072]{1,0:T(8,128)} %get-tuple-element.2332, f32[768,3072]{1,0:T(8,128)} %get-tuple-element.2330, f32[768,3072]{1,0:T(8,128)} %get-tuple-element.2329, f32[768,3072]{1,0:T(8,128)} %get-tuple-element.2328, ...), kind=kLoop, calls=%fused_computation.1200 | loop fusion | flops 14155776 | bytes 75497472 | tf_op jit(solution)/shard_map/broadcast_in_dim | solution.py:360
  649.6 25.4 %add_bitcast_fusion = f32[1,3072,768]{2,1,0:T(8,128)} fusion(f32[3072,768]{1,0:T(8,128)} %get-tuple-element.2338, f32[3072,768]{1,0:T(8,128)} %get-tuple-element.2339, f32[3072,768]{1,0:T(8,128)} %get-tuple-element.2337, f32[3072,768]{1,0:T(8,128)} %get-tuple-element.2336, f32[3072,768]{1,0:T(8,128)} %get-tuple-element.2335, ...), kind=kLoop, calls=%fused_computation.1199 | loop fusion | flops 14155776 | bytes 75497472 | tf_op jit(solution)/shard_map/broadcast_in_dim | solution.py:361
  703.0 32.9 %all-reduce = (f32[1,2,768]{2,1,0:T(2,128)}, f32[1,3840]{1,0:T(1,128)}, f32[3]{0:T(128)S(1)}) all-reduce(f32[1,2,768]{2,1,0:T(2,128)S(1)} %add_bitcast_fusion.2, f32[1,3840]{1,0:T(1,128)S(1)} %broadcast_in_dim.472, f32[3]{0:T(128)S(1)} %pad_maximum_fusion.56), channel_id=1, replica_groups=mesh['section'=4,'dp'=8] {'dp'}, use_global_device_ids=true, to_apply=%region_247.248 | all-reduce | flops 5379 | bytes 43032 | tf_op jit(solution)/shard_map/psum | solution.py:353
  739.0 357.8 %all-reduce.4.cloned.1.call-done = (f32[1,768,3072]{2,1,0:T(8,128)}, f32[1,3072,768]{2,1,0:T(8,128)}) async-done(((f32[1,768,3072]{2,1,0:T(8,128)}, f32[1,3072,768]{2,1,0:T(8,128)}), (f32[1,768,3072]{2,1,0:T(8,128)}, f32[1,3072,768]{2,1,0:T(8,128)})) %all-reduce.4.cloned.1.call-update) | async-done | bytes 18874384 | tf_op jit(solution)/shard_map/psum | solution.py:353
  (313 shorter events, 427.0 us)
Async XLA Ops:
  7.2 1089.6 %all-reduce.4.cloned.1.call-start = ((), (), s32[]{:S(2)}) async-start(), calls=%async_computation | async-start | bytes 37748736 | tf_op jit(solution)/shard_map/psum | solution.py:353
  8.2 32.7 %collective-permute-start = (bf16[2,128,768]{2,1,0:T(8,128)(2,1)S(1)}, bf16[2,128,768]{2,1,0:T(8,128)(2,1)S(1)}, u32[]{:S(2)}, u32[]{:S(2)}) collective-permute-start(bf16[2,128,768]{2,1,0:T(8,128)(2,1)S(1)} %get-tuple-element.2312), channel_id=1, source_target_pairs={{0,8},{8,16},{16,24},{1,9},{9,17},{17,25},{2,10},{10,18},{18,26},{... | collective-permute-start | bytes 1179656 | tf_op jit(solution)/shard_map/ppermute | solution.py:17
  13.4 28.7 %copy-start.3 = (f32[1,2,768]{2,1,0:T(2,128)S(1)}, f32[1,2,768]{2,1,0:T(2,128)}, u32[]{:S(2)}) copy-start(f32[1,2,768]{2,1,0:T(2,128)} %param.68) | copy-start | bytes 18436
  13.4 28.7 %copy-start.59 = (s32[8,128]{1,0:T(8,128)S(1)}, s32[8,128]{1,0:T(8,128)}, u32[]{:S(2)}) copy-start(s32[8,128]{1,0:T(8,128)} %param.71) | copy-start | bytes 12292
  13.4 28.7 %copy-start.64 = (s32[8,128]{1,0:T(8,128)S(1)}, s32[8,128]{1,0:T(8,128)}, u32[]{:S(2)}) copy-start(s32[8,128]{1,0:T(8,128)} %param.70) | copy-start | bytes 12292
  54.8 22.1 %copy-start.19 = (bf16[2,128,768]{2,1,0:T(8,128)(2,1)}, bf16[2,128,768]{2,1,0:T(8,128)(2,1)S(1)}, u32[]{:S(2)}) copy-start(bf16[2,128,768]{2,1,0:T(8,128)(2,1)S(1)} %get-tuple-element.2313) | copy-start | bytes 1179652
  54.8 22.1 %copy-start.72 = (f32[2]{0:T(128)}, f32[2]{0:T(128)S(1)}, u32[]{:S(2)}) copy-start(f32[2]{0:T(128)S(1)} %get-tuple-element.2355) | copy-start | bytes 28
  54.8 20.9 %collective-permute-start.1 = (bf16[2,128,768]{2,1,0:T(8,128)(2,1)S(1)}, bf16[2,128,768]{2,1,0:T(8,128)(2,1)S(1)}, u32[]{:S(2)}, u32[]{:S(2)}) collective-permute-start(bf16[2,128,768]{2,1,0:T(8,128)(2,1)S(1)} %get-tuple-element.2313), channel_id=1, source_target_pairs={{0,8},{8,16},{16,24},{1,9},{9,17},{17,25},{2,10},{10,18},{18,26},{... | collective-permute-start | bytes 1179656 | tf_op jit(solution)/shard_map/ppermute | solution.py:17
  89.3 21.7 %copy-start.73 = (f32[2]{0:T(128)}, f32[2]{0:T(128)S(1)}, u32[]{:S(2)}) copy-start(f32[2]{0:T(128)S(1)} %get-tuple-element.2356) | copy-start | bytes 28
  89.3 20.5 %collective-permute-start.2 = (bf16[2,128,768]{2,1,0:T(8,128)(2,1)}, bf16[2,128,768]{2,1,0:T(8,128)(2,1)S(1)}, u32[]{:S(2)}, u32[]{:S(2)}) collective-permute-start(bf16[2,128,768]{2,1,0:T(8,128)(2,1)} %get-tuple-element.2314), channel_id=1, source_target_pairs={{0,8},{8,16},{16,24},{1,9},{9,17},{17,25},{2,10},{10,18},{18,26},{... | collective-permute-start | bytes 1179656 | tf_op jit(solution)/shard_map/ppermute | solution.py:17
  123.0 20.9 %copy-start.74 = (f32[2]{0:T(128)}, f32[2]{0:T(128)S(1)}, u32[]{:S(2)}) copy-start(f32[2]{0:T(128)S(1)} %get-tuple-element.2357) | copy-start | bytes 28
  123.0 19.7 %collective-permute-start.3 = (bf16[2,128,768]{2,1,0:T(8,128)(2,1)S(1)}, bf16[2,128,768]{2,1,0:T(8,128)(2,1)S(1)}, u32[]{:S(2)}, u32[]{:S(2)}) collective-permute-start(bf16[2,128,768]{2,1,0:T(8,128)(2,1)S(1)} %get-tuple-element.2315), channel_id=1, source_target_pairs={{0,8},{8,16},{16,24},{1,9},{9,17},{17,25},{2,10},{10,18},{18,26},{... | collective-permute-start | bytes 1179656 | tf_op jit(solution)/shard_map/ppermute | solution.py:17
  156.7 17.8 %collective-permute-start.4 = (bf16[2,128,768]{2,1,0:T(8,128)(2,1)}, bf16[2,128,768]{2,1,0:T(8,128)(2,1)S(1)}, u32[]{:S(2)}, u32[]{:S(2)}) collective-permute-start(bf16[2,128,768]{2,1,0:T(8,128)(2,1)} %get-tuple-element.2316), channel_id=1, source_target_pairs={{0,8},{8,16},{16,24},{1,9},{9,17},{17,25},{2,10},{10,18},{18,26},{... | collective-permute-start | bytes 1179656 | tf_op jit(solution)/shard_map/ppermute | solution.py:17
  175.7 33.9 %copy-start.23 = (bf16[2,128,768]{2,1,0:T(8,128)(2,1)}, bf16[2,128,768]{2,1,0:T(8,128)(2,1)S(1)}, u32[]{:S(2)}) copy-start(bf16[2,128,768]{2,1,0:T(8,128)(2,1)S(1)} %get-tuple-element.2317) | copy-start | bytes 1179652
  175.7 33.9 %copy-start.76 = (f32[2]{0:T(128)}, f32[2]{0:T(128)S(1)}, u32[]{:S(2)}) copy-start(f32[2]{0:T(128)S(1)} %get-tuple-element.2359) | copy-start | bytes 28
  175.7 33.0 %copy-start.2 = (bf16[8,128,768]{2,1,0:T(8,128)(2,1)S(1)}, bf16[8,128,768]{2,1,0:T(8,128)(2,1)}, u32[]{:S(2)}) copy-start(bf16[8,128,768]{2,1,0:T(8,128)(2,1)} %param.64) | copy-start | bytes 4718596
  175.7 33.0 %collective-permute-start.5 = (bf16[2,128,768]{2,1,0:T(8,128)(2,1)S(1)}, bf16[2,128,768]{2,1,0:T(8,128)(2,1)S(1)}, u32[]{:S(2)}, u32[]{:S(2)}) collective-permute-start(bf16[2,128,768]{2,1,0:T(8,128)(2,1)S(1)} %get-tuple-element.2317), channel_id=1, source_target_pairs={{0,8},{8,16},{16,24},{1,9},{9,17},{17,25},{2,10},{10,18},{18,26},{... | collective-permute-start | bytes 1179656 | tf_op jit(solution)/shard_map/ppermute | solution.py:17
  231.5 9.9 collective-permute-start.6
  262.8 62.5 %collective-permute-start.7 = (bf16[2,128,768]{2,1,0:T(8,128)(2,1)S(1)}, bf16[2,128,768]{2,1,0:T(8,128)(2,1)S(1)}, u32[]{:S(2)}, u32[]{:S(2)}) collective-permute-start(bf16[2,128,768]{2,1,0:T(8,128)(2,1)S(1)} %convert_element_type.1103), channel_id=1, source_target_pairs={{8,0},{16,8},{24,16},{9,1},{17,9},{25,17},{10,2},{18,10},{26,18},{... | collective-permute-start | bytes 1179656 | tf_op jit(solution)/shard_map/ppermute | solution.py:17
  364.7 37.5 %collective-permute-start.8 = (bf16[2,128,768]{2,1,0:T(8,128)(2,1)S(1)}, bf16[2,128,768]{2,1,0:T(8,128)(2,1)S(1)}, u32[]{:S(2)}, u32[]{:S(2)}) collective-permute-start(bf16[2,128,768]{2,1,0:T(8,128)(2,1)S(1)} %convert_element_type.1105), channel_id=1, source_target_pairs={{8,0},{16,8},{24,16},{9,1},{17,9},{25,17},{10,2},{18,10},{26,18},{... | collective-permute-start | bytes 1179656 | tf_op jit(solution)/shard_map/ppermute | solution.py:17
  442.6 29.0 %collective-permute-start.9 = (bf16[2,128,768]{2,1,0:T(8,128)(2,1)S(1)}, bf16[2,128,768]{2,1,0:T(8,128)(2,1)S(1)}, u32[]{:S(2)}, u32[]{:S(2)}) collective-permute-start(bf16[2,128,768]{2,1,0:T(8,128)(2,1)S(1)} %convert_element_type.1107), channel_id=1, source_target_pairs={{8,0},{16,8},{24,16},{9,1},{17,9},{25,17},{10,2},{18,10},{26,18},{... | collective-permute-start | bytes 1179656 | tf_op jit(solution)/shard_map/ppermute | solution.py:17
  512.5 37.3 %collective-permute-start.10 = (bf16[2,128,768]{2,1,0:T(8,128)(2,1)S(1)}, bf16[2,128,768]{2,1,0:T(8,128)(2,1)S(1)}, u32[]{:S(2)}, u32[]{:S(2)}) collective-permute-start(bf16[2,128,768]{2,1,0:T(8,128)(2,1)S(1)} %convert_element_type.1109), channel_id=1, source_target_pairs={{8,0},{16,8},{24,16},{9,1},{17,9},{25,17},{10,2},{18,10},{26,18},{... | collective-permute-start | bytes 1179656 | tf_op jit(solution)/shard_map/ppermute | solution.py:17
  590.3 15.1 %collective-permute-start.11 = (bf16[2,128,768]{2,1,0:T(8,128)(2,1)S(1)}, bf16[2,128,768]{2,1,0:T(8,128)(2,1)S(1)}, u32[]{:S(2)}, u32[]{:S(2)}) collective-permute-start(bf16[2,128,768]{2,1,0:T(8,128)(2,1)S(1)} %convert_element_type.1111), channel_id=1, source_target_pairs={{8,0},{16,8},{24,16},{9,1},{17,9},{25,17},{10,2},{18,10},{26,18},{... | collective-permute-start | bytes 1179656 | tf_op jit(solution)/shard_map/ppermute | solution.py:17
  739.0 366.5 %copy-start = (f32[4,2,128,768]{3,2,1,0:T(8,128)}, f32[4,2,128,768]{3,2,1,0:T(8,128)S(1)}, u32[]{:S(2)}) copy-start(f32[4,2,128,768]{3,2,1,0:T(8,128)S(1)} %bitcast_dynamic-update-slice_fusion) | copy-start | bytes 9437188
  (25 other events, 162.8 us)
Sparse Core Ops, SparseCore 0:
  675.1 421.5 all-reduce.3
where the time goes:
time: 1130 us; the launch traced here: 1120 us
  waiting for transfers between devices  596 us (53%)
  matrix products  131 us (12%)
  other arithmetic  121 us (11%)
  starting transfers between devices  88.3 us (8%)
  loops' own time  67.4 us (6%)
  local copies, waits for them, and re-layouts  63.3 us (6%)
  blocking collectives  32.9 us (3%)
  between operations  16.3 us (1%)
    psum x1, waiting for transfers between devices, local(): lax.psum((merged[0], merged[1], merged[2], merged[3], local_sums), 'dp')  358 us
    ppermute x12, waiting for transfers between devices, passed_along(): return lax.ppermute(block, axis, route)  238 us
    ppermute x12, starting transfers between devices, passed_along(): return lax.ppermute(block, axis, route)  88.3 us
    another operation x7, loops' own time, local(): lax.cond(active, backward_step, backward_skip, kept_in[mb_slot], current,...  50.3 us
    dot_general x8, matrix products, contract_rows(): lax.dot_general(former, latter, (((0,), (0,)), ((), ())), preferred_eleme...  44 us
    another operation x20, local copies, waits for them, and re-layouts  35.2 us
    psum x1, blocking collectives, local(): lax.psum((merged[0], merged[1], merged[2], merged[3], local_sums), 'dp')  32.9 us
    dot_general x4, matrix products, dense_core(): jnp.dot(activation, narrow, preferred_element_type=jnp.float32)  30.9 us
  transfers between devices with their start and end apart: 13, of which 13 were waited for; matrix products, arithmetic and copies ran while one was open for 3% of the time, Pallas kernels for 0%

commit v1 on v0

v1 whole, which is shorter than its diff:
```python
import functools

import jax
import jax.numpy as jnp
from jax import lax
from jax.experimental import pallas as pl
from jax.experimental.pallas import tpu as pltpu
from jax.sharding import PartitionSpec as P

HEAD_DIM = 64
EPS = 1e-05
NEG_FILL = -1e30
MESH = pl.DeviceIdType.MESH
BF16 = jnp.bfloat16
F32 = jnp.float32
NN = (((1,), (0,)), ((), ()))
NT = (((1,), (1,)), ((), ()))
TN = (((0,), (0,)), ((), ()))
PAIR = 2 * HEAD_DIM
TILE = 1536
GELU_C = 0.7978845608028654
GELU_K = 0.044715


def dot(a, b, dims=NN):
    return lax.dot_general(a, b, dims, preferred_element_type=F32)


def gelu_and_slope(x):
    square = x * x
    t = jnp.tanh(GELU_C * (x + GELU_K * (square * x)))
    half = 0.5 * (1.0 + t)
    slope = half + (0.5 * GELU_C) * x * (1.0 - t * t) * (1.0 + (3.0 * GELU_K) * square)
    return x * half, slope


def fold(x):
    return x.reshape(x.shape[0] // 8, 8, x.shape[1]).sum(axis=0)


def normalize(hidden):
    mean = jnp.mean(hidden, axis=-1, keepdims=True)
    centered = hidden - mean
    variance = jnp.mean(centered * centered, axis=-1, keepdims=True)
    inv_std = lax.rsqrt(variance + EPS)
    return centered * inv_std, inv_std


def pipeline_kernel(
    start, cot, first, second, norm, bias, seg, val,
    res_o, sg_o, nrm_o, gin_o, act_o, mid_o, small_o,
    w1, w2, w1t, w2t, hin, hout, gin, gout, nrm, act, mid,
    sq_acc, norm_acc, in_acc, out_acc,
    load_sem, hs_sem, hr_sem, gs_sem, gr_sem, out_sem,
):
    section = lax.axis_index("section")
    dp = lax.axis_index("dp")
    last = lax.axis_size("section") - 1
    rows, seq, dim = start.shape
    ff = first.shape[2]
    pairs = dim // PAIR
    is_attention = section % 2 == 0
    nxt = jnp.minimum(section + 1, last)
    prv = jnp.maximum(section - 1, 0)

    first_load = pltpu.make_async_copy(first.at[0], w1, load_sem.at[0])
    second_load = pltpu.make_async_copy(second.at[0], w2, load_sem.at[1])
    start_load = pltpu.make_async_copy(start, hin, load_sem.at[2])
    cot_load = pltpu.make_async_copy(cot, gin, load_sem.at[3])
    first_load.start()

    @pl.when(section == 0)
    def _():
        start_load.start()

    @pl.when(jnp.logical_not(is_attention))
    def _():
        second_load.start()

    @pl.when(section == last)
    def _():
        cot_load.start()

    barrier = pltpu.get_barrier_semaphore()

    @pl.when(section > 0)
    def _():
        pl.semaphore_signal(barrier, inc=1, device_id=(prv, dp), device_id_type=MESH)

    @pl.when(section < last)
    def _():
        pl.semaphore_signal(barrier, inc=1, device_id=(nxt, dp), device_id_type=MESH)

    pl.semaphore_wait(barrier, jnp.where((section > 0) & (section < last), 2, 1))

    for ref in (sq_acc, norm_acc, in_acc, out_acc):
        ref[...] = jnp.zeros_like(ref)

    def h_copy(i):
        return pltpu.make_async_remote_copy(
            hout.at[i], hin.at[i], hs_sem.at[i], hr_sem.at[i],
            device_id=(nxt, dp), device_id_type=MESH,
        )

    def g_copy(i):
        return pltpu.make_async_remote_copy(
            gout.at[i], gin.at[i], gs_sem.at[i], gr_sem.at[i],
            device_id=(prv, dp), device_id_type=MESH,
        )

    def out_copy(k, i):
        src, dst = (
            (hout, res_o), (gout, sg_o), (nrm, nrm_o), (gin, gin_o), (act, act_o), (mid, mid_o),
        )[k]
        return pltpu.make_async_copy(src.at[i], dst.at[i], out_sem.at[k, i])

    eye = lax.broadcasted_iota(jnp.int32, (seq, seq), 0) == lax.broadcasted_iota(
        jnp.int32, (seq, seq), 1
    )

    def column(row):
        return jnp.sum(jnp.where(eye, row, 0.0), axis=1, keepdims=True)

    def valid_row(i):
        return val[pl.ds(i, 1), :].astype(F32)

    def entry(i):
        @pl.when(section > 0)
        def _():
            h_copy(i).wait_recv()

        hidden = hin[i].astype(F32)
        normal, _ = normalize(hidden)
        low = (normal * norm[0, 0:1, :] + norm[0, 1:2, :]).astype(BF16)
        nrm[i] = low
        return hidden, low

    def leave(i, hidden, branch):
        low = (hidden + branch).astype(BF16)
        hout[i] = low

        @pl.when(section < last)
        def _():
            h_copy(i).start()

        out_copy(0, i).start()
        out_copy(2, i).start()
        weight = column(valid_row(i))
        value = low.astype(F32)
        sq_acc[0] += fold(value * value * weight)
        sq_acc[1] += fold(branch * branch * weight)

    def grad_entry(i):
        @pl.when(section < last)
        def _():
            g_copy(i).wait_recv()

        @pl.when(section == last)
        def _():
            gin[i] = jnp.where(column(valid_row(i)) > 0, gin[i], jnp.zeros((seq, dim), BF16))

        grad = gin[i]
        out_copy(3, i).start()
        return grad

    def grad_leave(i, grad, normed_grad):
        grad_value = grad.astype(F32)
        normal, inv_std = normalize(hin[i].astype(F32))
        scaled = normed_grad * norm[0, 0:1, :]
        mean_one = jnp.mean(scaled, axis=-1, keepdims=True)
        mean_two = jnp.mean(scaled * normal, axis=-1, keepdims=True)
        low = (grad_value + inv_std * (scaled - mean_one - normal * mean_two)).astype(BF16)
        gout[i] = low

        @pl.when(section > 0)
        def _():
            g_copy(i).start()

        out_copy(1, i).start()
        norm_acc[0] += fold(normed_grad * normal)
        norm_acc[1] += fold(normed_grad)
        out_acc[...] += fold(grad_value)


    def dense_forward(i):
        hidden, low = entry(i)
        branch = jnp.zeros((seq, dim), F32)
        for at in range(0, ff, TILE):
            cols = slice(at, at + TILE)
            value, slope = gelu_and_slope(dot(low, w1[:, cols]) + bias[0:1, cols])
            value = value.astype(BF16)
            act[i, :, cols] = value
            mid[i, :, cols] = slope.astype(BF16)
            branch += dot(value, w2[cols, :])
        leave(i, hidden, branch + bias[0:1, ff:])
        out_copy(4, i).start()

    def dense_backward(i):
        grad = grad_entry(i)
        normed_grad = jnp.zeros((seq, dim), F32)
        for at in range(0, ff, TILE):
            cols = slice(at, at + TILE)
            inner = dot(grad, w2t[:, cols]) * mid[i, :, cols].astype(F32)
            low = inner.astype(BF16)
            mid[i, :, cols] = low
            in_acc[:, cols] += fold(low.astype(F32))
            normed_grad += dot(low, w1t[cols, :])
        out_copy(5, i).start()
        grad_leave(i, grad, normed_grad)


    lower = lax.broadcasted_iota(jnp.int32, (seq, PAIR), 1) < HEAD_DIM

    def split_heads(x):
        zero = jnp.zeros_like(x)
        return jnp.concatenate([jnp.where(lower, x, zero), jnp.where(lower, zero, x)], axis=0)

    def join_heads(x):
        return jnp.where(lower, x[:seq], x[seq:])

    def attention_forward(i):
        hidden, low = entry(i)
        projected = dot(low, w1[:, : 3 * dim])
        mid[i, :, :dim] = (projected[:, :dim] + bias[0:1, :dim]).astype(BF16)
        mid[i, :, dim : 2 * dim] = projected[:, dim : 2 * dim].astype(BF16)
        mid[i, :, 2 * dim : 3 * dim] = (
            projected[:, 2 * dim :] + bias[0:1, dim : 2 * dim]
        ).astype(BF16)
        seg_row = seg[pl.ds(i, 1), :].astype(F32)
        allowed = (column(seg_row) == seg_row) & ((valid_row(i) > 0) | eye)
        for p in range(pairs):
            at = p * PAIR
            query = mid[i, :, at : at + PAIR]
            keys = split_heads(mid[i, :, dim + at : dim + at + PAIR])
            values = split_heads(mid[i, :, 2 * dim + at : 2 * dim + at + PAIR])
            scores = dot(query, keys, NT) * HEAD_DIM**-0.5
            probs = []
            for half in (scores[:, :seq], scores[:, seq:]):
                half = jnp.where(allowed, half, NEG_FILL)
                weight = jnp.exp(half - jnp.max(half, axis=-1, keepdims=True))
                probs.append(weight / jnp.sum(weight, axis=-1, keepdims=True))
            prob = jnp.concatenate(probs, axis=1).astype(BF16)
            act[i, :, 2 * seq * p : 2 * seq * (p + 1)] = prob
            mid[i, :, 3 * dim + at : 3 * dim + at + PAIR] = dot(prob, values).astype(BF16)
        branch = dot(mid[i, :, 3 * dim :], w1t[3 * dim :, :]) + bias[0:1, ff:]
        leave(i, hidden, branch)

    def attention_backward(i):
        grad = grad_entry(i)
        mixed_grad = dot(grad, w1[:, 3 * dim :]).astype(BF16)
        for p in range(pairs):
            at = p * PAIR
            query = mid[i, :, at : at + PAIR]
            keys = split_heads(mid[i, :, dim + at : dim + at + PAIR])
            values = split_heads(mid[i, :, 2 * dim + at : 2 * dim + at + PAIR])
            prob = act[i, :, 2 * seq * p : 2 * seq * (p + 1)]
            out_grad = mixed_grad[:, at : at + PAIR]
            prob_grad = dot(out_grad, values, NT)
            prob_value = prob.astype(F32)
            parts = []
            for cols in (slice(0, seq), slice(seq, 2 * seq)):
                pv, pg = prob_value[:, cols], prob_grad[:, cols]
                parts.append(pv * (pg - jnp.sum(pv * pg, axis=-1, keepdims=True)))
            score_grad = jnp.concatenate(parts, axis=1).astype(BF16)
            query_grad = dot(score_grad, keys) * HEAD_DIM**-0.5
            key_grad = join_heads(dot(score_grad, query, TN)) * HEAD_DIM**-0.5
            value_grad = join_heads(dot(prob, out_grad, TN))
            mid[i, :, at : at + PAIR] = query_grad.astype(BF16)
            mid[i, :, dim + at : dim + at + PAIR] = key_grad.astype(BF16)
            mid[i, :, 2 * dim + at : 2 * dim + at + PAIR] = value_grad.astype(BF16)
        out_copy(5, i).start()
        packed = mid[i, :, : 3 * dim]
        normed_grad = dot(packed, w1t[: 3 * dim, :])
        grad_leave(i, grad, normed_grad)
        in_acc[:, :dim] += fold(packed[:, :dim].astype(F32))
        in_acc[:, dim : 2 * dim] += fold(packed[:, 2 * dim :].astype(F32))

    first_load.wait()

    def transpose(src, dst, low, high):
        for at in range(low, high, 2 * PAIR):
            dst[at : at + 2 * PAIR, :] = src[:, at : at + 2 * PAIR].T

    @pl.when(section == 0)
    def _():
        start_load.wait()

    @pl.when(section == last)
    def _():
        cot_load.wait()

    def run(forward, backward, lag, before_last):
        def step(i, carry):
            @pl.when(i == rows - 1)
            def _():
                before_last()

            @pl.when(i < rows)
            def _():
                forward(i)

            @pl.when(i >= lag)
            def _():
                backward(i - lag)

            return carry

        lax.fori_loop(0, rows + lag, step, 0)

    @pl.when(is_attention)
    def _():
        transpose(w1, w1t, 3 * dim, ff)

        def late():
            @pl.when(section == 0)
            def _():
                transpose(w1, w1t, 0, 3 * dim)

        @pl.when(section > 0)
        def _():
            transpose(w1, w1t, 0, 3 * dim)

        lag = jnp.where(section == 0, rows, rows // 2)
        run(attention_forward, attention_backward, lag, late)

    @pl.when(jnp.logical_not(is_attention))
    def _():
        second_load.wait()
        transpose(w1, w1t, 0, ff)
        for at in range(0, ff, 2 * PAIR):
            w2t[:, at : at + 2 * PAIR] = w2[at : at + 2 * PAIR, :].T
        lag = jnp.where(section == last, 0, rows - 1)
        run(dense_forward, dense_backward, lag, lambda: None)


    def total(x):
        return jnp.sum(x, axis=0, keepdims=True)

    lane = lax.broadcasted_iota(jnp.int32, (1, dim), 1)
    counts = jnp.zeros((1, dim), F32)
    for k, x in enumerate((sq_acc[0], sq_acc[1], val[...].astype(F32))):
        amount = jnp.sum(jnp.sum(x, axis=0, keepdims=True), axis=1, keepdims=True)
        counts = jnp.where(lane == k, amount, counts)
    small_o[0:1, :] = total(norm_acc[0])
    small_o[1:2, :] = total(norm_acc[1])
    for k in range(ff // dim):
        small_o[2 + k : 3 + k, :] = total(in_acc[:, k * dim : (k + 1) * dim])
    small_o[2 + ff // dim : 3 + ff // dim, :] = total(out_acc[...])
    small_o[3 + ff // dim : 4 + ff // dim, :] = counts

    def drain(i, carry):
        for k in (0, 1, 2, 3, 5):
            out_copy(k, i).wait()

        @pl.when(jnp.logical_not(is_attention))
        def _():
            out_copy(4, i).wait()

        @pl.when(section < last)
        def _():
            h_copy(i).wait_send()

        @pl.when(section > 0)
        def _():
            g_copy(i).wait_send()

        return carry

    lax.fori_loop(0, rows, drain, 0)


def run_pipeline(start, cot, first, second, norm, bias, seg, val):
    rows, seq, dim = start.shape
    ff = first.shape[2]
    block = (rows, seq, dim)
    wide = (rows, seq, ff)
    any_space = pl.BlockSpec(memory_space=pl.ANY)
    vmem = pl.BlockSpec(memory_space=pltpu.VMEM)
    out = jax.ShapeDtypeStruct
    return pl.pallas_call(
        pipeline_kernel,
        out_shape=(
            out(block, BF16), out(block, BF16), out(block, BF16), out(block, BF16),
            out(wide, BF16), out(wide, BF16), out((4 + ff // dim, dim), F32),
        ),
        in_specs=[any_space] * 4 + [vmem] * 4,
        out_specs=(any_space,) * 6 + (vmem,),
        scratch_shapes=[
            pltpu.VMEM((dim, ff), BF16), pltpu.VMEM((ff, dim), BF16),
            pltpu.VMEM((ff, dim), BF16), pltpu.VMEM((dim, ff), BF16),
            pltpu.VMEM(block, BF16), pltpu.VMEM(block, BF16),
            pltpu.VMEM(block, BF16), pltpu.VMEM(block, BF16),
            pltpu.VMEM(block, BF16), pltpu.VMEM(wide, BF16), pltpu.VMEM(wide, BF16),
            pltpu.VMEM((2, 8, dim), F32), pltpu.VMEM((2, 8, dim), F32),
            pltpu.VMEM((8, ff), F32), pltpu.VMEM((8, dim), F32),
            pltpu.SemaphoreType.DMA((4,)),
            pltpu.SemaphoreType.DMA((rows,)), pltpu.SemaphoreType.DMA((rows,)),
            pltpu.SemaphoreType.DMA((rows,)), pltpu.SemaphoreType.DMA((rows,)),
            pltpu.SemaphoreType.DMA((6, rows)),
        ],
        compiler_params=pltpu.CompilerParams(
            collective_id=0, has_side_effects=True, vmem_limit_bytes=58 * 2**20
        ),
        name="sublayer_pipeline",
    )(start, cot, first, second, norm, bias, seg, val)


def local(start, cot, first, second, norm, bias, seg, val):
    rows, seq, dim = start.shape
    ff = first.shape[2]
    tokens = rows * seq
    is_attention = lax.axis_index("section") % 2 == 0
    res, sg, nrm, gin, act, mid, small = run_pipeline(
        start, cot, first, second, norm, bias, seg, val
    )
    nrm, gin = nrm.reshape(tokens, dim), gin.reshape(tokens, dim)
    act, mid = act.reshape(tokens, ff), mid.reshape(tokens, ff)
    left = dot(nrm, mid[:, : 3 * dim], TN)
    right = dot(jnp.where(is_attention, gin, nrm), mid[:, 3 * dim :], TN)
    wide = jnp.concatenate([left, right], axis=1).astype(BF16)
    narrow = jnp.where(is_attention, 0.0, dot(act, gin, TN)).astype(BF16)
    wide, narrow, small = lax.psum((wide, narrow, small), "dp")
    stat = small[3 + ff // dim]
    rms = jnp.sqrt(stat[:2] / (stat[2] * dim))
    return (
        res[None],
        sg.astype(F32)[None],
        wide.astype(F32)[None],
        narrow.astype(F32)[None],
        small[:2][None],
        small[2 : 3 + ff // dim].reshape(1, -1),
        rms[None],
    )


def solution(mesh):
    in_specs = (
        P("dp", None, None),
        P("dp", None, None),
        P("section", None, None),
        P("section", None, None),
        P("section", None, None),
        P("section", None),
        P("dp", None),
        P("dp", None),
    )
    out_specs = (
        P("section", "dp", None, None),
        P("section", "dp", None, None),
        P("section", None, None),
        P("section", None, None),
        P("section", None, None),
        P("section", None),
        P("section", None),
    )
    return jax.shard_map(local, mesh=mesh, in_specs=in_specs, out_specs=out_specs, check_vma=False)
```

time: 1130 us -> 347 us (0.31); the launches traced: 1120 us -> 345 us
  waiting for transfers between devices: 596 us -> 173 us
  matrix products: 131 us -> 15.1 us
  other arithmetic: 121 us -> 17.7 us
  Pallas kernels: 0 us -> 96 us
  starting transfers between devices: 88.3 us -> 0.04 us
  loops' own time: 67.4 us -> 0 us
  local copies, waits for them, and re-layouts: 63.3 us -> 3.68 us
    ppermute x12 -> x0, waiting for transfers between devices: 238 us -> none  [passed_along(): return lax.ppermute(block, axis, route)]
    psum x1, waiting for transfers between devices: 358 us -> 173 us  [local(): wide, narrow, small = lax.psum((wide, narrow, small), 'dp')]
    dot_general x24 -> x3, matrix products: 131 us -> 15.1 us  [dot(): return lax.dot_general(a, b, dims, preferred_element_type=F32)]
    pallas_call x0 -> x1, Pallas kernels: none -> 96 us  [run_pipeline(): pl.pallas_call(pipeline_kernel, out_shape=(out(block, BF16), out(block, B...]
    ppermute x12 -> x0, starting transfers between devices: 88.3 us -> none  [passed_along(): return lax.ppermute(block, axis, route)]
    another operation x22 -> x0, loops' own time: 67.4 us -> none  [the longest x7 50.3 us: local(): lax.cond(active, backward_step, backward_skip, kept_in[mb_slot], current,...]
    broadcast_in_dim x4, other arithmetic: 53.4 us -> 16.8 us  [the longest x2 10.4 us: local(): wide.astype(F32)[None]]
    another operation x28 -> x0, local copies, waits for them, and re-layouts: 35.2 us -> none
  transfers between devices with their start and end apart: 13 -> 1, of which waited for: 13 -> 1; matrix products, arithmetic and copies ran while one was open for 3% -> 1% of each run, Pallas kernels for 0% -> 0%
where the time goes in v1:
time: 347 us; the launch traced here: 345 us
  waiting for transfers between devices  173 us (50%)
  Pallas kernels  96 us (28%)
  blocking collectives  25.3 us (7%)
  other arithmetic  17.7 us (5%)
  matrix products  15.1 us (4%)
  between operations  14.8 us (4%)
  local copies, waits for them, and re-layouts  3.68 us (1%)
    psum x1, waiting for transfers between devices, local(): wide, narrow, small = lax.psum((wide, narrow, small), 'dp')  173 us
    pallas_call x1, Pallas kernels, run_pipeline(): pl.pallas_call(pipeline_kernel, out_shape=(out(block, BF16), out(block, B...  96 us
    psum x1, blocking collectives, local(): wide, narrow, small = lax.psum((wide, narrow, small), 'dp')  25.3 us
    dot_general x3, matrix products, dot(): return lax.dot_general(a, b, dims, preferred_element_type=F32)  15.1 us
    broadcast_in_dim x2, other arithmetic, local(): wide.astype(F32)[None]  10.4 us
  transfers between devices with their start and end apart: 1, of which 1 were waited for; matrix products, arithmetic and copies ran while one was open for 1% of the time, Pallas kernels for 0%

profile of v1, /device:TPU:3, one launch (start us, length us, event | category | flops | bytes accessed | tf_op | source)
XLA Modules:
  0.0 345.3 jit_solution(2568029928086509614)
XLA Ops:
  7.2 0.0 all-reduce.3.cloned.1.call-start
  7.2 96.0 %sublayer_pipeline.1 = (bf16[8,128,768]{2,1,0:T(8,128)(2,1)}, bf16[8,128,768]{2,1,0:T(8,128)(2,1)}, bf16[8,128,768]{2,1,0:T(8,128)(2,1)}, bf16[8,128,768]{2,1,0:...) custom-call(bf16[8,128,768]{2,1,0:T(8,128)(2,1)} %start.1, ...), custom_call_target="tpu_custom_call" | custom-call | tf_op jit(solution)/shard_map/sublayer_pipeline/pallas_call | solution.py:380
  103.2 0.0 copy-start.1
  103.2 0.0 copy-start.2
  103.3 0.0 copy-start.6
  103.3 9.3 %fusion.2 = bf16[1,3072,768]{2,1,0:T(8,128)(2,1)} fusion(bf16[8,128,3072]{2,1,0:T(8,128)(2,1)} %get-tuple-element.19, bf16[8,128,768]{2,1,0:T(8,128)(2,1)} %get-tuple-element.18, pred[]{:T(512)S(6)} %eq.5), kind=kOutput, calls=%fused_computation.5 | convolution fusion | flops 4836556800 | bytes 12582913 | tf_op jit(solution)/shard_map/dot_general | solution.py:26
  112.5 0.0 copy-done.1
  112.6 0.4 bitcast_select_fusion.1
  112.9 1.5 fusion.5
  114.4 4.3 %convolution_convert_fusion = bf16[768,2304]{1,0:T(8,128)(2,1)S(1)} fusion(bf16[1024,768]{1,0:T(8,128)(2,1)S(1)} %bitcast.30, bf16[1024,3072]{1,0:T(8,128)(2,1)S(1)} %bitcast.34), kind=kOutput, calls=%fused_computation.2 | convolution fusion | flops 3625648128 | bytes 9830400 | tf_op jit(solution)/shard_map/dot_general | solution.py:26
  118.7 2.8 maximum_bitcast_fusion
  121.6 0.0 all-reduce.3.cloned.1.call-update
  121.6 0.7 copy-done.5
  122.3 25.3 %psum.23 = f32[8,768]{1,0:T(8,128)S(1)} all-reduce(f32[8,768]{1,0:T(8,128)S(1)} %copy-done.5), channel_id=1, replica_groups=mesh['section'=4,'dp'=8] {'dp'}, use_global_device_ids=true, to_apply=%region_2.3 | all-reduce | flops 6144 | bytes 49152 | tf_op jit(solution)/shard_map/psum | solution.py:422
  147.6 0.6 slice.34
  148.2 0.6 copy.19
  149.5 0.5 fusion.8
  150.0 0.6 slice_bitcast_fusion.1
  150.6 1.9 bitcast_convert_fusion
  152.6 172.7 %all-reduce.3.cloned.1.call-done = (bf16[1,768,3072]{2,1,0:T(8,128)(2,1)}, bf16[1,3072,768]{2,1,0:T(8,128)(2,1)}) async-done(((bf16[1,768,3072]{2,1,0:T(8,128)(2,1)}, bf16[1,3072,768]{2,1,0:T(8,128)(2,1)}), (bf16[1,768,3072]{2,1,0:T(8,128)(2,1)}, bf16[1,3072,768]{2,1,0:T(8,128)(2,1)})) %all-reduce.3.cloned.1.call-update) | async-done | bytes 9437200 | tf_op jit(solution)/shard_map/psum | solution.py:422
  325.3 7.5 %broadcast_in_dim.33 = f32[1,768,3072]{2,1,0:T(8,128)} convert(bf16[1,768,3072]{2,1,0:T(8,128)(2,1)} %get-tuple-element.21) | non-fusion elementwise | flops 2359296 | bytes 14155776 | tf_op jit(solution)/shard_map/broadcast_in_dim | solution.py:428
  332.8 4.5 %broadcast_in_dim.36 = f32[1,3072,768]{2,1,0:T(8,128)} convert(bf16[1,3072,768]{2,1,0:T(8,128)(2,1)S(1)} %copy-done) | non-fusion elementwise | flops 2359296 | bytes 14155776 | tf_op jit(solution)/shard_map/broadcast_in_dim | solution.py:429
  337.3 0.0 copy-done.3
  337.3 1.1 copy.23
  (9 shorter events, 0.0 us)
Async XLA Ops:
  7.2 318.1 %all-reduce.3.cloned.1.call-start = ((), (), s32[]{:S(2)}) async-start(), calls=%async_computation | async-start | bytes 18874368 | tf_op jit(solution)/shard_map/psum | solution.py:422
  103.2 9.3 %copy-start.1 = (bf16[8,128,768]{2,1,0:T(8,128)(2,1)S(1)}, bf16[8,128,768]{2,1,0:T(8,128)(2,1)}, u32[]{:S(2)}) copy-start(bf16[8,128,768]{2,1,0:T(8,128)(2,1)} %get-tuple-element.16) | copy-start | bytes 4718596
  103.2 9.3 %copy-start.2 = (bf16[8,128,768]{2,1,0:T(8,128)(2,1)S(1)}, bf16[8,128,768]{2,1,0:T(8,128)(2,1)}, u32[]{:S(2)}) copy-start(bf16[8,128,768]{2,1,0:T(8,128)(2,1)} %get-tuple-element.18) | copy-start | bytes 4718596
  103.3 9.7 %copy-start.6 = (bf16[8,128,3072]{2,1,0:T(8,128)(2,1)S(1)}, bf16[8,128,3072]{2,1,0:T(8,128)(2,1)}, u32[]{:S(2)}) copy-start(bf16[8,128,3072]{2,1,0:T(8,128)(2,1)} %get-tuple-element.17) | copy-start | bytes 18874372
  121.6 0.7 copy-start.5
  121.6 29.1 %copy-start.4 = (bf16[8,128,768]{2,1,0:T(8,128)(2,1)S(1)}, bf16[8,128,768]{2,1,0:T(8,128)(2,1)}, u32[]{:S(2)}) copy-start(bf16[8,128,768]{2,1,0:T(8,128)(2,1)} %get-tuple-element.15) | copy-start | bytes 4718596
  325.3 7.5 %copy-start = (bf16[1,3072,768]{2,1,0:T(8,128)(2,1)S(1)}, bf16[1,3072,768]{2,1,0:T(8,128)(2,1)}, u32[]{:S(2)}) copy-start(bf16[1,3072,768]{2,1,0:T(8,128)(2,1)} %get-tuple-element.22) | copy-start | bytes 14155780
  332.8 4.5 %copy-start.3 = (bf16[8,128,768]{2,1,0:T(8,128)(2,1)S(1)}, bf16[8,128,768]{2,1,0:T(8,128)(2,1)}, u32[]{:S(2)}) copy-start(bf16[8,128,768]{2,1,0:T(8,128)(2,1)} %get-tuple-element.14) | copy-start | bytes 4718596
Sparse Core Ops, SparseCore 0:
  121.7 203.5 all-reduce.2

commit v2 on v1

--- a/solution.py
+++ b/solution.py
@@ -18,6 +18,9 @@
 TN = (((0,), (0,)), ((), ()))
 PAIR = 2 * HEAD_DIM
 TILE = 1536
+CHUNK = 256
+SUB = 4
+HANDED = 10
 GELU_C = 0.7978845608028654
 GELU_K = 0.044715
 
@@ -46,13 +49,18 @@
     return centered * inv_std, inv_std
 
 
-def pipeline_kernel(
+def sublayer_kernel(
+    handed,
     start, cot, first, second, norm, bias, seg, val,
-    res_o, sg_o, nrm_o, gin_o, act_o, mid_o, small_o,
-    w1, w2, w1t, w2t, hin, hout, gin, gout, nrm, act, mid,
-    sq_acc, norm_acc, in_acc, out_acc,
-    load_sem, hs_sem, hr_sem, gs_sem, gr_sem, out_sem,
+    res_o, sg_o, first_o, second_o, small_o,
+    w1, w2, w1t, w2t, hin, hout, pair, gout, act, mid,
+    sq_acc, norm_acc, in_acc, out_acc, small,
+    sum_a1, sum_b1, sum_c1, sum_a2, sum_b2, sum_c2,
+    load_sem, hs_sem, hr_sem, gs_sem, gr_sem, out_sem, small_sem,
+    part_send, part_recv, given_recv, line_send, line_recv, whole_recv, back_send,
+    mate_send, mate_recv, store_sem,
 ):
+    nrm, gin = pair.at[0], pair.at[1]
     section = lax.axis_index("section")
     dp = lax.axis_index("dp")
     last = lax.axis_size("section") - 1
@@ -81,17 +89,41 @@
     def _():
         cot_load.start()
 
+    chips = lax.axis_size("dp") // 2
+    chip, core = dp // 2, dp % 2
+    mate = dp + 1 - 2 * core
+    on_left = chip < chips // 2
+    is_middle = (chip == chips // 2 - 1) | (chip == chips // 2)
+    has_outer = (chip > 0) & (chip < chips - 1)
+    inner = jnp.where(on_left, dp + 2, dp - 2)
+    outer = jnp.clip(jnp.where(on_left, dp - 2, dp + 2), 0, 2 * chips - 1)
+    helper = section + 1 - 2 * (section % 2)
+
     barrier = pltpu.get_barrier_semaphore()
 
+    def greet(to_section, to_dp):
+        pl.semaphore_signal(
+            barrier, inc=1, device_id=(to_section, to_dp), device_id_type=MESH
+        )
+
+    greet(section, mate)
+    greet(section, inner)
+
+    @pl.when(has_outer)
+    def _():
+        greet(section, outer)
+
     @pl.when(section > 0)
     def _():
-        pl.semaphore_signal(barrier, inc=1, device_id=(prv, dp), device_id_type=MESH)
+        greet(prv, dp)
 
     @pl.when(section < last)
     def _():
-        pl.semaphore_signal(barrier, inc=1, device_id=(nxt, dp), device_id_type=MESH)
-
-    pl.semaphore_wait(barrier, jnp.where((section > 0) & (section < last), 2, 1))
+        greet(nxt, dp)
+
+    peers = 3 + has_outer.astype(jnp.int32)
+    peers += ((section > 0) & (section < last)).astype(jnp.int32)
+    pl.semaphore_wait(barrier, peers)
 
     for ref in (sq_acc, norm_acc, in_acc, out_acc):
         ref[...] = jnp.zeros_like(ref)
@@ -109,9 +141,7 @@
         )
 
     def out_copy(k, i):
-        src, dst = (
-            (hout, res_o), (gout, sg_o), (nrm, nrm_o), (gin, gin_o), (act, act_o), (mid, mid_o),
-        )[k]
+        src, dst = ((hout, res_o), (gout, sg_o))[k]
         return pltpu.make_async_copy(src.at[i], dst.at[i], out_sem.at[k, i])
 
     eye = lax.broadcasted_iota(jnp.int32, (seq, seq), 0) == lax.broadcasted_iota(
@@ -144,7 +174,6 @@
             h_copy(i).start()
 
         out_copy(0, i).start()
-        out_copy(2, i).start()
         weight = column(valid_row(i))
         value = low.astype(F32)
         sq_acc[0] += fold(value * value * weight)
@@ -159,9 +188,7 @@
         def _():
             gin[i] = jnp.where(column(valid_row(i)) > 0, gin[i], jnp.zeros((seq, dim), BF16))
 
-        grad = gin[i]
-        out_copy(3, i).start()
-        return grad
+        return gin[i]
 
     def grad_leave(i, grad, normed_grad):
         grad_value = grad.astype(F32)
@@ -193,7 +220,6 @@
             mid[i, :, cols] = slope.astype(BF16)
             branch += dot(value, w2[cols, :])
         leave(i, hidden, branch + bias[0:1, ff:])
-        out_copy(4, i).start()
 
     def dense_backward(i):
         grad = grad_entry(i)
@@ -205,7 +231,6 @@
             mid[i, :, cols] = low
             in_acc[:, cols] += fold(low.astype(F32))
             normed_grad += dot(low, w1t[cols, :])
-        out_copy(5, i).start()
         grad_leave(i, grad, normed_grad)
 
 
@@ -268,7 +293,6 @@
             mid[i, :, at : at + PAIR] = query_grad.astype(BF16)
             mid[i, :, dim + at : dim + at + PAIR] = key_grad.astype(BF16)
             mid[i, :, 2 * dim + at : 2 * dim + at + PAIR] = value_grad.astype(BF16)
-        out_copy(5, i).start()
         packed = mid[i, :, : 3 * dim]
         normed_grad = dot(packed, w1t[: 3 * dim, :])
         grad_leave(i, grad, normed_grad)
@@ -341,92 +365,427 @@
     for k, x in enumerate((sq_acc[0], sq_acc[1], val[...].astype(F32))):
         amount = jnp.sum(jnp.sum(x, axis=0, keepdims=True), axis=1, keepdims=True)
         counts = jnp.where(lane == k, amount, counts)
-    small_o[0:1, :] = total(norm_acc[0])
-    small_o[1:2, :] = total(norm_acc[1])
+    small[0, 0:1, :] = total(norm_acc[0])
+    small[0, 1:2, :] = total(norm_acc[1])
     for k in range(ff // dim):
-        small_o[2 + k : 3 + k, :] = total(in_acc[:, k * dim : (k + 1) * dim])
-    small_o[2 + ff // dim : 3 + ff // dim, :] = total(out_acc[...])
-    small_o[3 + ff // dim : 4 + ff // dim, :] = counts
-
-    def drain(i, carry):
-        for k in (0, 1, 2, 3, 5):
-            out_copy(k, i).wait()
+        small[0, 2 + k : 3 + k, :] = total(in_acc[:, k * dim : (k + 1) * dim])
+    small[0, 2 + ff // dim : 3 + ff // dim, :] = total(out_acc[...])
+    small[0, 3 + ff // dim : 4 + ff // dim, :] = counts
+
+    def remote(src, dst, send, recv, to):
+        return pltpu.make_async_remote_copy(
+            src, dst, send, recv, device_id=to, device_id_type=MESH
+        )
+
+    small_mate = remote(
+        small.at[0], small.at[1], small_sem.at[0], small_sem.at[1], (section, mate)
+    )
+    small_line = remote(
+        small.at[0], small.at[2], small_sem.at[2], small_sem.at[3], (section, inner)
+    )
+    small_cross = remote(
+        small.at[0], small.at[3], small_sem.at[2], small_sem.at[4], (section, inner)
+    )
+    small_back = remote(
+        small.at[3], small.at[3], small_sem.at[5], small_sem.at[4], (section, outer)
+    )
+    small_mate.start()
+
+
+    tokens = rows * seq
+    half = ff // 2
+    steps = (half // CHUNK) * SUB
+    tall, short = dim // SUB, CHUNK // SUB
+    mine, theirs = core * half, (1 - core) * half
+
+    def own(k, v):
+        if k == 0:
+            return w1.at[
+                pl.ds(pl.multiple_of((v % SUB) * tall, 16), tall),
+                pl.ds(pl.multiple_of(mine + (v // SUB) * CHUNK, CHUNK), CHUNK),
+            ]
+        return w2.at[pl.ds(pl.multiple_of(mine + v * short, 16), short), :]
+
+    def stored(k, v):
+        if k == 0:
+            return first_o.at[
+                pl.ds(pl.multiple_of((v % SUB) * tall, 16), tall),
+                pl.ds(pl.multiple_of(mine + (v // SUB) * CHUNK, CHUNK), CHUNK),
+            ]
+        return second_o.at[pl.ds(pl.multiple_of(mine + v * short, 16), short), :]
+
+    def slot(ref, k, v):
+        if k == 0:
+            return ref.at[
+                pl.ds(pl.multiple_of((v % SUB) * tall, 16), tall),
+                pl.ds(pl.multiple_of((v // SUB) * CHUNK, CHUNK), CHUNK),
+            ]
+        return ref.at[pl.ds(pl.multiple_of(v * short, 16), short), :]
+
+    near, line, whole = (sum_a1, sum_a2), (sum_b1, sum_b2), (sum_c1, sum_c2)
+
+    def part_copy(k, c):
+        at = pl.ds(pl.multiple_of(theirs + c * CHUNK, CHUNK), CHUNK)
+        to = pl.ds(pl.multiple_of(c * CHUNK, CHUNK), CHUNK)
+        src, dst = (w1.at[:, at], sum_a1.at[:, to]) if k == 0 else (w2.at[at, :], sum_a2.at[to, :])
+        return remote(src, dst, part_send.at[k, c], part_recv.at[k, c], (section, mate))
+
+    def line_copy(k, v):
+        return remote(
+            own(k, v), slot(line[k], k, v), line_send.at[k, v], line_recv.at[k, v], (section, inner)
+        )
+
+    def cross_copy(k, v):
+        return remote(
+            own(k, v), slot(whole[k], k, v), line_send.at[k, v], whole_recv.at[k, v], (section, inner)
+        )
+
+    def given_copy(v):
+        return remote(
+            own(1, v), slot(sum_a2, 1, v), line_send.at[1, v], given_recv.at[v], (helper, dp)
+        )
+
+    def return_copy(v):
+        ref = slot(sum_c2, 1, v)
+        return remote(ref, ref, mate_send.at[1, v], whole_recv.at[1, v], (helper, dp))
+
+    def back_copy(k, v):
+        ref = slot(whole[k], k, v)
+        return remote(ref, ref, back_send.at[k, v], whole_recv.at[k, v], (section, outer))
+
+    def mate_copy(k, v):
+        return remote(
+            slot(whole[k], k, v), stored(k, v), mate_send.at[k, v], mate_recv.at[k, v], (section, mate)
+        )
+
+    def store_copy(k, v):
+        return pltpu.make_async_copy(slot(whole[k], k, v), stored(k, v), store_sem.at[k, v])
+
+    def compute(k, c):
+        for base, is_sent in ((theirs, True), (mine, False)):
+            at = pl.ds(pl.multiple_of(base + c * CHUNK, CHUNK), CHUNK)
+            if k == 0:
+                side = is_attention & (base + c * CHUNK >= 3 * dim)
+                left = pair[side.astype(jnp.int32)].reshape(tokens, dim)
+                right = mid[:, :, at].reshape(tokens, CHUNK)
+                w1[:, at] = dot(left, right, TN).astype(BF16)
+            else:
+                left = act[:, :, at].reshape(tokens, CHUNK)
+                w2[at, :] = dot(left, gin[...].reshape(tokens, dim), TN).astype(BF16)
+            if is_sent:
+                part_copy(k, c).start()
+
+    def combine(dst, *refs):
+        value = refs[0][...].astype(F32)
+        for ref in refs[1:]:
+            value += ref[...].astype(F32)
+        dst[...] = value.astype(BF16)
+
+    def send_in(k, v, *refs):
+        @pl.when(has_outer)
+        def _():
+            line_copy(k, v).wait_recv()
+            combine(own(k, v), *refs, slot(line[k], k, v))
+
+        @pl.when(jnp.logical_not(has_outer))
+        def _():
+            combine(own(k, v), *refs)
+
+        @pl.when(is_middle)
+        def _():
+            cross_copy(k, v).start()
+
+        @pl.when(jnp.logical_not(is_middle))
+        def _():
+            line_copy(k, v).start()
+
+    def send_first(v):
+        @pl.when(v % SUB == 0)
+        def _():
+            part_copy(0, v // SUB).wait_recv()
+
+        send_in(0, v, own(0, v), slot(sum_a1, 0, v))
+
+    def send_second(v):
+        @pl.when(v % SUB == 0)
+        def _():
+            part_copy(1, v // SUB).wait_recv()
+
+        @pl.when(v < handed)
+        def _():
+            combine(own(1, v), own(1, v), slot(sum_a2, 1, v))
+            given_copy(v).start()
+
+        @pl.when(v >= handed)
+        def _():
+            send_in(1, v, own(1, v), slot(sum_a2, 1, v))
+
+    def send_given(v):
+        given_copy(v).wait_recv()
+        send_in(1, v, slot(sum_a2, 1, v))
+
+    def settle(k, v):
+        cross_copy(k, v).wait_recv()
+
+        @pl.when(is_middle)
+        def _():
+            combine(slot(whole[k], k, v), own(k, v), slot(whole[k], k, v))
+
+        @pl.when(has_outer)
+        def _():
+            back_copy(k, v).start()
+
+    def finish(k, v):
+        mate_copy(k, v).start()
+        store_copy(k, v).start()
+
+    def settle_second(v):
+        @pl.when(v < handed)
+        def _():
+            cross_copy(1, v).wait_recv()
+
+        @pl.when(v >= handed)
+        def _():
+            settle(1, v)
+
+        finish(1, v)
+
+    def settle_first(v):
+        settle(0, v)
+        finish(0, v)
+
+    def settle_given(v):
+        settle(1, v)
+        return_copy(v).start()
+
+    def small_in():
+        small_mate.wait_recv()
+        small_mate.wait_send()
+        small[0] += small[1]
+
+        @pl.when(has_outer)
+        def _():
+            small_line.wait_recv()
+            small[0] += small[2]
+
+        @pl.when(is_middle)
+        def _():
+            small_cross.start()
+
+        @pl.when(jnp.logical_not(is_middle))
+        def _():
+            small_line.start()
+
+    def small_settle():
+        small_cross.wait_recv()
+
+        @pl.when(is_middle)
+        def _():
+            small[3] += small[0]
+
+        @pl.when(has_outer)
+        def _():
+            small_back.start()
+
+        small_o[...] = small[3]
+
+    gap = jnp.where(on_left, chips // 2 - 1 - chip, chip - chips // 2)
+    lag = 2 + 6 * gap
+    begin = jnp.where(is_attention, min(steps - handed, steps - SUB), 0)
+
+    @pl.when(jnp.logical_not(is_attention))
+    def _():
+        compute(1, 0)
+
+    def step(u, carry):
+        @pl.when(u < steps)
+        def _():
+            v = u - (steps - handed)
+
+            @pl.when(jnp.logical_not(is_attention))
+            def _():
+                send_second(u)
+
+            @pl.when(is_attention & (v >= 0))
+            def _():
+                send_given(v)
+
+        @pl.when((u >= steps) & (u < 2 * steps))
+        def _():
+            send_first(u - steps)
+
+        t = u - lag
+
+        @pl.when((t >= begin) & is_attention)
+        def _():
+            v = t - (steps - handed)
+
+            @pl.when((v >= 0) & (v < handed))
+            def _():
+                settle_given(v)
+
+            @pl.when((t >= steps) & (t < 2 * steps))
+            def _():
+                settle_first(t - steps)
+
+        @pl.when((t >= handed) & jnp.logical_not(is_attention))
+        def _():
+            @pl.when(t < steps)
+            def _():
+                settle_second(t)
+
+            @pl.when((t >= steps) & (t < 2 * steps))
+            def _():
+                settle_first(t - steps)
+
+            @pl.when(t >= 2 * steps)
+            def _():
+                settle_second(t - 2 * steps)
+
+        @pl.when(u % SUB == 0)
+        def _():
+            c = u // SUB + 1
+
+            @pl.when((c < steps // SUB) & jnp.logical_not(is_attention))
+            def _():
+                compute(1, c)
+
+            @pl.when((c >= steps // SUB) & (c < 2 * (steps // SUB)))
+            def _():
+                compute(0, c - steps // SUB)
+
+        @pl.when(u == steps + SUB)
+        def _():
+            small_in()
+
+        @pl.when(t == steps + SUB)
+        def _():
+            small_settle()
+
+        return carry
+
+    lax.fori_loop(begin, 2 * steps + handed + lag, step, 0)
+
+
+    def drain_streams(i, carry):
+        out_copy(0, i).wait()
+        out_copy(1, i).wait()
+
+        @pl.when(section < last)
+        def _():
+            h_copy(i).wait_send()
+
+        @pl.when(section > 0)
+        def _():
+            g_copy(i).wait_send()
+
+        return carry
+
+    lax.fori_loop(0, rows, drain_streams, 0)
+
+    def drain_chunks(c, carry):
+        part_copy(0, c).wait_send()
 
         @pl.when(jnp.logical_not(is_attention))
         def _():
-            out_copy(4, i).wait()
-
-        @pl.when(section < last)
-        def _():
-            h_copy(i).wait_send()
-
-        @pl.when(section > 0)
-        def _():
-            g_copy(i).wait_send()
+            part_copy(1, c).wait_send()
 
         return carry
 
-    lax.fori_loop(0, rows, drain, 0)
-
-
-def run_pipeline(start, cot, first, second, norm, bias, seg, val):
+    lax.fori_loop(0, steps // SUB, drain_chunks, 0)
+
+    def drain_sums(v, carry):
+        def both(k, there):
+            line_copy(k, v).wait_send()
+
+            @pl.when(there & has_outer)
+            def _():
+                back_copy(k, v).wait_send()
+
+        both(0, True)
+        mate_copy(0, v).wait()
+        store_copy(0, v).wait()
+
+        @pl.when(jnp.logical_not(is_attention))
+        def _():
+            both(1, v >= handed)
+            mate_copy(1, v).wait()
+            store_copy(1, v).wait()
+
+        @pl.when(is_attention & (v < handed))
+        def _():
+            both(1, True)
+            return_copy(v).wait_send()
+
+        return carry
+
+    lax.fori_loop(0, steps, drain_sums, 0)
+    small_line.wait_send()
+
+    @pl.when(has_outer)
+    def _():
+        small_back.wait_send()
+
+
+def run_sublayers(start, cot, first, second, norm, bias, seg, val):
     rows, seq, dim = start.shape
     ff = first.shape[2]
+    half = ff // 2
+    steps = (half // CHUNK) * SUB
     block = (rows, seq, dim)
     wide = (rows, seq, ff)
+    small = (4 + ff // dim, dim)
     any_space = pl.BlockSpec(memory_space=pl.ANY)
     vmem = pl.BlockSpec(memory_space=pltpu.VMEM)
     out = jax.ShapeDtypeStruct
+    dma = pltpu.SemaphoreType.DMA
     return pl.pallas_call(
-        pipeline_kernel,
+        functools.partial(sublayer_kernel, HANDED),
         out_shape=(
-            out(block, BF16), out(block, BF16), out(block, BF16), out(block, BF16),
-            out(wide, BF16), out(wide, BF16), out((4 + ff // dim, dim), F32),
+            out(block, BF16), out(block, BF16), out((dim, ff), BF16), out((ff, dim), BF16),
+            out(small, F32),
         ),
         in_specs=[any_space] * 4 + [vmem] * 4,
-        out_specs=(any_space,) * 6 + (vmem,),
+        out_specs=(any_space,) * 4 + (vmem,),
         scratch_shapes=[
             pltpu.VMEM((dim, ff), BF16), pltpu.VMEM((ff, dim), BF16),
             pltpu.VMEM((ff, dim), BF16), pltpu.VMEM((dim, ff), BF16),
             pltpu.VMEM(block, BF16), pltpu.VMEM(block, BF16),
-            pltpu.VMEM(block, BF16), pltpu.VMEM(block, BF16),
-            pltpu.VMEM(block, BF16), pltpu.VMEM(wide, BF16), pltpu.VMEM(wide, BF16),
+            pltpu.VMEM((2, *block), BF16), pltpu.VMEM(block, BF16),
+            pltpu.VMEM(wide, BF16), pltpu.VMEM(wide, BF16),
             pltpu.VMEM((2, 8, dim), F32), pltpu.VMEM((2, 8, dim), F32),
             pltpu.VMEM((8, ff), F32), pltpu.VMEM((8, dim), F32),
-            pltpu.SemaphoreType.DMA((4,)),
-            pltpu.SemaphoreType.DMA((rows,)), pltpu.SemaphoreType.DMA((rows,)),
-            pltpu.SemaphoreType.DMA((rows,)), pltpu.SemaphoreType.DMA((rows,)),
-            pltpu.SemaphoreType.DMA((6, rows)),
+            pltpu.VMEM((4, *small), F32),
+            pltpu.VMEM((dim, half), BF16), pltpu.VMEM((dim, half), BF16),
+            pltpu.VMEM((dim, half), BF16), pltpu.VMEM((half, dim), BF16),
+            pltpu.VMEM((half, dim), BF16), pltpu.VMEM((half, dim), BF16),
+            dma((4,)), dma((rows,)), dma((rows,)), dma((rows,)), dma((rows,)),
+            dma((2, rows)), dma((6,)),
+            dma((2, steps // SUB)), dma((2, steps // SUB)), dma((steps,)),
+            dma((2, steps)), dma((2, steps)), dma((2, steps)), dma((2, steps)),
+            dma((2, steps)), dma((2, steps)), dma((2, steps)),
         ],
         compiler_params=pltpu.CompilerParams(
-            collective_id=0, has_side_effects=True, vmem_limit_bytes=58 * 2**20
+            collective_id=0, has_side_effects=True, vmem_limit_bytes=60 * 2**20
         ),
-        name="sublayer_pipeline",
+        name="sublayer",
     )(start, cot, first, second, norm, bias, seg, val)
 
 
 def local(start, cot, first, second, norm, bias, seg, val):
     rows, seq, dim = start.shape
     ff = first.shape[2]
-    tokens = rows * seq
     is_attention = lax.axis_index("section") % 2 == 0
-    res, sg, nrm, gin, act, mid, small = run_pipeline(
+    res, sg, wide, narrow, small = run_sublayers(
         start, cot, first, second, norm, bias, seg, val
     )
-    nrm, gin = nrm.reshape(tokens, dim), gin.reshape(tokens, dim)
-    act, mid = act.reshape(tokens, ff), mid.reshape(tokens, ff)
-    left = dot(nrm, mid[:, : 3 * dim], TN)
-    right = dot(jnp.where(is_attention, gin, nrm), mid[:, 3 * dim :], TN)
-    wide = jnp.concatenate([left, right], axis=1).astype(BF16)
-    narrow = jnp.where(is_attention, 0.0, dot(act, gin, TN)).astype(BF16)
-    wide, narrow, small = lax.psum((wide, narrow, small), "dp")
     stat = small[3 + ff // dim]
     rms = jnp.sqrt(stat[:2] / (stat[2] * dim))
     return (
         res[None],
         sg.astype(F32)[None],
         wide.astype(F32)[None],
-        narrow.astype(F32)[None],
+        jnp.where(is_attention, 0.0, narrow.astype(F32))[None],
         small[:2][None],
         small[2 : 3 + ff // dim].reshape(1, -1),
         rms[None],

time: 347 us -> 220 us (0.63)
  waiting for transfers between devices: 173 us -> 0 us
  Pallas kernels: 96 us -> 201 us
  blocking collectives: 25.3 us -> 0 us
  matrix products: 15.1 us -> 0 us
  between operations: 14.8 us -> 1.33 us
    psum x1 -> x0, waiting for transfers between devices: 173 us -> none  [local(): wide, narrow, small = lax.psum((wide, narrow, small), 'dp')]
    pallas_call x1, Pallas kernels: 96 us -> 201 us  [run_sublayers(): pl.pallas_call(functools.partial(sublayer_kernel, HANDED), out_shape=(out...]
    psum x1 -> x0, blocking collectives: 25.3 us -> none  [local(): wide, narrow, small = lax.psum((wide, narrow, small), 'dp')]
    dot_general x3 -> x0, matrix products: 15.1 us -> none  [dot(): return lax.dot_general(a, b, dims, preferred_element_type=F32)]
    broadcast_in_dim x2 -> x1, other arithmetic: 10.4 us -> 5.05 us  [local(): wide.astype(F32)[None]]
  transfers between devices with their start and end apart: 1 -> 0, of which waited for: 1 -> 0; matrix products, arithmetic and copies ran while one was open for 1% -> 0% of each run, Pallas kernels for 0% -> 0%
where the time goes in v2:
time: 220 us
  Pallas kernels  201 us (91%)
  other arithmetic  14.5 us (7%)
  local copies, waits for them, and re-layouts  2.96 us (1%)
    pallas_call x1, Pallas kernels, run_sublayers(): pl.pallas_call(functools.partial(sublayer_kernel, HANDED), out_shape=(out...  201 us
    broadcast_in_dim x1, other arithmetic, local(): jnp.where(is_attention, 0.0, narrow.astype(F32))[None]  6.97 us
    broadcast_in_dim x1, other arithmetic, local(): wide.astype(F32)[None]  5.05 us

profile of v2, /device:TPU:3, one launch (start us, length us, event | category | flops | bytes accessed | tf_op | source)
XLA Modules:
  0.0 219.8 jit_solution(11706797744251925914)
XLA Ops:
  0.6 201.0 %sublayer.1 = (bf16[8,128,768]{2,1,0:T(8,128)(2,1)}, bf16[8,128,768]{2,1,0:T(8,128)(2,1)}, bf16[768,3072]{1,0:T(8,128)(2,1)}, bf16[3072,768]{1,0:T(8,128)(2,1)}, f32[8,768]{1,0:T(8,128)}) custom-call(bf16[8,128,768]{2,1,0:T(8,128)(2,1)} %start.1, bf16[8,128,768]{2,1,0:T(8,128)(2,1)} %cot.1, bf16[1,768,3072]{2,1,0:T(8,128)(2,1)} %first.1, ...), custom_call_target="tpu_custom_call" | custom-call | tf_op jit(solution)/shard_map/sublayer/pallas_call | solution.py:742
  201.7 0.0 copy-start.3
  201.7 0.0 copy-start
  201.7 7.0 %select_bitcast_fusion = f32[1,3072,768]{2,1,0:T(8,128)} fusion(bf16[3072,768]{1,0:T(8,128)(2,1)} %get-tuple-element.15, pred[]{:T(512)S(6)} %eq.5), kind=kLoop, calls=%fused_computation | loop fusion | flops 4718592 | bytes 14155777 | tf_op jit(solution)/shard_map/broadcast_in_dim | solution.py:788
  208.7 0.0 copy-done.3
  208.7 0.6 slice.20
  209.9 0.5 divide_sqrt_fusion
  210.4 0.6 copy.15
  211.1 0.6 slice_bitcast_fusion.1
  211.6 0.0 copy-done
  211.7 0.0 copy-start.2
  211.7 5.0 %bitcast_convert_fusion = f32[1,768,3072]{2,1,0:T(8,128)} fusion(bf16[768,3072]{1,0:T(8,128)(2,1)S(1)} %copy-done), kind=kLoop, calls=%fused_computation.1 | loop fusion | flops 2359296 | bytes 14155776 | tf_op jit(solution)/shard_map/broadcast_in_dim | solution.py:787
  216.7 0.0 copy-start.1
  216.7 0.0 copy-done.2
  216.7 1.9 bitcast_convert_fusion.1
  218.7 0.0 copy-done.1
  218.7 1.1 copy.17
  (1 shorter events, 0.0 us)
Async XLA Ops:
  201.7 7.0 %copy-start.3 = (f32[8,768]{1,0:T(8,128)S(1)}, f32[8,768]{1,0:T(8,128)}, u32[]{:S(2)}) copy-start(f32[8,768]{1,0:T(8,128)} %get-tuple-element.16) | copy-start | bytes 73732
  201.7 10.0 %copy-start = (bf16[768,3072]{1,0:T(8,128)(2,1)S(1)}, bf16[768,3072]{1,0:T(8,128)(2,1)}, u32[]{:S(2)}) copy-start(bf16[768,3072]{1,0:T(8,128)(2,1)} %get-tuple-element.14) | copy-start | bytes 14155780
  211.7 5.1 %copy-start.2 = (bf16[8,128,768]{2,1,0:T(8,128)(2,1)S(1)}, bf16[8,128,768]{2,1,0:T(8,128)(2,1)}, u32[]{:S(2)}) copy-start(bf16[8,128,768]{2,1,0:T(8,128)(2,1)} %get-tuple-element.13) | copy-start | bytes 4718596
  216.7 2.0 copy-start.1

commit v3 on v2

--- a/solution.py
+++ b/solution.py
@@ -21,6 +21,10 @@
 CHUNK = 256
 SUB = 4
 HANDED = 10
+LOADS = 4
+WRITES = 12
+SUBLAYER_VMEM = 50 * 2**20
+FINISH_VMEM = 40 * 2**20
 GELU_C = 0.7978845608028654
 GELU_K = 0.044715
 
@@ -51,14 +55,14 @@
 
 def sublayer_kernel(
     handed,
-    start, cot, first, second, norm, bias, seg, val,
-    res_o, sg_o, first_o, second_o, small_o,
-    w1, w2, w1t, w2t, hin, hout, pair, gout, act, mid,
-    sq_acc, norm_acc, in_acc, out_acc, small,
-    sum_a1, sum_b1, sum_c1, sum_a2, sum_b2, sum_c2,
-    load_sem, hs_sem, hr_sem, gs_sem, gr_sem, out_sem, small_sem,
+    start, cot, first, second, norm_in, bias_in, seg_in, val_in,
+    hout, gout, first_o, second_o, small_o,
+    w1, w2, w1t, w2t, hin, pair, act, mid,
+    norm, bias, seg, val, sq_acc, norm_acc, in_acc, out_acc, small,
+    sum_a1, sum_b1, sum_a2, sum_b2,
+    load_sem, hs_sem, hr_sem, gs_sem, gr_sem, small_sem,
     part_send, part_recv, given_recv, line_send, line_recv, whole_recv, back_send,
-    mate_send, mate_recv, store_sem,
+    mate_send, mate_recv,
 ):
     nrm, gin = pair.at[0], pair.at[1]
     section = lax.axis_index("section")
@@ -75,15 +79,32 @@
     second_load = pltpu.make_async_copy(second.at[0], w2, load_sem.at[1])
     start_load = pltpu.make_async_copy(start, hin, load_sem.at[2])
     cot_load = pltpu.make_async_copy(cot, gin, load_sem.at[3])
-    first_load.start()
+    small_loads = [
+        pltpu.make_async_copy(src, dst, load_sem.at[4 + k])
+        for k, (src, dst) in enumerate(
+            ((norm_in, norm), (bias_in, bias), (seg_in, seg), (val_in, val))
+        )
+    ]
+
+    def split_load(src, dst, k):
+        count = dst.shape[0] // LOADS
+        for at in range(0, dst.shape[0], count):
+            pltpu.make_async_copy(
+                src.at[0, pl.ds(at, count)], dst.at[pl.ds(at, count)], load_sem.at[k]
+            ).start()
+
+    split_load(first, w1, 0)
 
     @pl.when(section == 0)
     def _():
         start_load.start()
 
+    for load in small_loads:
+        load.start()
+
     @pl.when(jnp.logical_not(is_attention))
     def _():
-        second_load.start()
+        split_load(second, w2, 1)
 
     @pl.when(section == last)
     def _():
@@ -123,26 +144,21 @@
 
     peers = 3 + has_outer.astype(jnp.int32)
     peers += ((section > 0) & (section < last)).astype(jnp.int32)
-    pl.semaphore_wait(barrier, peers)
 
     for ref in (sq_acc, norm_acc, in_acc, out_acc):
         ref[...] = jnp.zeros_like(ref)
 
     def h_copy(i):
         return pltpu.make_async_remote_copy(
-            hout.at[i], hin.at[i], hs_sem.at[i], hr_sem.at[i],
+            hout.at[i], hin.at[i], hs_sem, hr_sem.at[i],
             device_id=(nxt, dp), device_id_type=MESH,
         )
 
     def g_copy(i):
         return pltpu.make_async_remote_copy(
-            gout.at[i], gin.at[i], gs_sem.at[i], gr_sem.at[i],
+            gout.at[i], gin.at[i], gs_sem, gr_sem.at[i],
             device_id=(prv, dp), device_id_type=MESH,
         )
-
-    def out_copy(k, i):
-        src, dst = ((hout, res_o), (gout, sg_o))[k]
-        return pltpu.make_async_copy(src.at[i], dst.at[i], out_sem.at[k, i])
 
     eye = lax.broadcasted_iota(jnp.int32, (seq, seq), 0) == lax.broadcasted_iota(
         jnp.int32, (seq, seq), 1
@@ -173,7 +189,6 @@
         def _():
             h_copy(i).start()
 
-        out_copy(0, i).start()
         weight = column(valid_row(i))
         value = low.astype(F32)
         sq_acc[0] += fold(value * value * weight)
@@ -203,7 +218,6 @@
         def _():
             g_copy(i).start()
 
-        out_copy(1, i).start()
         norm_acc[0] += fold(normed_grad * normal)
         norm_acc[1] += fold(normed_grad)
         out_acc[...] += fold(grad_value)
@@ -299,6 +313,8 @@
         in_acc[:, :dim] += fold(packed[:, :dim].astype(F32))
         in_acc[:, dim : 2 * dim] += fold(packed[:, 2 * dim :].astype(F32))
 
+    for load in small_loads:
+        load.wait()
     first_load.wait()
 
     def transpose(src, dst, low, high):
@@ -314,6 +330,8 @@
         cot_load.wait()
 
     def run(forward, backward, lag, before_last):
+        pl.semaphore_wait(barrier, peers)
+
         def step(i, carry):
             @pl.when(i == rows - 1)
             def _():
@@ -406,7 +424,7 @@
             ]
         return w2.at[pl.ds(pl.multiple_of(mine + v * short, 16), short), :]
 
-    def stored(k, v):
+    def whole(k, v):
         if k == 0:
             return first_o.at[
                 pl.ds(pl.multiple_of((v % SUB) * tall, 16), tall),
@@ -422,44 +440,40 @@
             ]
         return ref.at[pl.ds(pl.multiple_of(v * short, 16), short), :]
 
-    near, line, whole = (sum_a1, sum_a2), (sum_b1, sum_b2), (sum_c1, sum_c2)
+    line = (sum_b1, sum_b2)
 
     def part_copy(k, c):
         at = pl.ds(pl.multiple_of(theirs + c * CHUNK, CHUNK), CHUNK)
         to = pl.ds(pl.multiple_of(c * CHUNK, CHUNK), CHUNK)
         src, dst = (w1.at[:, at], sum_a1.at[:, to]) if k == 0 else (w2.at[at, :], sum_a2.at[to, :])
-        return remote(src, dst, part_send.at[k, c], part_recv.at[k, c], (section, mate))
+        return remote(src, dst, part_send.at[k], part_recv.at[k, c], (section, mate))
 
     def line_copy(k, v):
         return remote(
-            own(k, v), slot(line[k], k, v), line_send.at[k, v], line_recv.at[k, v], (section, inner)
+            own(k, v), slot(line[k], k, v), line_send.at[k], line_recv.at[k, v], (section, inner)
         )
 
     def cross_copy(k, v):
         return remote(
-            own(k, v), slot(whole[k], k, v), line_send.at[k, v], whole_recv.at[k, v], (section, inner)
+            own(k, v), whole(k, v), line_send.at[k], whole_recv.at[k, v], (section, inner)
         )
 
     def given_copy(v):
         return remote(
-            own(1, v), slot(sum_a2, 1, v), line_send.at[1, v], given_recv.at[v], (helper, dp)
+            own(1, v), slot(sum_a2, 1, v), line_send.at[1], given_recv.at[v], (helper, dp)
         )
 
     def return_copy(v):
-        ref = slot(sum_c2, 1, v)
-        return remote(ref, ref, mate_send.at[1, v], whole_recv.at[1, v], (helper, dp))
+        ref = whole(1, v)
+        return remote(ref, ref, mate_send.at[1], whole_recv.at[1, v], (helper, dp))
 
     def back_copy(k, v):
-        ref = slot(whole[k], k, v)
-        return remote(ref, ref, back_send.at[k, v], whole_recv.at[k, v], (section, outer))
+        ref = whole(k, v)
+        return remote(ref, ref, back_send.at[k], whole_recv.at[k, v], (section, outer))
 
     def mate_copy(k, v):
-        return remote(
-            slot(whole[k], k, v), stored(k, v), mate_send.at[k, v], mate_recv.at[k, v], (section, mate)
-        )
-
-    def store_copy(k, v):
-        return pltpu.make_async_copy(slot(whole[k], k, v), stored(k, v), store_sem.at[k, v])
+        ref = whole(k, v)
+        return remote(ref, ref, mate_send.at[k], mate_recv.at[k], (section, mate))
 
     def compute(k, c):
         for base, is_sent in ((theirs, True), (mine, False)):
@@ -529,15 +543,11 @@
 
         @pl.when(is_middle)
         def _():
-            combine(slot(whole[k], k, v), own(k, v), slot(whole[k], k, v))
+            combine(whole(k, v), own(k, v), whole(k, v))
 
         @pl.when(has_outer)
         def _():
             back_copy(k, v).start()
-
-    def finish(k, v):
-        mate_copy(k, v).start()
-        store_copy(k, v).start()
 
     def settle_second(v):
         @pl.when(v < handed)
@@ -548,11 +558,11 @@
         def _():
             settle(1, v)
 
-        finish(1, v)
+        mate_copy(1, v).start()
 
     def settle_first(v):
         settle(0, v)
-        finish(0, v)
+        mate_copy(0, v).start()
 
     def settle_given(v):
         settle(1, v)
@@ -667,64 +677,85 @@
     lax.fori_loop(begin, 2 * steps + handed + lag, step, 0)
 
 
-    def drain_streams(i, carry):
-        out_copy(0, i).wait()
-        out_copy(1, i).wait()
-
-        @pl.when(section < last)
-        def _():
-            h_copy(i).wait_send()
-
-        @pl.when(section > 0)
-        def _():
-            g_copy(i).wait_send()
-
-        return carry
-
-    lax.fori_loop(0, rows, drain_streams, 0)
-
-    def drain_chunks(c, carry):
-        part_copy(0, c).wait_send()
-
-        @pl.when(jnp.logical_not(is_attention))
-        def _():
-            part_copy(1, c).wait_send()
-
-        return carry
-
-    lax.fori_loop(0, steps // SUB, drain_chunks, 0)
-
-    def drain_sums(v, carry):
-        def both(k, there):
-            line_copy(k, v).wait_send()
-
-            @pl.when(there & has_outer)
-            def _():
-                back_copy(k, v).wait_send()
-
-        both(0, True)
-        mate_copy(0, v).wait()
-        store_copy(0, v).wait()
-
-        @pl.when(jnp.logical_not(is_attention))
-        def _():
-            both(1, v >= handed)
-            mate_copy(1, v).wait()
-            store_copy(1, v).wait()
-
-        @pl.when(is_attention & (v < handed))
-        def _():
-            both(1, True)
-            return_copy(v).wait_send()
-
-        return carry
-
-    lax.fori_loop(0, steps, drain_sums, 0)
+    @pl.when(section < last)
+    def _():
+        remote(hout, hin, hs_sem, hr_sem.at[0], (nxt, dp)).wait_send()
+
+    @pl.when(section > 0)
+    def _():
+        remote(gout, gin, gs_sem, gr_sem.at[0], (prv, dp)).wait_send()
+
+    def taken(k, sem, count):
+        if k == 0:
+            ref = w1.at[:, pl.ds(0, (count // SUB) * CHUNK)]
+        else:
+            ref = w2.at[pl.ds(0, count * short), :]
+        pltpu.make_async_copy(ref, ref, sem.at[k]).wait()
+
+    taken(0, part_send, steps)
+    taken(0, line_send, steps)
+    taken(0, mate_send, steps)
+    taken(0, mate_recv, steps)
+
+    @pl.when(has_outer)
+    def _():
+        taken(0, back_send, steps)
+        small_back.wait_send()
+
+    @pl.when(jnp.logical_not(is_attention))
+    def _():
+        taken(1, part_send, steps)
+        taken(1, line_send, steps)
+        taken(1, mate_send, steps)
+        taken(1, mate_recv, steps)
+
+        @pl.when(has_outer)
+        def _():
+            taken(1, back_send, steps - handed)
+
+    @pl.when(is_attention)
+    def _():
+        taken(1, line_send, handed)
+        taken(1, mate_send, handed)
+
+        @pl.when(has_outer)
+        def _():
+            taken(1, back_send, handed)
+
+        second_o[...] = jnp.zeros_like(second_o)
+
     small_line.wait_send()
 
-    @pl.when(has_outer)
-    def _():
-        small_back.wait_send()
+
+def finish_kernel(
+    res, sg, first, second, small,
+    res_o, sg_o, first_o, second_o, norm_o, bias_o, rms_o,
+    sg_wide, first_wide, second_wide, sem, first_sem, second_sem,
+):
+    rows, _, dim = sg.shape
+    ff = first.shape[1]
+    copies = [pltpu.make_async_copy(res, res_o.at[0], sem.at[0])]
+    copies[0].start()
+    for src, wide, dst, sems in (
+        (first, first_wide, first_o, first_sem), (second, second_wide, second_o, second_sem),
+    ):
+        count = src.shape[0] // WRITES
+        for k in range(WRITES):
+            at = pl.ds(k * count, count)
+            wide[at, :] = src[at, :].astype(F32)
+            copies.append(pltpu.make_async_copy(wide.at[at], dst.at[0, at], sems.at[k]))
+            copies[-1].start()
+    sg_wide[...] = sg[...].astype(F32)
+    copies.append(pltpu.make_async_copy(sg_wide, sg_o.at[0], sem.at[1]))
+    copies[-1].start()
+    norm_o[0] = small[0:2, :]
+    count = ff // dim + 1
+    for k in range(count):
+        bias_o[0:1, k * dim : (k + 1) * dim] = small[2 + k : 3 + k, :]
+    stat = small[2 + count : 3 + count, :]
+    rms_o[...] = jnp.sqrt(stat[:, 0:2] / (stat[:, 2:3] * dim))
+    for copy in copies:
+        copy.wait()
 
 
 def run_sublayers(start, cot, first, second, norm, bias, seg, val):
@@ -742,54 +773,63 @@
     return pl.pallas_call(
         functools.partial(sublayer_kernel, HANDED),
         out_shape=(
-            out(block, BF16), out(block, BF16), out((dim, ff), BF16), out((ff, dim), BF16),
-            out(small, F32),
+            pltpu.VMEM(block, BF16), pltpu.VMEM(block, BF16),
+            pltpu.VMEM((dim, ff), BF16), pltpu.VMEM((ff, dim), BF16), pltpu.VMEM(small, F32),
         ),
-        in_specs=[any_space] * 4 + [vmem] * 4,
-        out_specs=(any_space,) * 4 + (vmem,),
+        in_specs=[any_space] * 8,
+        out_specs=(vmem,) * 5,
         scratch_shapes=[
             pltpu.VMEM((dim, ff), BF16), pltpu.VMEM((ff, dim), BF16),
             pltpu.VMEM((ff, dim), BF16), pltpu.VMEM((dim, ff), BF16),
-            pltpu.VMEM(block, BF16), pltpu.VMEM(block, BF16),
-            pltpu.VMEM((2, *block), BF16), pltpu.VMEM(block, BF16),
+            pltpu.VMEM(block, BF16), pltpu.VMEM((2, *block), BF16),
             pltpu.VMEM(wide, BF16), pltpu.VMEM(wide, BF16),
+            pltpu.VMEM(norm.shape, F32), pltpu.VMEM(bias.shape, F32),
+            pltpu.VMEM(seg.shape, jnp.int32), pltpu.VMEM(val.shape, jnp.int32),
             pltpu.VMEM((2, 8, dim), F32), pltpu.VMEM((2, 8, dim), F32),
             pltpu.VMEM((8, ff), F32), pltpu.VMEM((8, dim), F32),
             pltpu.VMEM((4, *small), F32),
             pltpu.VMEM((dim, half), BF16), pltpu.VMEM((dim, half), BF16),
-            pltpu.VMEM((dim, half), BF16), pltpu.VMEM((half, dim), BF16),
             pltpu.VMEM((half, dim), BF16), pltpu.VMEM((half, dim), BF16),
-            dma((4,)), dma((rows,)), dma((rows,)), dma((rows,)), dma((rows,)),
-            dma((2, rows)), dma((6,)),
-            dma((2, steps // SUB)), dma((2, steps // SUB)), dma((steps,)),
-            dma((2, steps)), dma((2, steps)), dma((2, steps)), dma((2, steps)),
-            dma((2, steps)), dma((2, steps)), dma((2, steps)),
+            dma((8,)), dma, dma((rows,)), dma, dma((rows,)), dma((6,)),
+            dma((2,)), dma((2, steps // SUB)), dma((HANDED,)),
+            dma((2,)), dma((2, steps)), dma((2, steps)), dma((2,)),
+            dma((2,)), dma((2,)),
         ],
         compiler_params=pltpu.CompilerParams(
-            collective_id=0, has_side_effects=True, vmem_limit_bytes=60 * 2**20
+            collective_id=0, has_side_effects=True, vmem_limit_bytes=SUBLAYER_VMEM
         ),
         name="sublayer",
     )(start, cot, first, second, norm, bias, seg, val)
 
 
+def run_finish(res, sg, first, second, small):
+    rows, seq, dim = res.shape
+    ff = first.shape[1]
+    any_space = pl.BlockSpec(memory_space=pl.ANY)
+    vmem = pl.BlockSpec(memory_space=pltpu.VMEM)
+    out = jax.ShapeDtypeStruct
+    dma = pltpu.SemaphoreType.DMA
+    return pl.pallas_call(
+        finish_kernel,
+        out_shape=(
+            out((1, rows, seq, dim), BF16), out((1, rows, seq, dim), F32),
+            out((1, dim, ff), F32), out((1, ff, dim), F32),
+            out((1, 2, dim), F32), out((1, ff + dim), F32), out((1, 2), F32),
+        ),
+        in_specs=[vmem] * 5,
+        out_specs=(any_space,) * 4 + (vmem,) * 3,
+        scratch_shapes=[
+            pltpu.VMEM((rows, seq, dim), F32),
+            pltpu.VMEM((dim, ff), F32), pltpu.VMEM((ff, dim), F32),
+            dma((2,)), dma((WRITES,)), dma((WRITES,)),
+        ],
+        compiler_params=pltpu.CompilerParams(vmem_limit_bytes=FINISH_VMEM),
+        name="finish",
+    )(res, sg, first, second, small)
+
+
 def local(start, cot, first, second, norm, bias, seg, val):
-    rows, seq, dim = start.shape
-    ff = first.shape[2]
-    is_attention = lax.axis_index("section") % 2 == 0
-    res, sg, wide, narrow, small = run_sublayers(
-        start, cot, first, second, norm, bias, seg, val
-    )
-    stat = small[3 + ff // dim]
-    rms = jnp.sqrt(stat[:2] / (stat[2] * dim))
-    return (
-        res[None],
-        sg.astype(F32)[None],
-        wide.astype(F32)[None],
-        jnp.where(is_attention, 0.0, narrow.astype(F32))[None],
-        small[:2][None],
-        small[2 : 3 + ff // dim].reshape(1, -1),
-        rms[None],
-    )
+    return run_finish(*run_sublayers(start, cot, first, second, norm, bias, seg, val))
 
 
 def solution(mesh):

time: 220 us -> 206 us (0.936)
  other arithmetic: 14.5 us -> 0 us
  Pallas kernels: 201 us -> 205 us
  local copies, waits for them, and re-layouts: 2.96 us -> 0 us
    broadcast_in_dim x3 -> x0, other arithmetic: 14 us -> none  [the longest x1 6.97 us: local(): jnp.where(is_attention, 0.0, narrow.astype(F32))[None]]
    pallas_call x1 -> x2, Pallas kernels: 201 us -> 205 us  [the longest x1 197 us: run_sublayers(): pl.pallas_call(functools.partial(sublayer_kernel, HANDED), out_shape=(plt...]
where the time goes in v3:
time: 206 us
  Pallas kernels  205 us (100%)
    pallas_call x1, Pallas kernels, run_sublayers(): pl.pallas_call(functools.partial(sublayer_kernel, HANDED), out_shape=(plt...  197 us
    pallas_call x1, Pallas kernels, run_finish(): pl.pallas_call(finish_kernel, out_shape=(out((1, rows, seq, dim), BF16),...  8.83 us

profile of v3, /device:TPU:3, one launch (start us, length us, event | category | flops | bytes accessed | tf_op | source)
XLA Modules:
  0.0 206.3 jit_solution(17233491450974127184)
XLA Ops:
  0.6 196.7 %sublayer.1 = (bf16[8,128,768]{2,1,0:T(8,128)(2,1)S(1)}, bf16[8,128,768]{2,1,0:T(8,128)(2,1)S(1)}, bf16[768,3072]{1,0:T(8,128)(2,1)S(1)}, bf16[3072,768]{1,0:T(8,128)(2,1)S(1)}, f32[8,768]{1,0:T(8,128)S(1)}) custom-call(bf16[8,128,768]{2,1,0:T(8,128)(2,1)} %start.1, bf16[8,128,768]{2,1,0:T(8,128)(2,1)} %cot.1, bf16[1,768,3072]{2,1,0:T(8,128)(2,1)} %first.1, ...), custom_call_target="tpu_custom_call" | custom-call | tf_op jit(solution)/shard_map/sublayer/pallas_call | solution.py:773
  197.3 8.8 %finish.1 = (bf16[1,8,128,768]{3,2,1,0:T(8,128)(2,1)}, f32[1,8,128,768]{3,2,1,0:T(8,128)}, f32[1,768,3072]{2,1,0:T(8,128)}, f32[1,3072,768]{2,1,0:T(8,128)}, f32...) custom-call(bf16[8,128,768]{2,1,0:T(8,128)(2,1)S(1)} %get-tuple-element.12.res, ...), custom_call_target="tpu_custom_call" | custom-call | tf_op jit(solution)/shard_map/finish/pallas_call | solution.py:812

commit v4 on v3

--- a/solution.py
+++ b/solution.py
@@ -1,5 +1,3 @@
-import functools
-
 import jax
 import jax.numpy as jnp
 from jax import lax
@@ -20,7 +18,8 @@
 TILE = 1536
 CHUNK = 256
 SUB = 4
-HANDED = 10
+NEAR = (6, 5)
+FAR = 9
 LOADS = 4
 WRITES = 12
 SUBLAYER_VMEM = 50 * 2**20
@@ -54,7 +53,6 @@
 
 
 def sublayer_kernel(
-    handed,
     start, cot, first, second, norm_in, bias_in, seg_in, val_in,
     hout, gout, first_o, second_o, small_o,
     w1, w2, w1t, w2t, hin, pair, act, mid,
@@ -119,6 +117,9 @@
     inner = jnp.where(on_left, dp + 2, dp - 2)
     outer = jnp.clip(jnp.where(on_left, dp - 2, dp + 2), 0, 2 * chips - 1)
     helper = section + 1 - 2 * (section % 2)
+    near = jnp.where(section < 2, NEAR[0], NEAR[1])
+    far = jnp.where((section == 1) | (section == 2), FAR, 0)
+    handed = near + far
 
     barrier = pltpu.get_barrier_semaphore()
 
@@ -459,13 +460,12 @@
         )
 
     def given_copy(v):
-        return remote(
-            own(1, v), slot(sum_a2, 1, v), line_send.at[1], given_recv.at[v], (helper, dp)
-        )
-
-    def return_copy(v):
+        to = jnp.where(v < near, helper, nxt)
+        return remote(own(1, v), slot(sum_a2, 1, v), line_send.at[1], given_recv.at[v], (to, dp))
+
+    def return_copy(v, to):
         ref = whole(1, v)
-        return remote(ref, ref, mate_send.at[1], whole_recv.at[1, v], (helper, dp))
+        return remote(ref, ref, mate_send.at[1], whole_recv.at[1, v], (to, dp))
 
     def back_copy(k, v):
         ref = whole(k, v)
@@ -564,9 +564,9 @@
         settle(0, v)
         mate_copy(0, v).start()
 
-    def settle_given(v):
+    def settle_given(v, to):
         settle(1, v)
-        return_copy(v).start()
+        return_copy(v, to).start()
 
     def small_in():
         small_mate.wait_recv()
@@ -601,24 +601,24 @@
 
     gap = jnp.where(on_left, chips // 2 - 1 - chip, chip - chips // 2)
     lag = 2 + 6 * gap
-    begin = jnp.where(is_attention, min(steps - handed, steps - SUB), 0)
+    begin = jnp.where(is_attention, jnp.minimum(steps - near, steps - SUB), 0)
 
     @pl.when(jnp.logical_not(is_attention))
     def _():
         compute(1, 0)
 
     def step(u, carry):
-        @pl.when(u < steps)
-        def _():
-            v = u - (steps - handed)
-
-            @pl.when(jnp.logical_not(is_attention))
-            def _():
-                send_second(u)
-
-            @pl.when(is_attention & (v >= 0))
-            def _():
-                send_given(v)
+        @pl.when((u < steps) & jnp.logical_not(is_attention))
+        def _():
+            send_second(u)
+
+        @pl.when((u < steps) & (u >= steps - near) & is_attention)
+        def _():
+            send_given(u - (steps - near))
+
+        @pl.when((u >= 2 * steps) & (u < 2 * steps + far) & is_attention)
+        def _():
+            send_given(NEAR[0] + u - 2 * steps)
 
         @pl.when((u >= steps) & (u < 2 * steps))
         def _():
@@ -628,11 +628,13 @@
 
         @pl.when((t >= begin) & is_attention)
         def _():
-            v = t - (steps - handed)
-
-            @pl.when((v >= 0) & (v < handed))
-            def _():
-                settle_given(v)
+            @pl.when((t >= steps - near) & (t < steps))
+            def _():
+                settle_given(t - (steps - near), helper)
+
+            @pl.when((t >= 2 * steps) & (t < 2 * steps + far))
+            def _():
+                settle_given(NEAR[0] + t - 2 * steps, prv)
 
             @pl.when((t >= steps) & (t < 2 * steps))
             def _():
@@ -674,7 +676,8 @@
 
         return carry
 
-    lax.fori_loop(begin, 2 * steps + handed + lag, step, 0)
+    tail = jnp.where(is_attention, far, handed)
+    lax.fori_loop(begin, 2 * steps + tail + lag, step, 0)
 
 
     @pl.when(section < last)
@@ -709,22 +712,29 @@
         taken(1, mate_send, steps)
         taken(1, mate_recv, steps)
 
-        @pl.when(has_outer)
-        def _():
-            taken(1, back_send, steps - handed)
+    for which, count in enumerate((NEAR[0], NEAR[0] + FAR, NEAR[1] + FAR, NEAR[1])):
+        if which % 2:
+
+            @pl.when((section == which) & has_outer)
+            def _(count=count):
+                taken(1, back_send, steps - count)
+
+        else:
+
+            @pl.when(section == which)
+            def _(count=count):
+                taken(1, line_send, count)
+                taken(1, mate_send, count)
+
+            @pl.when((section == which) & has_outer)
+            def _(count=count):
+                taken(1, back_send, count)
+
+    small_line.wait_send()
 
     @pl.when(is_attention)
     def _():
-        taken(1, line_send, handed)
-        taken(1, mate_send, handed)
-
-        @pl.when(has_outer)
-        def _():
-            taken(1, back_send, handed)
-
         second_o[...] = jnp.zeros_like(second_o)
-
-    small_line.wait_send()
 
 
 def finish_kernel(
@@ -771,7 +781,7 @@
     out = jax.ShapeDtypeStruct
     dma = pltpu.SemaphoreType.DMA
     return pl.pallas_call(
-        functools.partial(sublayer_kernel, HANDED),
+        sublayer_kernel,
         out_shape=(
             pltpu.VMEM(block, BF16), pltpu.VMEM(block, BF16),
             pltpu.VMEM((dim, ff), BF16), pltpu.VMEM((ff, dim), BF16), pltpu.VMEM(small, F32),
@@ -791,7 +801,7 @@
             pltpu.VMEM((dim, half), BF16), pltpu.VMEM((dim, half), BF16),
             pltpu.VMEM((half, dim), BF16), pltpu.VMEM((half, dim), BF16),
             dma((8,)), dma, dma((rows,)), dma, dma((rows,)), dma((6,)),
-            dma((2,)), dma((2, steps // SUB)), dma((HANDED,)),
+            dma((2,)), dma((2, steps // SUB)), dma((NEAR[0] + FAR,)),
             dma((2,)), dma((2, steps)), dma((2, steps)), dma((2,)),
             dma((2,)), dma((2,)),
         ],

time: 206 us -> 199 us (0.966)
  Pallas kernels: 205 us -> 198 us
    pallas_call x1, Pallas kernels: 197 us -> 189 us  [run_sublayers(): pl.pallas_call(sublayer_kernel, out_shape=(pltpu.VMEM(block, BF16), pltpu...]
where the time goes in v4:
time: 199 us
  Pallas kernels  198 us (99%)
    pallas_call x1, Pallas kernels, run_sublayers(): pl.pallas_call(sublayer_kernel, out_shape=(pltpu.VMEM(block, BF16), pltpu...  189 us
    pallas_call x1, Pallas kernels, run_finish(): pl.pallas_call(finish_kernel, out_shape=(out((1, rows, seq, dim), BF16),...  8.83 us

profile of v4, /device:TPU:3, one launch (start us, length us, event | category | flops | bytes accessed | tf_op | source)
XLA Modules:
  0.0 199.0 jit_solution(11669745364615237911)
XLA Ops:
  0.6 189.3 %sublayer.1 = (bf16[8,128,768]{2,1,0:T(8,128)(2,1)S(1)}, bf16[8,128,768]{2,1,0:T(8,128)(2,1)S(1)}, bf16[768,3072]{1,0:T(8,128)(2,1)S(1)}, bf16[3072,768]{1,0:T(8,128)(2,1)S(1)}, f32[8,768]{1,0:T(8,128)S(1)}) custom-call(bf16[8,128,768]{2,1,0:T(8,128)(2,1)} %start.1, bf16[8,128,768]{2,1,0:T(8,128)(2,1)} %cot.1, bf16[1,768,3072]{2,1,0:T(8,128)(2,1)} %first.1, ...), custom_call_target="tpu_custom_call" | custom-call | tf_op jit(solution)/shard_map/sublayer/pallas_call | solution.py:783
  190.0 8.8 %finish.1 = (bf16[1,8,128,768]{3,2,1,0:T(8,128)(2,1)}, f32[1,8,128,768]{3,2,1,0:T(8,128)}, f32[1,768,3072]{2,1,0:T(8,128)}, f32[1,3072,768]{2,1,0:T(8,128)}, f32...) custom-call(bf16[8,128,768]{2,1,0:T(8,128)(2,1)S(1)} %get-tuple-element.12.res, ...), custom_call_target="tpu_custom_call" | custom-call | tf_op jit(solution)/shard_map/finish/pallas_call | solution.py:822

commit v5 on v4

--- a/solution.py
+++ b/solution.py
@@ -267,52 +267,54 @@
             projected[:, 2 * dim :] + bias[0:1, dim : 2 * dim]
         ).astype(BF16)
         seg_row = seg[pl.ds(i, 1), :].astype(F32)
-        allowed = (column(seg_row) == seg_row) & ((valid_row(i) > 0) | eye)
+        allowed = (column(seg_row) == seg_row) & ((column(valid_row(i)) > 0) | eye)
+        packed = [mid[i, :, k * PAIR : (k + 1) * PAIR] for k in range(3 * pairs)]
+        scores = [
+            dot(split_heads(packed[pairs + p]), packed[p], NT) * HEAD_DIM**-0.5
+            for p in range(pairs)
+        ]
+        mixed = []
         for p in range(pairs):
-            at = p * PAIR
-            query = mid[i, :, at : at + PAIR]
-            keys = split_heads(mid[i, :, dim + at : dim + at + PAIR])
-            values = split_heads(mid[i, :, 2 * dim + at : 2 * dim + at + PAIR])
-            scores = dot(query, keys, NT) * HEAD_DIM**-0.5
             probs = []
-            for half in (scores[:, :seq], scores[:, seq:]):
+            for half in (scores[p][:seq], scores[p][seq:]):
                 half = jnp.where(allowed, half, NEG_FILL)
-                weight = jnp.exp(half - jnp.max(half, axis=-1, keepdims=True))
-                probs.append(weight / jnp.sum(weight, axis=-1, keepdims=True))
-            prob = jnp.concatenate(probs, axis=1).astype(BF16)
-            act[i, :, 2 * seq * p : 2 * seq * (p + 1)] = prob
-            mid[i, :, 3 * dim + at : 3 * dim + at + PAIR] = dot(prob, values).astype(BF16)
-        branch = dot(mid[i, :, 3 * dim :], w1t[3 * dim :, :]) + bias[0:1, ff:]
+                weight = jnp.exp(half - jnp.max(half, axis=0, keepdims=True))
+                probs.append((weight / jnp.sum(weight, axis=0, keepdims=True)).astype(BF16))
+                act[i, :, (2 * p + len(probs) - 1) * seq : (2 * p + len(probs)) * seq] = probs[-1]
+            prob = jnp.concatenate(probs, axis=0)
+            mixed.append(dot(prob, split_heads(packed[2 * pairs + p]), TN).astype(BF16))
+        mixed = jnp.concatenate(mixed, axis=1)
+        mid[i, :, 3 * dim :] = mixed
+        branch = dot(mixed, w1t[3 * dim :, :]) + bias[0:1, ff:]
         leave(i, hidden, branch)
 
     def attention_backward(i):
         grad = grad_entry(i)
         mixed_grad = dot(grad, w1[:, 3 * dim :]).astype(BF16)
+        packed = [mid[i, :, k * PAIR : (k + 1) * PAIR] for k in range(3 * pairs)]
+        probs = [act[i, :, k * seq : (k + 1) * seq] for k in range(2 * pairs)]
+        grads = [None] * (3 * pairs)
         for p in range(pairs):
-            at = p * PAIR
-            query = mid[i, :, at : at + PAIR]
-            keys = split_heads(mid[i, :, dim + at : dim + at + PAIR])
-            values = split_heads(mid[i, :, 2 * dim + at : 2 * dim + at + PAIR])
-            prob = act[i, :, 2 * seq * p : 2 * seq * (p + 1)]
-            out_grad = mixed_grad[:, at : at + PAIR]
-            prob_grad = dot(out_grad, values, NT)
-            prob_value = prob.astype(F32)
+            out_grad = mixed_grad[:, p * PAIR : (p + 1) * PAIR]
+            prob_grad = dot(split_heads(packed[2 * pairs + p]), out_grad, NT)
             parts = []
-            for cols in (slice(0, seq), slice(seq, 2 * seq)):
-                pv, pg = prob_value[:, cols], prob_grad[:, cols]
-                parts.append(pv * (pg - jnp.sum(pv * pg, axis=-1, keepdims=True)))
-            score_grad = jnp.concatenate(parts, axis=1).astype(BF16)
-            query_grad = dot(score_grad, keys) * HEAD_DIM**-0.5
-            key_grad = join_heads(dot(score_grad, query, TN)) * HEAD_DIM**-0.5
-            value_grad = join_heads(dot(prob, out_grad, TN))
-            mid[i, :, at : at + PAIR] = query_grad.astype(BF16)
-            mid[i, :, dim + at : dim + at + PAIR] = key_grad.astype(BF16)
-            mid[i, :, 2 * dim + at : 2 * dim + at + PAIR] = value_grad.astype(BF16)
-        packed = mid[i, :, : 3 * dim]
-        normed_grad = dot(packed, w1t[: 3 * dim, :])
+            for k in range(2):
+                value, grad_of = probs[2 * p + k].astype(F32), prob_grad[k * seq : (k + 1) * seq]
+                inner = jnp.sum(value * grad_of, axis=0, keepdims=True)
+                parts.append((value * (grad_of - inner)).astype(BF16))
+            score_grad = jnp.concatenate(parts, axis=0)
+            prob = jnp.concatenate(probs[2 * p : 2 * p + 2], axis=0)
+            query_grad = dot(score_grad, split_heads(packed[pairs + p]), TN) * HEAD_DIM**-0.5
+            key_grad = join_heads(dot(score_grad, packed[p])) * HEAD_DIM**-0.5
+            grads[p] = query_grad.astype(BF16)
+            grads[pairs + p] = key_grad.astype(BF16)
+            grads[2 * pairs + p] = join_heads(dot(prob, out_grad)).astype(BF16)
+        packed_grad = jnp.concatenate(grads, axis=1)
+        mid[i, :, : 3 * dim] = packed_grad
+        normed_grad = dot(packed_grad, w1t[: 3 * dim, :])
         grad_leave(i, grad, normed_grad)
-        in_acc[:, :dim] += fold(packed[:, :dim].astype(F32))
-        in_acc[:, dim : 2 * dim] += fold(packed[:, 2 * dim :].astype(F32))
+        in_acc[:, :dim] += fold(packed_grad[:, :dim].astype(F32))
+        in_acc[:, dim : 2 * dim] += fold(packed_grad[:, 2 * dim :].astype(F32))
 
     for load in small_loads:
         load.wait()

time: 199 us -> 199 us (level)
  no operation moved by 1% of the time
where the time goes in v5:
time: 199 us
  Pallas kernels  198 us (99%)
    pallas_call x1, Pallas kernels, run_sublayers(): pl.pallas_call(sublayer_kernel, out_shape=(pltpu.VMEM(block, BF16), pltpu...  189 us
    pallas_call x1, Pallas kernels, run_finish(): pl.pallas_call(finish_kernel, out_shape=(out((1, rows, seq, dim), BF16),...  8.83 us

profile of v5, /device:TPU:3, one launch (start us, length us, event | category | flops | bytes accessed | tf_op | source)
XLA Modules:
  0.0 198.5 jit_solution(4056660537381067359)
XLA Ops:
  0.6 188.9 %sublayer.1 = (bf16[8,128,768]{2,1,0:T(8,128)(2,1)S(1)}, bf16[8,128,768]{2,1,0:T(8,128)(2,1)S(1)}, bf16[768,3072]{1,0:T(8,128)(2,1)S(1)}, bf16[3072,768]{1,0:T(8,128)(2,1)S(1)}, f32[8,768]{1,0:T(8,128)S(1)}) custom-call(bf16[8,128,768]{2,1,0:T(8,128)(2,1)} %start.1, bf16[8,128,768]{2,1,0:T(8,128)(2,1)} %cot.1, bf16[1,768,3072]{2,1,0:T(8,128)(2,1)} %first.1, ...), custom_call_target="tpu_custom_call" | custom-call | tf_op jit(solution)/shard_map/sublayer/pallas_call | solution.py:785
  189.5 8.8 %finish.1 = (bf16[1,8,128,768]{3,2,1,0:T(8,128)(2,1)}, f32[1,8,128,768]{3,2,1,0:T(8,128)}, f32[1,768,3072]{2,1,0:T(8,128)}, f32[1,3072,768]{2,1,0:T(8,128)}, f32...) custom-call(bf16[8,128,768]{2,1,0:T(8,128)(2,1)S(1)} %get-tuple-element.12.res, ...), custom_call_target="tpu_custom_call" | custom-call | tf_op jit(solution)/shard_map/finish/pallas_call | solution.py:824

commit v6 on v5

--- a/solution.py
+++ b/solution.py
@@ -18,8 +18,9 @@
 TILE = 1536
 CHUNK = 256
 SUB = 4
-NEAR = (6, 5)
-FAR = 9
+NEAR = (6, 6)
+FAR = 10
+RELAYED = 4
 LOADS = 4
 WRITES = 12
 SUBLAYER_VMEM = 50 * 2**20
@@ -58,7 +59,7 @@
     w1, w2, w1t, w2t, hin, pair, act, mid,
     norm, bias, seg, val, sq_acc, norm_acc, in_acc, out_acc, small,
     sum_a1, sum_b1, sum_a2, sum_b2,
-    load_sem, hs_sem, hr_sem, gs_sem, gr_sem, small_sem,
+    load_sem, hs_sem, hr_sem, gs_sem, gr_sem, relay_send, relay_recv, small_sem,
     part_send, part_recv, given_recv, line_send, line_recv, whole_recv, back_send,
     mate_send, mate_recv,
 ):
@@ -143,7 +144,12 @@
     def _():
         greet(nxt, dp)
 
+    @pl.when((section == 0) | (section == 2))
+    def _():
+        greet(2 - section, dp)
+
     peers = 3 + has_outer.astype(jnp.int32)
+    peers += ((section == 0) | (section == 2)).astype(jnp.int32)
     peers += ((section > 0) & (section < last)).astype(jnp.int32)
 
     for ref in (sq_acc, norm_acc, in_acc, out_acc):
@@ -160,6 +166,26 @@
             gout.at[i], gin.at[i], gs_sem, gr_sem.at[i],
             device_id=(prv, dp), device_id_type=MESH,
         )
+
+    def via(i):
+        return w2.at[pl.ds(pl.multiple_of(i * seq, seq), seq), :]
+
+    def relay_in(i):
+        return pltpu.make_async_remote_copy(
+            gout.at[i], via(i), gs_sem, relay_recv.at[i],
+            device_id=(0, dp), device_id_type=MESH,
+        )
+
+    def relay_out(i):
+        return pltpu.make_async_remote_copy(
+            via(i), gin.at[i], relay_send, gr_sem.at[i],
+            device_id=(nxt, dp), device_id_type=MESH,
+        )
+
+    def pass_on(i, carry):
+        relay_in(i).wait_recv()
+        relay_out(i).start()
+        return carry
 
     eye = lax.broadcasted_iota(jnp.int32, (seq, seq), 0) == lax.broadcasted_iota(
         jnp.int32, (seq, seq), 1
@@ -215,7 +241,11 @@
         low = (grad_value + inv_std * (scaled - mean_one - normal * mean_two)).astype(BF16)
         gout[i] = low
 
-        @pl.when(section > 0)
+        @pl.when((section == 2) & (i < RELAYED))
+        def _():
+            relay_in(i).start()
+
+        @pl.when((section > 0) & ((section != 2) | (i >= RELAYED)))
         def _():
             g_copy(i).start()
 
@@ -332,7 +362,7 @@
     def _():
         cot_load.wait()
 
-    def run(forward, backward, lag, before_last):
+    def run(forward, backward, lag, before_last, after_last):
         pl.semaphore_wait(barrier, peers)
 
         def step(i, carry):
@@ -344,6 +374,10 @@
             def _():
                 forward(i)
 
+            @pl.when(i == rows)
+            def _():
+                after_last()
+
             @pl.when(i >= lag)
             def _():
                 backward(i - lag)
@@ -365,8 +399,19 @@
         def _():
             transpose(w1, w1t, 0, 3 * dim)
 
+        def relay():
+            @pl.when(section == 0)
+            def _():
+                lax.fori_loop(0, RELAYED, pass_on, 0)
+
         lag = jnp.where(section == 0, rows, rows // 2)
-        run(attention_forward, attention_backward, lag, late)
+        run(attention_forward, attention_backward, lag, late, relay)
+
+        @pl.when(section == 0)
+        def _():
+            ref = w2.at[pl.ds(0, RELAYED * seq), :]
+            pltpu.make_async_copy(ref, ref, relay_send).wait()
+
 
     @pl.when(jnp.logical_not(is_attention))
     def _():
@@ -375,7 +420,7 @@
         for at in range(0, ff, 2 * PAIR):
             w2t[:, at : at + 2 * PAIR] = w2[at : at + 2 * PAIR, :].T
         lag = jnp.where(section == last, 0, rows - 1)
-        run(dense_forward, dense_backward, lag, lambda: None)
+        run(dense_forward, dense_backward, lag, lambda: None, lambda: None)
 
 
     def total(x):
@@ -802,7 +847,7 @@
             pltpu.VMEM((4, *small), F32),
             pltpu.VMEM((dim, half), BF16), pltpu.VMEM((dim, half), BF16),
             pltpu.VMEM((half, dim), BF16), pltpu.VMEM((half, dim), BF16),
-            dma((8,)), dma, dma((rows,)), dma, dma((rows,)), dma((6,)),
+            dma((8,)), dma, dma((rows,)), dma, dma((rows,)), dma, dma((RELAYED,)), dma((6,)),
             dma((2,)), dma((2, steps // SUB)), dma((NEAR[0] + FAR,)),
             dma((2,)), dma((2, steps)), dma((2, steps)), dma((2,)),
             dma((2,)), dma((2,)),

time: 199 us -> 183 us (0.920)
  Pallas kernels: 198 us -> 182 us
    pallas_call x1, Pallas kernels: 189 us -> 173 us  [run_sublayers(): pl.pallas_call(sublayer_kernel, out_shape=(pltpu.VMEM(block, BF16), pltpu...]
where the time goes in v6:
time: 183 us
  Pallas kernels  182 us (99%)
    pallas_call x1, Pallas kernels, run_sublayers(): pl.pallas_call(sublayer_kernel, out_shape=(pltpu.VMEM(block, BF16), pltpu...  173 us
    pallas_call x1, Pallas kernels, run_finish(): pl.pallas_call(finish_kernel, out_shape=(out((1, rows, seq, dim), BF16),...  8.83 us

profile of v6, /device:TPU:3, one launch (start us, length us, event | category | flops | bytes accessed | tf_op | source)
XLA Modules:
  0.0 182.5 jit_solution(190947837205472925)
XLA Ops:
  0.6 172.9 %sublayer.1 = (bf16[8,128,768]{2,1,0:T(8,128)(2,1)S(1)}, bf16[8,128,768]{2,1,0:T(8,128)(2,1)S(1)}, bf16[768,3072]{1,0:T(8,128)(2,1)S(1)}, bf16[3072,768]{1,0:T(8,128)(2,1)S(1)}, f32[8,768]{1,0:T(8,128)S(1)}) custom-call(bf16[8,128,768]{2,1,0:T(8,128)(2,1)} %start.1, bf16[8,128,768]{2,1,0:T(8,128)(2,1)} %cot.1, bf16[1,768,3072]{2,1,0:T(8,128)(2,1)} %first.1, ...), custom_call_target="tpu_custom_call" | custom-call | tf_op jit(solution)/shard_map/sublayer/pallas_call | solution.py:830
  173.5 8.8 %finish.1 = (bf16[1,8,128,768]{3,2,1,0:T(8,128)(2,1)}, f32[1,8,128,768]{3,2,1,0:T(8,128)}, f32[1,768,3072]{2,1,0:T(8,128)}, f32[1,3072,768]{2,1,0:T(8,128)}, f32...) custom-call(bf16[8,128,768]{2,1,0:T(8,128)(2,1)S(1)} %get-tuple-element.12.res, ...), custom_call_target="tpu_custom_call" | custom-call | tf_op jit(solution)/shard_map/finish/pallas_call | solution.py:869

commit v7 on v6

--- a/solution.py
+++ b/solution.py
@@ -18,7 +18,8 @@
 TILE = 1536
 CHUNK = 256
 SUB = 4
-NEAR = (6, 6)
+QUARTER = SUB // 4
+NEAR = (5, 5)
 FAR = 10
 RELAYED = 4
 LOADS = 4
@@ -57,9 +58,9 @@
     start, cot, first, second, norm_in, bias_in, seg_in, val_in,
     hout, gout, first_o, second_o, small_o,
     w1, w2, w1t, w2t, hin, pair, act, mid,
-    norm, bias, seg, val, sq_acc, norm_acc, in_acc, out_acc, small,
+    norm, bias, seg, val, sq_acc, norm_acc, small,
     sum_a1, sum_b1, sum_a2, sum_b2,
-    load_sem, hs_sem, hr_sem, gs_sem, gr_sem, relay_send, relay_recv, small_sem,
+    load_sem, turn_sem, hs_sem, hr_sem, gs_sem, gr_sem, relay_send, relay_recv, small_sem,
     part_send, part_recv, given_recv, line_send, line_recv, whole_recv, back_send,
     mate_send, mate_recv,
 ):
@@ -152,7 +153,7 @@
     peers += ((section == 0) | (section == 2)).astype(jnp.int32)
     peers += ((section > 0) & (section < last)).astype(jnp.int32)
 
-    for ref in (sq_acc, norm_acc, in_acc, out_acc):
+    for ref in (sq_acc, norm_acc, small):
         ref[...] = jnp.zeros_like(ref)
 
     def h_copy(i):
@@ -167,6 +168,17 @@
             device_id=(prv, dp), device_id_type=MESH,
         )
 
+    def send_in_turn(i):
+        @pl.when((i == 0) & (core == 1))
+        def _():
+            pl.semaphore_wait(turn_sem, 1)
+
+        h_copy(i).start()
+
+        @pl.when((i == 0) & (core == 0))
+        def _():
+            pl.semaphore_signal(turn_sem, inc=1, device_id=(section, mate), device_id_type=MESH)
+
     def via(i):
         return w2.at[pl.ds(pl.multiple_of(i * seq, seq), seq), :]
 
@@ -212,9 +224,13 @@
         low = (hidden + branch).astype(BF16)
         hout[i] = low
 
-        @pl.when(section < last)
+        @pl.when((section > 0) & (section < last))
         def _():
             h_copy(i).start()
+
+        @pl.when(section == 0)
+        def _():
+            send_in_turn(i)
 
         weight = column(valid_row(i))
         value = low.astype(F32)
@@ -251,7 +267,6 @@
 
         norm_acc[0] += fold(normed_grad * normal)
         norm_acc[1] += fold(normed_grad)
-        out_acc[...] += fold(grad_value)
 
 
     def dense_forward(i):
@@ -274,7 +289,6 @@
             inner = dot(grad, w2t[:, cols]) * mid[i, :, cols].astype(F32)
             low = inner.astype(BF16)
             mid[i, :, cols] = low
-            in_acc[:, cols] += fold(low.astype(F32))
             normed_grad += dot(low, w1t[cols, :])
         grad_leave(i, grad, normed_grad)
 
@@ -343,8 +357,6 @@
         mid[i, :, : 3 * dim] = packed_grad
         normed_grad = dot(packed_grad, w1t[: 3 * dim, :])
         grad_leave(i, grad, normed_grad)
-        in_acc[:, :dim] += fold(packed_grad[:, :dim].astype(F32))
-        in_acc[:, dim : 2 * dim] += fold(packed_grad[:, 2 * dim :].astype(F32))
 
     for load in small_loads:
         load.wait()
@@ -421,22 +433,6 @@
             w2t[:, at : at + 2 * PAIR] = w2[at : at + 2 * PAIR, :].T
         lag = jnp.where(section == last, 0, rows - 1)
         run(dense_forward, dense_backward, lag, lambda: None, lambda: None)
-
-
-    def total(x):
-        return jnp.sum(x, axis=0, keepdims=True)
-
-    lane = lax.broadcasted_iota(jnp.int32, (1, dim), 1)
-    counts = jnp.zeros((1, dim), F32)
-    for k, x in enumerate((sq_acc[0], sq_acc[1], val[...].astype(F32))):
-        amount = jnp.sum(jnp.sum(x, axis=0, keepdims=True), axis=1, keepdims=True)
-        counts = jnp.where(lane == k, amount, counts)
-    small[0, 0:1, :] = total(norm_acc[0])
-    small[0, 1:2, :] = total(norm_acc[1])
-    for k in range(ff // dim):
-        small[0, 2 + k : 3 + k, :] = total(in_acc[:, k * dim : (k + 1) * dim])
-    small[0, 2 + ff // dim : 3 + ff // dim, :] = total(out_acc[...])
-    small[0, 3 + ff // dim : 4 + ff // dim, :] = counts
 
     def remote(src, dst, send, recv, to):
         return pltpu.make_async_remote_copy(
@@ -455,7 +451,6 @@
     small_back = remote(
         small.at[3], small.at[3], small_sem.at[5], small_sem.at[4], (section, outer)
     )
-    small_mate.start()
 
 
     tokens = rows * seq
@@ -522,19 +517,48 @@
         ref = whole(k, v)
         return remote(ref, ref, mate_send.at[k], mate_recv.at[k], (section, mate))
 
-    def compute(k, c):
-        for base, is_sent in ((theirs, True), (mine, False)):
-            at = pl.ds(pl.multiple_of(base + c * CHUNK, CHUNK), CHUNK)
-            if k == 0:
-                side = is_attention & (base + c * CHUNK >= 3 * dim)
-                left = pair[side.astype(jnp.int32)].reshape(tokens, dim)
-                right = mid[:, :, at].reshape(tokens, CHUNK)
-                w1[:, at] = dot(left, right, TN).astype(BF16)
-            else:
-                left = act[:, :, at].reshape(tokens, CHUNK)
-                w2[at, :] = dot(left, gin[...].reshape(tokens, dim), TN).astype(BF16)
-            if is_sent:
-                part_copy(k, c).start()
+    def token_sum(matrix):
+        return jnp.sum(fold(matrix.astype(F32)), axis=0, keepdims=True)
+
+    def small_start():
+        lane = lax.broadcasted_iota(jnp.int32, (1, dim), 1)
+        counts = jnp.zeros((1, dim), F32)
+        for k, x in enumerate((sq_acc[0], sq_acc[1], val[...].astype(F32))):
+            amount = jnp.sum(jnp.sum(x, axis=0, keepdims=True), axis=1, keepdims=True)
+            counts = jnp.where(lane == k, amount, counts)
+        small[0, 0:1, :] = jnp.sum(norm_acc[0], axis=0, keepdims=True)
+        small[0, 1:2, :] = jnp.sum(norm_acc[1], axis=0, keepdims=True)
+        small[0, 2 + ff // dim : 3 + ff // dim, :] = token_sum(gin[...].reshape(tokens, dim))
+        small[0, 3 + ff // dim : 4 + ff // dim, :] = counts
+        small_mate.start()
+
+    def bias_sum(matrix, col):
+        third = col // dim
+        row = jnp.where(is_attention, third // 2, third) + 2
+        at = pl.ds(pl.multiple_of(col - third * dim, CHUNK), CHUNK)
+
+        @pl.when(jnp.logical_not(is_attention) | (third == 0) | (third == 2))
+        def _():
+            small[0, pl.ds(row, 1), at] = token_sum(matrix)
+
+    def compute(k, c, is_mine):
+        base = jnp.where(is_mine, mine, theirs) + c * CHUNK
+        at = pl.ds(pl.multiple_of(base, CHUNK), CHUNK)
+        if k == 0:
+            side = is_attention & (base >= 3 * dim)
+            left = pair[side.astype(jnp.int32)].reshape(tokens, dim)
+            right = mid[:, :, at].reshape(tokens, CHUNK)
+            w1[:, at] = dot(left, right, TN).astype(BF16)
+        else:
+            left = act[:, :, at].reshape(tokens, CHUNK)
+            w2[at, :] = dot(left, gin[...].reshape(tokens, dim), TN).astype(BF16)
+
+        @pl.when(jnp.logical_not(is_mine))
+        def _():
+            part_copy(k, c).start()
+
+        if k == 0:
+            bias_sum(mid[:, :, at].reshape(tokens, CHUNK), base)
 
     def combine(dst, *refs):
         value = refs[0][...].astype(F32)
@@ -581,7 +605,7 @@
         def _():
             send_in(1, v, own(1, v), slot(sum_a2, 1, v))
 
-    def send_given(v):
+    def send_given(v, to):
         given_copy(v).wait_recv()
         send_in(1, v, slot(sum_a2, 1, v))
 
@@ -647,84 +671,90 @@
         small_o[...] = small[3]
 
     gap = jnp.where(on_left, chips // 2 - 1 - chip, chip - chips // 2)
-    lag = 2 + 6 * gap
-    begin = jnp.where(is_attention, jnp.minimum(steps - near, steps - SUB), 0)
-
-    @pl.when(jnp.logical_not(is_attention))
-    def _():
-        compute(1, 0)
+    lag = 2 + 8 * gap
+    blocks = steps // SUB
+    is_dense = jnp.logical_not(is_attention)
+    length = jnp.where(is_attention, steps + near + far, 2 * steps - handed)
+
+    ahead = jnp.where(is_middle, SUB, 0)
+
+    @pl.when(is_dense)
+    def _():
+        compute(0, 0, False)
+        compute(0, 0, True)
+
+    def in_line(u, first_part, second_part, given_part):
+        @pl.when((u >= 0) & (u < length) & is_dense)
+        def _():
+            @pl.when(u < steps)
+            def _():
+                first_part(u)
+
+            @pl.when(u >= steps)
+            def _():
+                second_part(u - steps + handed)
+
+        @pl.when((u >= 0) & (u < length) & is_attention)
+        def _():
+            @pl.when(u < near)
+            def _():
+                given_part(u, helper)
+
+            @pl.when((u >= near) & (u < steps + near))
+            def _():
+                first_part(u - near)
+
+            @pl.when(u >= steps + near)
+            def _():
+                given_part(NEAR[0] + u - steps - near, prv)
 
     def step(u, carry):
-        @pl.when((u < steps) & jnp.logical_not(is_attention))
-        def _():
-            send_second(u)
-
-        @pl.when((u < steps) & (u >= steps - near) & is_attention)
-        def _():
-            send_given(u - (steps - near))
-
-        @pl.when((u >= 2 * steps) & (u < 2 * steps + far) & is_attention)
-        def _():
-            send_given(NEAR[0] + u - 2 * steps)
-
-        @pl.when((u >= steps) & (u < 2 * steps))
-        def _():
-            send_first(u - steps)
-
-        t = u - lag
-
-        @pl.when((t >= begin) & is_attention)
-        def _():
-            @pl.when((t >= steps - near) & (t < steps))
-            def _():
-                settle_given(t - (steps - near), helper)
-
-            @pl.when((t >= 2 * steps) & (t < 2 * steps + far))
-            def _():
-                settle_given(NEAR[0] + t - 2 * steps, prv)
-
-            @pl.when((t >= steps) & (t < 2 * steps))
-            def _():
-                settle_first(t - steps)
-
-        @pl.when((t >= handed) & jnp.logical_not(is_attention))
-        def _():
-            @pl.when(t < steps)
-            def _():
-                settle_second(t)
-
-            @pl.when((t >= steps) & (t < 2 * steps))
-            def _():
-                settle_first(t - steps)
-
-            @pl.when(t >= 2 * steps)
-            def _():
-                settle_second(t - 2 * steps)
-
-        @pl.when(u % SUB == 0)
-        def _():
-            c = u // SUB + 1
-
-            @pl.when((c < steps // SUB) & jnp.logical_not(is_attention))
-            def _():
-                compute(1, c)
-
-            @pl.when((c >= steps // SUB) & (c < 2 * (steps // SUB)))
-            def _():
-                compute(0, c - steps // SUB)
-
-        @pl.when(u == steps + SUB)
+        in_line(u - ahead, send_first, send_second, send_given)
+
+        @pl.when((u % SUB >= SUB // 2) & is_dense)
+        def _():
+            for k in range(2):
+                v = u // SUB * SUB + 2 * (u % SUB - SUB // 2) + k
+
+                @pl.when(v < handed)
+                def _(v=v):
+                    send_second(v)
+
+        t = u - ahead - lag
+
+        @pl.when(t == length - 1)
+        def _():
+            small_settle()
+
+        in_line(t, settle_first, settle_second, settle_given)
+
+        @pl.when((t >= length) & (t < length + handed) & is_dense)
+        def _():
+            settle_second(t - length)
+
+        c, q = u // SUB, u % SUB // QUARTER
+        on_time = (u % QUARTER == 0) & (c < blocks)
+
+        @pl.when(on_time & (q < 2) & is_dense)
+        def _():
+            compute(1, c, q == 1)
+
+        @pl.when(on_time & jnp.where(is_attention, q < 2, (q >= 2) & (c + 1 < blocks)))
+        def _():
+            compute(0, jnp.where(is_attention, c, c + 1), q % 2 == 1)
+
+        @pl.when(u == steps - 2)
+        def _():
+            small_start()
+
+        @pl.when(u - ahead == steps + jnp.where((chip > 0) & (chip < chips - 1), SUB, 0))
         def _():
             small_in()
 
-        @pl.when(t == steps + SUB)
-        def _():
-            small_settle()
-
         return carry
 
-    tail = jnp.where(is_attention, far, handed)
-    lax.fori_loop(begin, 2 * steps + tail + lag, step, 0)
+    tail = jnp.where(is_attention, 0, handed)
+    lax.fori_loop(0, length + ahead + lag + tail, step, 0)
 
 
     @pl.when(section < last)
@@ -843,11 +873,10 @@
             pltpu.VMEM(norm.shape, F32), pltpu.VMEM(bias.shape, F32),
             pltpu.VMEM(seg.shape, jnp.int32), pltpu.VMEM(val.shape, jnp.int32),
             pltpu.VMEM((2, 8, dim), F32), pltpu.VMEM((2, 8, dim), F32),
-            pltpu.VMEM((8, ff), F32), pltpu.VMEM((8, dim), F32),
             pltpu.VMEM((4, *small), F32),
             pltpu.VMEM((dim, half), BF16), pltpu.VMEM((dim, half), BF16),
             pltpu.VMEM((half, dim), BF16), pltpu.VMEM((half, dim), BF16),
-            dma((8,)), dma, dma((rows,)), dma, dma((rows,)), dma, dma((RELAYED,)), dma((6,)),
+            dma((8,)), pltpu.SemaphoreType.REGULAR, dma, dma((rows,)), dma, dma((rows,)), dma, dma((RELAYED,)), dma((6,)),
             dma((2,)), dma((2, steps // SUB)), dma((NEAR[0] + FAR,)),
             dma((2,)), dma((2, steps)), dma((2, steps)), dma((2,)),
             dma((2,)), dma((2,)),

time: 183 us -> 183 us (level)
  no operation moved by 1% of the time
where the time goes in v7:
time: 183 us
  Pallas kernels  182 us (99%)
    pallas_call x1, Pallas kernels, run_sublayers(): pl.pallas_call(sublayer_kernel, out_shape=(pltpu.VMEM(block, BF16), pltpu...  173 us
    pallas_call x1, Pallas kernels, run_finish(): pl.pallas_call(finish_kernel, out_shape=(out((1, rows, seq, dim), BF16),...  8.83 us

profile of v7, /device:TPU:3, one launch (start us, length us, event | category | flops | bytes accessed | tf_op | source)
XLA Modules:
  0.0 182.7 jit_solution(18309843405932353457)
XLA Ops:
  0.6 173.0 %sublayer.1 = (bf16[8,128,768]{2,1,0:T(8,128)(2,1)S(1)}, bf16[8,128,768]{2,1,0:T(8,128)(2,1)S(1)}, bf16[768,3072]{1,0:T(8,128)(2,1)S(1)}, bf16[3072,768]{1,0:T(8,128)(2,1)S(1)}, f32[8,768]{1,0:T(8,128)S(1)}) custom-call(bf16[8,128,768]{2,1,0:T(8,128)(2,1)} %start.1, bf16[8,128,768]{2,1,0:T(8,128)(2,1)} %cot.1, bf16[1,768,3072]{2,1,0:T(8,128)(2,1)} %first.1, ...), custom_call_target="tpu_custom_call" | custom-call | tf_op jit(solution)/shard_map/sublayer/pallas_call | solution.py:860
  173.7 8.8 %finish.1 = (bf16[1,8,128,768]{3,2,1,0:T(8,128)(2,1)}, f32[1,8,128,768]{3,2,1,0:T(8,128)}, f32[1,768,3072]{2,1,0:T(8,128)}, f32[1,3072,768]{2,1,0:T(8,128)}, f32...) custom-call(bf16[8,128,768]{2,1,0:T(8,128)(2,1)S(1)} %get-tuple-element.12.res, ...), custom_call_target="tpu_custom_call" | custom-call | tf_op jit(solution)/shard_map/finish/pallas_call | solution.py:898

commit v8 on v7

--- a/solution.py
+++ b/solution.py
@@ -17,11 +17,12 @@
 PAIR = 2 * HEAD_DIM
 TILE = 1536
 CHUNK = 256
-SUB = 4
+SUB = 8
 QUARTER = SUB // 4
-NEAR = (5, 5)
-FAR = 10
+NEAR = (10, 12)
+FAR = 19
 RELAYED = 4
+RING = 32
 LOADS = 4
 WRITES = 12
 SUBLAYER_VMEM = 50 * 2**20
@@ -61,7 +62,7 @@
     norm, bias, seg, val, sq_acc, norm_acc, small,
     sum_a1, sum_b1, sum_a2, sum_b2,
     load_sem, turn_sem, hs_sem, hr_sem, gs_sem, gr_sem, relay_send, relay_recv, small_sem,
-    part_send, part_recv, given_recv, line_send, line_recv, whole_recv, back_send,
+    part_send, part_recv, hand_recv, line_send, line_recv, whole_recv, back_send,
     mate_send, mate_recv,
 ):
     nrm, gin = pair.at[0], pair.at[1]
@@ -491,27 +492,31 @@
         src, dst = (w1.at[:, at], sum_a1.at[:, to]) if k == 0 else (w2.at[at, :], sum_a2.at[to, :])
         return remote(src, dst, part_send.at[k], part_recv.at[k, c], (section, mate))
 
-    def line_copy(k, v):
+    ring = line_recv.shape[0]
+
+    def line_copy(k, v, p):
         return remote(
-            own(k, v), slot(line[k], k, v), line_send.at[k], line_recv.at[k, v], (section, inner)
+            own(k, v), slot(line[k], k, v), line_send.at[k], line_recv.at[p % ring], (section, inner)
         )
 
-    def cross_copy(k, v):
+    def cross_copy(k, v, p):
         return remote(
-            own(k, v), whole(k, v), line_send.at[k], whole_recv.at[k, v], (section, inner)
+            own(k, v), whole(k, v), line_send.at[k], whole_recv.at[p % ring], (section, inner)
         )
+
+    def back_copy(k, v, p):
+        ref = whole(k, v)
+        return remote(ref, ref, back_send.at[k], whole_recv.at[p % ring], (section, outer))
+
+    shift = jnp.where(section >= 2, NEAR[0] + FAR, 0)
 
     def given_copy(v):
         to = jnp.where(v < near, helper, nxt)
-        return remote(own(1, v), slot(sum_a2, 1, v), line_send.at[1], given_recv.at[v], (to, dp))
-
-    def return_copy(v, to):
-        ref = whole(1, v)
-        return remote(ref, ref, mate_send.at[1], whole_recv.at[1, v], (to, dp))
-
-    def back_copy(k, v):
-        ref = whole(k, v)
-        return remote(ref, ref, back_send.at[k], whole_recv.at[k, v], (section, outer))
+        w = jnp.where(v < near, v + shift, v)
+        return remote(own(1, v), slot(sum_a2, 1, w), line_send.at[1], hand_recv.at[w], (to, dp))
+
+    def return_copy(w, to, v):
+        return remote(whole(1, w), whole(1, v), mate_send.at[1], hand_recv.at[v], (to, dp))
 
     def mate_copy(k, v):
         ref = whole(k, v)
@@ -566,10 +571,10 @@
             value += ref[...].astype(F32)
         dst[...] = value.astype(BF16)
 
-    def send_in(k, v, *refs):
+    def send_in(k, v, p, *refs):
         @pl.when(has_outer)
         def _():
-            line_copy(k, v).wait_recv()
+            line_copy(k, v, p).wait_recv()
             combine(own(k, v), *refs, slot(line[k], k, v))
 
         @pl.when(jnp.logical_not(has_outer))
@@ -578,39 +583,36 @@
 
         @pl.when(is_middle)
         def _():
-            cross_copy(k, v).start()
+            cross_copy(k, v, p).start()
 
         @pl.when(jnp.logical_not(is_middle))
         def _():
-            line_copy(k, v).start()
-
-    def send_first(v):
+            line_copy(k, v, p).start()
+
+    def part_wait(k, v):
         @pl.when(v % SUB == 0)
         def _():
-            part_copy(0, v // SUB).wait_recv()
-
-        send_in(0, v, own(0, v), slot(sum_a1, 0, v))
-
-    def send_second(v):
-        @pl.when(v % SUB == 0)
-        def _():
-            part_copy(1, v // SUB).wait_recv()
-
-        @pl.when(v < handed)
-        def _():
-            combine(own(1, v), own(1, v), slot(sum_a2, 1, v))
-            given_copy(v).start()
-
-        @pl.when(v >= handed)
-        def _():
-            send_in(1, v, own(1, v), slot(sum_a2, 1, v))
-
-    def send_given(v, to):
-        given_copy(v).wait_recv()
-        send_in(1, v, slot(sum_a2, 1, v))
-
-    def settle(k, v):
-        cross_copy(k, v).wait_recv()
+            part_copy(k, v // SUB).wait_recv()
+
+    def send_first(v, p):
+        part_wait(0, v)
+        send_in(0, v, p, own(0, v), slot(sum_a1, 0, v))
+
+    def send_second(v, p):
+        part_wait(1, v)
+        send_in(1, v, p, own(1, v), slot(sum_a2, 1, v))
+
+    def hand_over(v):
+        part_wait(1, v)
+        combine(own(1, v), own(1, v), slot(sum_a2, 1, v))
+        given_copy(v).start()
+
+    def send_given(w, to, v, p):
+        return_copy(w, to, w).wait_recv()
+        send_in(1, w, p, slot(sum_a2, 1, w))
+
+    def settle(k, v, p):
+        cross_copy(k, v, p).wait_recv()
 
         @pl.when(is_middle)
         def _():
@@ -618,26 +620,23 @@
 
         @pl.when(has_outer)
         def _():
-            back_copy(k, v).start()
-
-    def settle_second(v):
-        @pl.when(v < handed)
-        def _():
-            cross_copy(1, v).wait_recv()
-
-        @pl.when(v >= handed)
-        def _():
-            settle(1, v)
-
+            back_copy(k, v, p).start()
+
+    def settle_first(v, p):
+        settle(0, v, p)
+        mate_copy(0, v).start()
+
+    def settle_second(v, p):
+        settle(1, v, p)
         mate_copy(1, v).start()
 
-    def settle_first(v):
-        settle(0, v)
-        mate_copy(0, v).start()
-
-    def settle_given(v, to):
-        settle(1, v)
-        return_copy(v, to).start()
+    def settle_handed(v):
+        return_copy(v, helper, v).wait_recv()
+        mate_copy(1, v).start()
+
+    def settle_given(w, to, v, p):
+        settle(1, w, p)
+        return_copy(w, to, v).start()
 
     def small_in():
         small_mate.wait_recv()
@@ -671,8 +670,9 @@
         small_o[...] = small[3]
 
     gap = jnp.where(on_left, chips // 2 - 1 - chip, chip - chips // 2)
-    lag = 2 + 8 * gap
+    lag = 4 + 14 * gap
     blocks = steps // SUB
+    early = (blocks * 2 // 3) * SUB
     is_dense = jnp.logical_not(is_attention)
     length = jnp.where(is_attention, steps + near + far, 2 * steps - handed)
 
@@ -688,25 +688,30 @@
         def _():
             @pl.when(u < steps)
             def _():
-                first_part(u)
+                first_part(u, u)
 
             @pl.when(u >= steps)
             def _():
-                second_part(u - steps + handed)
+                second_part(u - steps + handed, u)
 
         @pl.when((u >= 0) & (u < length) & is_attention)
         def _():
             @pl.when(u < near)
             def _():
-                given_part(u, helper)
-
-            @pl.when((u >= near) & (u < steps + near))
-            def _():
-                first_part(u - near)
-
-            @pl.when(u >= steps + near)
-            def _():
-                given_part(NEAR[0] + u - steps - near, prv)
+                given_part(u + shift, helper, u, u)
+
+            @pl.when((u >= near) & (u < near + early))
+            def _():
+                first_part(u - near, u)
+
+            @pl.when((u >= near + early) & (u < near + early + far))
+            def _():
+                v = NEAR[0] + u - near - early
+                given_part(v, prv, v, u)
+
+            @pl.when(u >= near + early + far)
+            def _():
+                first_part(u - near - far, u)
 
     def step(u, carry):
         in_line(u - ahead, send_first, send_second, send_given)
@@ -718,7 +723,7 @@
 
                 @pl.when(v < handed)
                 def _(v=v):
-                    send_second(v)
+                    hand_over(v)
 
         t = u - ahead - lag
 
@@ -730,7 +735,7 @@
 
         @pl.when((t >= length) & (t < length + handed) & is_dense)
         def _():
-            settle_second(t - length)
+            settle_handed(t - length)
 
         c, q = u // SUB, u % SUB // QUARTER
         on_time = (u % QUARTER == 0) & (c < blocks)
@@ -853,6 +858,7 @@
     block = (rows, seq, dim)
     wide = (rows, seq, ff)
     small = (4 + ff // dim, dim)
+    ring = RING if lax.axis_size("dp") <= 8 else 2 * steps
     any_space = pl.BlockSpec(memory_space=pl.ANY)
     vmem = pl.BlockSpec(memory_space=pltpu.VMEM)
     out = jax.ShapeDtypeStruct
@@ -877,8 +883,8 @@
             pltpu.VMEM((dim, half), BF16), pltpu.VMEM((dim, half), BF16),
             pltpu.VMEM((half, dim), BF16), pltpu.VMEM((half, dim), BF16),
             dma((8,)), pltpu.SemaphoreType.REGULAR, dma, dma((rows,)), dma, dma((rows,)), dma, dma((RELAYED,)), dma((6,)),
-            dma((2,)), dma((2, steps // SUB)), dma((NEAR[0] + FAR,)),
-            dma((2,)), dma((2, steps)), dma((2, steps)), dma((2,)),
+            dma((2,)), dma((2, steps // SUB)), dma((sum(NEAR) + FAR,)),
+            dma((2,)), dma((ring,)), dma((ring,)), dma((2,)),
             dma((2,)), dma((2,)),
         ],
         compiler_params=pltpu.CompilerParams(

time: 183 us -> 177 us (0.967)
  Pallas kernels: 182 us -> 176 us
    pallas_call x1, Pallas kernels: 173 us -> 167 us  [run_sublayers(): pl.pallas_call(sublayer_kernel, out_shape=(pltpu.VMEM(block, BF16), pltpu...]
where the time goes in v8:
time: 177 us; the launch traced here: 176 us
  Pallas kernels  176 us (99%)
    pallas_call x1, Pallas kernels, run_sublayers(): pl.pallas_call(sublayer_kernel, out_shape=(pltpu.VMEM(block, BF16), pltpu...  167 us
    pallas_call x1, Pallas kernels, run_finish(): pl.pallas_call(finish_kernel, out_shape=(out((1, rows, seq, dim), BF16),...  8.83 us

profile of v8, /device:TPU:3, one launch (start us, length us, event | category | flops | bytes accessed | tf_op | source)
XLA Modules:
  0.0 176.5 jit_solution(18286308896101122221)
XLA Ops:
  0.6 166.8 %sublayer.1 = (bf16[8,128,768]{2,1,0:T(8,128)(2,1)S(1)}, bf16[8,128,768]{2,1,0:T(8,128)(2,1)S(1)}, bf16[768,3072]{1,0:T(8,128)(2,1)S(1)}, bf16[3072,768]{1,0:T(8,128)(2,1)S(1)}, f32[8,768]{1,0:T(8,128)S(1)}) custom-call(bf16[8,128,768]{2,1,0:T(8,128)(2,1)} %start.1, bf16[8,128,768]{2,1,0:T(8,128)(2,1)} %cot.1, bf16[1,768,3072]{2,1,0:T(8,128)(2,1)} %first.1, ...), custom_call_target="tpu_custom_call" | custom-call | tf_op jit(solution)/shard_map/sublayer/pallas_call | solution.py:866
  167.5 8.8 %finish.1 = (bf16[1,8,128,768]{3,2,1,0:T(8,128)(2,1)}, f32[1,8,128,768]{3,2,1,0:T(8,128)}, f32[1,768,3072]{2,1,0:T(8,128)}, f32[1,3072,768]{2,1,0:T(8,128)}, f32...) custom-call(bf16[8,128,768]{2,1,0:T(8,128)(2,1)S(1)} %get-tuple-element.12.res, ...), custom_call_target="tpu_custom_call" | custom-call | tf_op jit(solution)/shard_map/finish/pallas_call | solution.py:904

commit v9 on v8

--- a/solution.py
+++ b/solution.py
@@ -15,12 +15,11 @@
 NT = (((1,), (1,)), ((), ()))
 TN = (((0,), (0,)), ((), ()))
 PAIR = 2 * HEAD_DIM
-TILE = 1536
 CHUNK = 256
 SUB = 8
 QUARTER = SUB // 4
-NEAR = (10, 12)
-FAR = 19
+NEAR = (9, 12)
+FAR = 20
 RELAYED = 4
 RING = 32
 LOADS = 4
@@ -61,7 +60,7 @@
     w1, w2, w1t, w2t, hin, pair, act, mid,
     norm, bias, seg, val, sq_acc, norm_acc, small,
     sum_a1, sum_b1, sum_a2, sum_b2,
-    load_sem, turn_sem, hs_sem, hr_sem, gs_sem, gr_sem, relay_send, relay_recv, small_sem,
+    load_sem, hs_sem, hr_sem, gs_sem, gr_sem, relay_send, relay_recv, small_sem,
     part_send, part_recv, hand_recv, line_send, line_recv, whole_recv, back_send,
     mate_send, mate_recv,
 ):
@@ -76,9 +75,15 @@
     nxt = jnp.minimum(section + 1, last)
     prv = jnp.maximum(section - 1, 0)
 
-    first_load = pltpu.make_async_copy(first.at[0], w1, load_sem.at[0])
+    wide, out_cols = 3 * dim, pl.ds(3 * dim, ff - 3 * dim)
+    first_load = pltpu.make_async_copy(
+        first.at[0, :, pl.ds(0, wide)], w1.at[:, pl.ds(0, wide)], load_sem.at[0]
+    )
+    out_load = pltpu.make_async_copy(first.at[0, :, out_cols], w1.at[:, out_cols], load_sem.at[8])
     second_load = pltpu.make_async_copy(second.at[0], w2, load_sem.at[1])
-    start_load = pltpu.make_async_copy(start, hin, load_sem.at[2])
+    start_load = pltpu.make_async_copy(start.at[0], hin.at[0], load_sem.at[2])
+    others = pl.ds(1, rows - 1)
+    rest_load = pltpu.make_async_copy(start.at[others], hin.at[others], load_sem.at[9])
     cot_load = pltpu.make_async_copy(cot, gin, load_sem.at[3])
     small_loads = [
         pltpu.make_async_copy(src, dst, load_sem.at[4 + k])
@@ -87,25 +92,30 @@
         )
     ]
 
-    def split_load(src, dst, k):
+    def split_load(src, dst, cols, k):
         count = dst.shape[0] // LOADS
         for at in range(0, dst.shape[0], count):
             pltpu.make_async_copy(
-                src.at[0, pl.ds(at, count)], dst.at[pl.ds(at, count)], load_sem.at[k]
+                src.at[0, pl.ds(at, count), cols], dst.at[pl.ds(at, count), cols], load_sem.at[k]
             ).start()
-
-    split_load(first, w1, 0)
-
-    @pl.when(section == 0)
-    def _():
-        start_load.start()
 
     for load in small_loads:
         load.start()
 
+    @pl.when(section == 0)
+    def _():
+        start_load.start()
+
+    out_load.start()
+    split_load(first, w1, pl.ds(0, wide), 0)
+
+    @pl.when(section == 0)
+    def _():
+        rest_load.start()
+
     @pl.when(jnp.logical_not(is_attention))
     def _():
-        split_load(second, w2, 1)
+        split_load(second, w2, pl.ds(0, dim), 1)
 
     @pl.when(section == last)
     def _():
@@ -169,17 +179,6 @@
             device_id=(prv, dp), device_id_type=MESH,
         )
 
-    def send_in_turn(i):
-        @pl.when((i == 0) & (core == 1))
-        def _():
-            pl.semaphore_wait(turn_sem, 1)
-
-        h_copy(i).start()
-
-        @pl.when((i == 0) & (core == 0))
-        def _():
-            pl.semaphore_signal(turn_sem, inc=1, device_id=(section, mate), device_id_type=MESH)
-
     def via(i):
         return w2.at[pl.ds(pl.multiple_of(i * seq, seq), seq), :]
 
@@ -225,13 +224,9 @@
         low = (hidden + branch).astype(BF16)
         hout[i] = low
 
-        @pl.when((section > 0) & (section < last))
+        @pl.when(section < last)
         def _():
             h_copy(i).start()
-
-        @pl.when(section == 0)
-        def _():
-            send_in_turn(i)
 
         weight = column(valid_row(i))
         value = low.astype(F32)
@@ -272,26 +267,17 @@
 
     def dense_forward(i):
         hidden, low = entry(i)
-        branch = jnp.zeros((seq, dim), F32)
-        for at in range(0, ff, TILE):
-            cols = slice(at, at + TILE)
-            value, slope = gelu_and_slope(dot(low, w1[:, cols]) + bias[0:1, cols])
-            value = value.astype(BF16)
-            act[i, :, cols] = value
-            mid[i, :, cols] = slope.astype(BF16)
-            branch += dot(value, w2[cols, :])
-        leave(i, hidden, branch + bias[0:1, ff:])
+        value, slope = gelu_and_slope(dot(low, w1[...]) + bias[0:1, :ff])
+        value = value.astype(BF16)
+        act[i] = value
+        mid[i] = slope.astype(BF16)
+        leave(i, hidden, dot(value, w2[...]) + bias[0:1, ff:])
 
     def dense_backward(i):
         grad = grad_entry(i)
-        normed_grad = jnp.zeros((seq, dim), F32)
-        for at in range(0, ff, TILE):
-            cols = slice(at, at + TILE)
-            inner = dot(grad, w2t[:, cols]) * mid[i, :, cols].astype(F32)
-            low = inner.astype(BF16)
-            mid[i, :, cols] = low
-            normed_grad += dot(low, w1t[cols, :])
-        grad_leave(i, grad, normed_grad)
+        low = (dot(grad, w2t[...]) * mid[i].astype(F32)).astype(BF16)
+        mid[i] = low
+        grad_leave(i, grad, dot(low, w1t[...]))
 
 
     lower = lax.broadcasted_iota(jnp.int32, (seq, PAIR), 1) < HEAD_DIM
@@ -304,6 +290,10 @@
         return jnp.where(lower, x[:seq], x[seq:])
 
     def attention_forward(i):
+        @pl.when((section == 0) & (i == 1))
+        def _():
+            rest_load.wait()
+
         hidden, low = entry(i)
         projected = dot(low, w1[:, : 3 * dim])
         mid[i, :, :dim] = (projected[:, :dim] + bias[0:1, :dim]).astype(BF16)
@@ -361,7 +351,6 @@
 
     for load in small_loads:
         load.wait()
-    first_load.wait()
 
     def transpose(src, dst, low, high):
         for at in range(low, high, 2 * PAIR):
@@ -401,7 +390,9 @@
 
     @pl.when(is_attention)
     def _():
+        out_load.wait()
         transpose(w1, w1t, 3 * dim, ff)
+        first_load.wait()
 
         def late():
             @pl.when(section == 0)
@@ -428,6 +419,8 @@
 
     @pl.when(jnp.logical_not(is_attention))
     def _():
+        out_load.wait()
+        first_load.wait()
         second_load.wait()
         transpose(w1, w1t, 0, ff)
         for at in range(0, ff, 2 * PAIR):
@@ -882,7 +875,7 @@
             pltpu.VMEM((4, *small), F32),
             pltpu.VMEM((dim, half), BF16), pltpu.VMEM((dim, half), BF16),
             pltpu.VMEM((half, dim), BF16), pltpu.VMEM((half, dim), BF16),
-            dma((8,)), pltpu.SemaphoreType.REGULAR, dma, dma((rows,)), dma, dma((rows,)), dma, dma((RELAYED,)), dma((6,)),
+            dma((10,)), dma, dma((rows,)), dma, dma((rows,)), dma, dma((RELAYED,)), dma((6,)),
             dma((2,)), dma((2, steps // SUB)), dma((sum(NEAR) + FAR,)),
             dma((2,)), dma((ring,)), dma((ring,)), dma((2,)),
             dma((2,)), dma((2,)),

time: 177 us -> 175 us (0.989)
  Pallas kernels: 176 us -> 173 us
    pallas_call x1, Pallas kernels: 167 us -> 164 us  [run_sublayers(): pl.pallas_call(sublayer_kernel, out_shape=(pltpu.VMEM(block, BF16), pltpu...]
where the time goes in v9:
time: 175 us; the launch traced here: 174 us
  Pallas kernels  173 us (99%)
    pallas_call x1, Pallas kernels, run_sublayers(): pl.pallas_call(sublayer_kernel, out_shape=(pltpu.VMEM(block, BF16), pltpu...  164 us
    pallas_call x1, Pallas kernels, run_finish(): pl.pallas_call(finish_kernel, out_shape=(out((1, rows, seq, dim), BF16),...  8.83 us

profile of v9, /device:TPU:3, one launch (start us, length us, event | category | flops | bytes accessed | tf_op | source)
XLA Modules:
  0.0 174.1 jit_solution(9524018784553310938)
XLA Ops:
  0.6 164.5 %sublayer.1 = (bf16[8,128,768]{2,1,0:T(8,128)(2,1)S(1)}, bf16[8,128,768]{2,1,0:T(8,128)(2,1)S(1)}, bf16[768,3072]{1,0:T(8,128)(2,1)S(1)}, bf16[3072,768]{1,0:T(8,128)(2,1)S(1)}, f32[8,768]{1,0:T(8,128)S(1)}) custom-call(bf16[8,128,768]{2,1,0:T(8,128)(2,1)} %start.1, bf16[8,128,768]{2,1,0:T(8,128)(2,1)} %cot.1, bf16[1,768,3072]{2,1,0:T(8,128)(2,1)} %first.1, ...), custom_call_target="tpu_custom_call" | custom-call | tf_op jit(solution)/shard_map/sublayer/pallas_call | solution.py:859
  165.1 8.8 %finish.1 = (bf16[1,8,128,768]{3,2,1,0:T(8,128)(2,1)}, f32[1,8,128,768]{3,2,1,0:T(8,128)}, f32[1,768,3072]{2,1,0:T(8,128)}, f32[1,3072,768]{2,1,0:T(8,128)}, f32...) custom-call(bf16[8,128,768]{2,1,0:T(8,128)(2,1)S(1)} %get-tuple-element.12.res, ...), custom_call_target="tpu_custom_call" | custom-call | tf_op jit(solution)/shard_map/finish/pallas_call | solution.py:897

commit v10 on v9

--- a/solution.py
+++ b/solution.py
@@ -558,6 +558,10 @@
         if k == 0:
             bias_sum(mid[:, :, at].reshape(tokens, CHUNK), base)
 
+    def clear(base):
+        at = pl.ds(pl.multiple_of(base, CHUNK), half)
+        second_o[at, :] = jnp.zeros((half, dim), BF16)
+
     def combine(dst, *refs):
         value = refs[0][...].astype(F32)
         for ref in refs[1:]:
@@ -745,6 +749,10 @@
         def _():
             small_start()
 
+        @pl.when((u == steps) & is_attention)
+        def _():
+            clear(theirs)
+
         @pl.when(u - ahead == steps + jnp.where((chip > 0) & (chip < chips - 1), SUB, 0))
         def _():
             small_in()
@@ -809,18 +817,34 @@
 
     @pl.when(is_attention)
     def _():
-        second_o[...] = jnp.zeros_like(second_o)
+        clear(mine)
 
 
 def finish_kernel(
     res, sg, first, second, small,
     res_o, sg_o, first_o, second_o, norm_o, bias_o, rms_o,
-    sg_wide, first_wide, second_wide, sem, first_sem, second_sem,
+    sg_wide, first_wide, second_wide, norm, bias, rms, sem, first_sem, second_sem,
 ):
-    rows, _, dim = sg.shape
+    dim = sg.shape[2]
     ff = first.shape[1]
-    copies = [pltpu.make_async_copy(res, res_o.at[0], sem.at[0])]
-    copies[0].start()
+    copies = []
+
+    def write(src, dst, sem):
+        copies.append(pltpu.make_async_copy(src, dst, sem))
+        copies[-1].start()
+
+    write(res, res_o.at[0], sem.at[0])
+    norm[0] = small[0:2, :]
+    write(norm, norm_o, sem.at[1])
+    count = ff // dim + 1
+    for k in range(count):
+        bias[0:1, k * dim : (k + 1) * dim] = small[2 + k : 3 + k, :]
+    write(bias, bias_o, sem.at[2])
+    stat = small[2 + count : 3 + count, :]
+    rms[...] = jnp.sqrt(stat[:, 0:2] / (stat[:, 2:3] * dim))
+    write(rms, rms_o, sem.at[3])
+    sg_wide[...] = sg[...].astype(F32)
+    write(sg_wide, sg_o.at[0], sem.at[4])
     for src, wide, dst, sems in (
         (first, first_wide, first_o, first_sem), (second, second_wide, second_o, second_sem),
     ):
@@ -828,17 +852,7 @@
         for k in range(WRITES):
             at = pl.ds(k * count, count)
             wide[at, :] = src[at, :].astype(F32)
-            copies.append(pltpu.make_async_copy(wide.at[at], dst.at[0, at], sems.at[k]))
-            copies[-1].start()
-    sg_wide[...] = sg[...].astype(F32)
-    copies.append(pltpu.make_async_copy(sg_wide, sg_o.at[0], sem.at[1]))
-    copies[-1].start()
-    norm_o[0] = small[0:2, :]
-    count = ff // dim + 1
-    for k in range(count):
-        bias_o[0:1, k * dim : (k + 1) * dim] = small[2 + k : 3 + k, :]
-    stat = small[2 + count : 3 + count, :]
-    rms_o[...] = jnp.sqrt(stat[:, 0:2] / (stat[:, 2:3] * dim))
+            write(wide.at[at], dst.at[0, at], sems.at[k])
     for copy in copies:
         copy.wait()
 
@@ -902,11 +916,12 @@
             out((1, 2, dim), F32), out((1, ff + dim), F32), out((1, 2), F32),
         ),
         in_specs=[vmem] * 5,
-        out_specs=(any_space,) * 4 + (vmem,) * 3,
+        out_specs=(any_space,) * 7,
         scratch_shapes=[
             pltpu.VMEM((rows, seq, dim), F32),
             pltpu.VMEM((dim, ff), F32), pltpu.VMEM((ff, dim), F32),
-            dma((2,)), dma((WRITES,)), dma((WRITES,)),
+            pltpu.VMEM((1, 2, dim), F32), pltpu.VMEM((1, ff + dim), F32), pltpu.VMEM((1, 2), F32),
+            dma((5,)), dma((WRITES,)), dma((WRITES,)),
         ],
         compiler_params=pltpu.CompilerParams(vmem_limit_bytes=FINISH_VMEM),
         name="finish",

time: 175 us -> 174 us (level)
  no operation moved by 1% of the time
where the time goes in v10:
time: 174 us
  Pallas kernels  173 us (99%)
    pallas_call x1, Pallas kernels, run_sublayers(): pl.pallas_call(sublayer_kernel, out_shape=(pltpu.VMEM(block, BF16), pltpu...  165 us
    pallas_call x1, Pallas kernels, run_finish(): pl.pallas_call(finish_kernel, out_shape=(out((1, rows, seq, dim), BF16),...  8.19 us

profile of v10, /device:TPU:3, one launch (start us, length us, event | category | flops | bytes accessed | tf_op | source)
XLA Modules:
  0.0 173.7 jit_solution(6873706486644626291)
XLA Ops:
  0.6 164.7 %sublayer.1 = (bf16[8,128,768]{2,1,0:T(8,128)(2,1)S(1)}, bf16[8,128,768]{2,1,0:T(8,128)(2,1)S(1)}, bf16[768,3072]{1,0:T(8,128)(2,1)S(1)}, bf16[3072,768]{1,0:T(8,128)(2,1)S(1)}, f32[8,768]{1,0:T(8,128)S(1)}) custom-call(bf16[8,128,768]{2,1,0:T(8,128)(2,1)} %start.1, bf16[8,128,768]{2,1,0:T(8,128)(2,1)} %cot.1, bf16[1,768,3072]{2,1,0:T(8,128)(2,1)} %first.1, ...), custom_call_target="tpu_custom_call" | custom-call | tf_op jit(solution)/shard_map/sublayer/pallas_call | solution.py:873
  165.3 8.2 %finish.1 = (bf16[1,8,128,768]{3,2,1,0:T(8,128)(2,1)}, f32[1,8,128,768]{3,2,1,0:T(8,128)}, f32[1,768,3072]{2,1,0:T(8,128)}, f32[1,3072,768]{2,1,0:T(8,128)}, f32...) custom-call(bf16[8,128,768]{2,1,0:T(8,128)(2,1)S(1)} %get-tuple-element.12.res, ...), custom_call_target="tpu_custom_call" | custom-call | tf_op jit(solution)/shard_map/finish/pallas_call | solution.py:911

commit v11 on v10

--- a/solution.py
+++ b/solution.py
@@ -18,9 +18,10 @@
 CHUNK = 256
 SUB = 8
 QUARTER = SUB // 4
-NEAR = (9, 12)
-FAR = 20
+NEAR = (11, 12)
+FAR = 19
 RELAYED = 4
+PARTS = 4
 RING = 32
 LOADS = 4
 WRITES = 12
@@ -179,24 +180,29 @@
             device_id=(prv, dp), device_id_type=MESH,
         )
 
-    def via(i):
-        return w2.at[pl.ds(pl.multiple_of(i * seq, seq), seq), :]
-
-    def relay_in(i):
+    part = seq // PARTS
+
+    def via(i, k):
+        return w2.at[pl.ds(pl.multiple_of(i * seq + k * part, part), part), :]
+
+    def part_of(ref, i, k):
+        return ref.at[i, pl.ds(pl.multiple_of(k * part, part), part)]
+
+    def relay_in(i, k):
         return pltpu.make_async_remote_copy(
-            gout.at[i], via(i), gs_sem, relay_recv.at[i],
+            part_of(gout, i, k), via(i, k), gs_sem, relay_recv.at[i, k],
             device_id=(0, dp), device_id_type=MESH,
         )
 
-    def relay_out(i):
+    def relay_out(i, k):
         return pltpu.make_async_remote_copy(
-            via(i), gin.at[i], relay_send, gr_sem.at[i],
+            via(i, k), part_of(gin, i, k), relay_send, gr_sem.at[i],
             device_id=(nxt, dp), device_id_type=MESH,
         )
 
-    def pass_on(i, carry):
-        relay_in(i).wait_recv()
-        relay_out(i).start()
+    def pass_on(n, carry):
+        relay_in(n // PARTS, n % PARTS).wait_recv()
+        relay_out(n // PARTS, n % PARTS).start()
         return carry
 
     eye = lax.broadcasted_iota(jnp.int32, (seq, seq), 0) == lax.broadcasted_iota(
@@ -255,7 +261,8 @@
 
         @pl.when((section == 2) & (i < RELAYED))
         def _():
-            relay_in(i).start()
+            for k in range(PARTS):
+                relay_in(i, k).start()
 
         @pl.when((section > 0) & ((section != 2) | (i >= RELAYED)))
         def _():
@@ -406,7 +413,7 @@
         def relay():
             @pl.when(section == 0)
             def _():
-                lax.fori_loop(0, RELAYED, pass_on, 0)
+                lax.fori_loop(0, PARTS * RELAYED, pass_on, 0)
 
         lag = jnp.where(section == 0, rows, rows // 2)
         run(attention_forward, attention_backward, lag, late, relay)
@@ -889,7 +896,7 @@
             pltpu.VMEM((4, *small), F32),
             pltpu.VMEM((dim, half), BF16), pltpu.VMEM((dim, half), BF16),
             pltpu.VMEM((half, dim), BF16), pltpu.VMEM((half, dim), BF16),
-            dma((10,)), dma, dma((rows,)), dma, dma((rows,)), dma, dma((RELAYED,)), dma((6,)),
+            dma((10,)), dma, dma((rows,)), dma, dma((rows,)), dma, dma((RELAYED, PARTS)), dma((6,)),
             dma((2,)), dma((2, steps // SUB)), dma((sum(NEAR) + FAR,)),
             dma((2,)), dma((ring,)), dma((ring,)), dma((2,)),
             dma((2,)), dma((2,)),

time: 174 us -> 174 us (level)
  no operation moved by 1% of the time
where the time goes in v11:
time: 174 us; the launch traced here: 173 us
  Pallas kernels  172 us (99%)
    pallas_call x1, Pallas kernels, run_sublayers(): pl.pallas_call(sublayer_kernel, out_shape=(pltpu.VMEM(block, BF16), pltpu...  164 us
    pallas_call x1, Pallas kernels, run_finish(): pl.pallas_call(finish_kernel, out_shape=(out((1, rows, seq, dim), BF16),...  8.19 us

profile of v11, /device:TPU:3, one launch (start us, length us, event | category | flops | bytes accessed | tf_op | source)
XLA Modules:
  0.0 173.3 jit_solution(8904842824990896852)
XLA Ops:
  0.6 164.3 %sublayer.1 = (bf16[8,128,768]{2,1,0:T(8,128)(2,1)S(1)}, bf16[8,128,768]{2,1,0:T(8,128)(2,1)S(1)}, bf16[768,3072]{1,0:T(8,128)(2,1)S(1)}, bf16[3072,768]{1,0:T(8,128)(2,1)S(1)}, f32[8,768]{1,0:T(8,128)S(1)}) custom-call(bf16[8,128,768]{2,1,0:T(8,128)(2,1)} %start.1, bf16[8,128,768]{2,1,0:T(8,128)(2,1)} %cot.1, bf16[1,768,3072]{2,1,0:T(8,128)(2,1)} %first.1, ...), custom_call_target="tpu_custom_call" | custom-call | tf_op jit(solution)/shard_map/sublayer/pallas_call | solution.py:880
  164.9 8.2 %finish.1 = (bf16[1,8,128,768]{3,2,1,0:T(8,128)(2,1)}, f32[1,8,128,768]{3,2,1,0:T(8,128)}, f32[1,768,3072]{2,1,0:T(8,128)}, f32[1,3072,768]{2,1,0:T(8,128)}, f32...) custom-call(bf16[8,128,768]{2,1,0:T(8,128)(2,1)S(1)} %get-tuple-element.12.res, ...), custom_call_target="tpu_custom_call" | custom-call | tf_op jit(solution)/shard_map/finish/pallas_call | solution.py:918

commit v12 on v11

--- a/solution.py
+++ b/solution.py
@@ -22,9 +22,9 @@
 FAR = 19
 RELAYED = 4
 PARTS = 4
-RING = 32
+RING = 24
 LOADS = 4
-WRITES = 12
+WRITES = 3
 SUBLAYER_VMEM = 50 * 2**20
 FINISH_VMEM = 40 * 2**20
 GELU_C = 0.7978845608028654

time: 174 us -> 173 us (level)
  no operation moved by 1% of the time
where the time goes in v12:
time: 173 us
  Pallas kernels  172 us (99%)
    pallas_call x1, Pallas kernels, run_sublayers(): pl.pallas_call(sublayer_kernel, out_shape=(pltpu.VMEM(block, BF16), pltpu...  164 us
    pallas_call x1, Pallas kernels, run_finish(): pl.pallas_call(finish_kernel, out_shape=(out((1, rows, seq, dim), BF16),...  8.06 us

profile of v12, /device:TPU:3, one launch (start us, length us, event | category | flops | bytes accessed | tf_op | source)
XLA Modules:
  0.0 173.0 jit_solution(11947073836178389400)
XLA Ops:
  0.6 164.1 %sublayer.1 = (bf16[8,128,768]{2,1,0:T(8,128)(2,1)S(1)}, bf16[8,128,768]{2,1,0:T(8,128)(2,1)S(1)}, bf16[768,3072]{1,0:T(8,128)(2,1)S(1)}, bf16[3072,768]{1,0:T(8,128)(2,1)S(1)}, f32[8,768]{1,0:T(8,128)S(1)}) custom-call(bf16[8,128,768]{2,1,0:T(8,128)(2,1)} %start.1, bf16[8,128,768]{2,1,0:T(8,128)(2,1)} %cot.1, bf16[1,768,3072]{2,1,0:T(8,128)(2,1)} %first.1, ...), custom_call_target="tpu_custom_call" | custom-call | tf_op jit(solution)/shard_map/sublayer/pallas_call | solution.py:880
  164.8 8.1 %finish.1 = (bf16[1,8,128,768]{3,2,1,0:T(8,128)(2,1)}, f32[1,8,128,768]{3,2,1,0:T(8,128)}, f32[1,768,3072]{2,1,0:T(8,128)}, f32[1,3072,768]{2,1,0:T(8,128)}, f32...) custom-call(bf16[8,128,768]{2,1,0:T(8,128)(2,1)S(1)} %get-tuple-element.12.res, ...), custom_call_target="tpu_custom_call" | custom-call | tf_op jit(solution)/shard_map/finish/pallas_call | solution.py:918

commit v13 on v12

--- a/solution.py
+++ b/solution.py
@@ -18,7 +18,7 @@
 CHUNK = 256
 SUB = 8
 QUARTER = SUB // 4
-NEAR = (11, 12)
+NEAR = (10, 13)
 FAR = 19
 RELAYED = 4
 PARTS = 4
@@ -674,13 +674,13 @@
         small_o[...] = small[3]
 
     gap = jnp.where(on_left, chips // 2 - 1 - chip, chip - chips // 2)
-    lag = 4 + 14 * gap
+    lag = 3 + 13 * gap
     blocks = steps // SUB
     early = (blocks * 2 // 3) * SUB
     is_dense = jnp.logical_not(is_attention)
     length = jnp.where(is_attention, steps + near + far, 2 * steps - handed)
 
-    ahead = jnp.where(is_middle, SUB, 0)
+    ahead = jnp.where(is_middle, SUB // 2, 0)
 
     @pl.when(is_dense)
     def _():

time: 173 us -> 174 us (level)
  no operation moved by 1% of the time
where the time goes in v13:
time: 174 us
  Pallas kernels  173 us (99%)
    pallas_call x1, Pallas kernels, run_sublayers(): pl.pallas_call(sublayer_kernel, out_shape=(pltpu.VMEM(block, BF16), pltpu...  165 us
    pallas_call x1, Pallas kernels, run_finish(): pl.pallas_call(finish_kernel, out_shape=(out((1, rows, seq, dim), BF16),...  8.06 us

profile of v13, /device:TPU:3, one launch (start us, length us, event | category | flops | bytes accessed | tf_op | source)
XLA Modules:
  0.0 173.9 jit_solution(3638572931838724407)
XLA Ops:
  0.6 165.0 %sublayer.1 = (bf16[8,128,768]{2,1,0:T(8,128)(2,1)S(1)}, bf16[8,128,768]{2,1,0:T(8,128)(2,1)S(1)}, bf16[768,3072]{1,0:T(8,128)(2,1)S(1)}, bf16[3072,768]{1,0:T(8,128)(2,1)S(1)}, f32[8,768]{1,0:T(8,128)S(1)}) custom-call(bf16[8,128,768]{2,1,0:T(8,128)(2,1)} %start.1, bf16[8,128,768]{2,1,0:T(8,128)(2,1)} %cot.1, bf16[1,768,3072]{2,1,0:T(8,128)(2,1)} %first.1, ...), custom_call_target="tpu_custom_call" | custom-call | tf_op jit(solution)/shard_map/sublayer/pallas_call | solution.py:880
  165.7 8.1 %finish.1 = (bf16[1,8,128,768]{3,2,1,0:T(8,128)(2,1)}, f32[1,8,128,768]{3,2,1,0:T(8,128)}, f32[1,768,3072]{2,1,0:T(8,128)}, f32[1,3072,768]{2,1,0:T(8,128)}, f32...) custom-call(bf16[8,128,768]{2,1,0:T(8,128)(2,1)S(1)} %get-tuple-element.12.res, ...), custom_call_target="tpu_custom_call" | custom-call | tf_op jit(solution)/shard_map/finish/pallas_call | solution.py:918
